TPU v7x, 32 devices: a whole 2x2x4 slice. The times are simulated.
32 devices in a mesh: gy: 4 (over y, core), gz: 8 (over z, x).
Axes of the slice: x: 2, y: 2, z: 4, core: 2. Of those that a mesh axis runs over, the one named last changes fastest.
Arguments:
- fields: float32 [3, 132, 64, 1024], P(None, None, 'gy', 'gz'), may hold values from -25 to 25
Outputs:
- enstrophy: float32 [128, 64, 1024], P(None, 'gy', 'gz')
- strain_rate: float32 [128, 64, 1024], P(None, 'gy', 'gz')
- factor: float32 [128, 128], replicated
All inputs are finite; a program needn't handle non-finite values.
Results may differ from a plain program's by a relative error of at most 0.0003.
Values sent between devices are 32-bit elements; how exact they have to be, the bound alone decides.
No kernel may reach another device: no remote copies, remote signals or barrier semaphores. Data moves between devices by JAX's collectives and lax.ppermute only.
A program may use at most 64 MiB of HBM per device.

v0:
```python
import jax
import jax.numpy as jnp
from jax import lax
from jax.sharding import PartitionSpec as P


def with_halo(cells, sides, width):
    for axis, dim in sides:
        count = lax.axis_size(axis)
        head = lax.slice_in_dim(cells, 0, width, axis=dim)
        tail = lax.slice_in_dim(cells, cells.shape[dim] - width, cells.shape[dim], axis=dim)
        cells = jnp.concatenate(
            [
                lax.ppermute(tail, axis, [(i, (i + 1) % count) for i in range(count)]),
                cells,
                lax.ppermute(head, axis, [((i + 1) % count, i) for i in range(count)]),
            ],
            axis=dim,
        )
    return cells


def stencil(minus_two, minus_one, plus_one, plus_two):
    return (minus_two - 8.0 * minus_one + 8.0 * plus_one - plus_two) / 12.0


def invariants(along_x, along_y, along_z):
    gradient = (along_x, along_y, along_z)
    strain_rate = (
        gradient[0][0] * gradient[0][0]
        + gradient[1][1] * gradient[1][1]
        + gradient[2][2] * gradient[2][2]
    )
    enstrophy = jnp.zeros_like(strain_rate)
    for source_axis, target_axis in ((0, 1), (0, 2), (1, 2)):
        rotation = gradient[source_axis][target_axis] - gradient[target_axis][source_axis]
        shearing = gradient[source_axis][target_axis] + gradient[target_axis][source_axis]
        enstrophy = enstrophy + 0.5 * rotation * rotation
        strain_rate = strain_rate + 0.5 * shearing * shearing
    return (enstrophy, strain_rate)


def per_device(fields):
    planes = fields.shape[1] - 4
    rows_y = fields.shape[2]
    cols_z = fields.shape[3]
    padded = with_halo(fields, (("gy", 2), ("gz", 3)), 2)
    inner = padded[:, :, 2 : rows_y + 2, 2 : cols_z + 2]
    along_x = stencil(
        inner[:, 0:planes],
        inner[:, 1 : planes + 1],
        inner[:, 3 : planes + 3],
        inner[:, 4 : planes + 4],
    )
    middle = padded[:, 2 : planes + 2]
    along_y = stencil(
        middle[:, :, 0:rows_y, 2 : cols_z + 2],
        middle[:, :, 1 : rows_y + 1, 2 : cols_z + 2],
        middle[:, :, 3 : rows_y + 3, 2 : cols_z + 2],
        middle[:, :, 4 : rows_y + 4, 2 : cols_z + 2],
    )
    along_z = stencil(
        middle[:, :, 2 : rows_y + 2, 0:cols_z],
        middle[:, :, 2 : rows_y + 2, 1 : cols_z + 1],
        middle[:, :, 2 : rows_y + 2, 3 : cols_z + 3],
        middle[:, :, 2 : rows_y + 2, 4 : cols_z + 4],
    )
    enstrophy, strain_rate = invariants(along_x, along_y, along_z)
    cells = rows_y * cols_z
    stacked = jnp.concatenate(
        [
            fields[:, 2 : planes + 2].reshape(3, planes, cells),
            enstrophy.reshape(1, planes, cells),
            strain_rate.reshape(1, planes, cells),
        ],
        axis=0,
    )
    local_grams = jnp.einsum(
        "fxc,fyc->fxy",
        stacked,
        stacked,
        precision=lax.Precision.HIGHEST,
        preferred_element_type=jnp.float32,
    )
    total_cells = cells * lax.axis_size("gy") * lax.axis_size("gz")
    grams = lax.psum(local_grams, ("gy", "gz"))
    squares = jnp.trace(grams, axis1=1, axis2=2)
    denominators = 5.0 * total_cells * (squares / (planes * total_cells) + 1e-06)
    cross = jnp.sum(grams / denominators[:, None, None], axis=0)
    factor = jnp.linalg.cholesky(cross)
    return (enstrophy, strain_rate, factor)


def solution(mesh):
    return jax.shard_map(
        per_device,
        mesh=mesh,
        in_specs=(P(None, None, "gy", "gz"),),
        out_specs=(P(None, "gy", "gz"), P(None, "gy", "gz"), P()),
        check_vma=False,
    )
```

profile of v0, /device:TPU:0, one launch (start us, length us, event | category | flops | bytes accessed | tf_op | source)
XLA Modules:
  0.0 233.3 jit_solution(14791016864557472085)
XLA Ops:
  7.2 2.9 %fusion.34 = (f32[3,132,2,128]{3,2,1,0:T(2,128)}, f32[3,132,2,128]{3,2,1,0:T(2,128)S(1)}) fusion(f32[3,132,16,128]{3,2,1,0:T(8,128)} %param.1), kind=kLoop, calls=%fused_computation.79 | loop fusion | bytes 1622016 | tf_op jit(solution)/shard_map/slice | solution.py:11
  10.6 2.0 collective-permute-start.1
  12.6 6.7 %copy.24 = f32[3,132,16,128]{1,3,2,0:T(8,128)} copy(f32[3,132,16,128]{3,2,1,0:T(8,128)} %param.1) | data formatting | bytes 6488064 | tf_op args[0]
  19.2 1.9 slice-done.2
  21.1 2.4 %reshape.233 = f32[3,128,2048]{2,1,0:T(8,128)} reshape(f32[3,128,16,128]{3,2,1,0:T(8,128)S(1)} %slice-done.2) | data formatting | bytes 6291456 | tf_op jit(solution)/shard_map/reshape | solution.py:72
  24.8 1.6 copy.31
  26.4 1.5 pad_maximum_fusion.10
  28.0 2.3 collective-permute-start.2
  30.3 3.1 %collective-permute-start.3 = (f32[3,132,20,2]{1,3,2,0:T(2,128)S(1)}, f32[3,132,20,2]{1,3,2,0:T(2,128)S(1)}, u32[]{:S(2)}, u32[]{:S(2)}) collective-permute-start(f32[3,132,20,2]{1,3,2,0:T(2,128)S(1)} %get-tuple-element.23), channel_id=1, source_target_pairs={{1,0},{2,1},{3,2},{4,3},{5,4},{6,5},{7,6},{0,7},{9,8},{10,9},{11,1... | collective-permute-start | bytes 190088 | tf_op jit(solution)/shard_map/ppermute | solution.py:16
  33.4 22.1 %fusion.16 = (f32[3,128,16,128]{1,3,2,0:T(8,128)S(1)}, f32[3,128,16,128]{1,3,2,0:T(8,128)S(1)}) fusion(f32[3,132,16,128]{1,3,2,0:T(8,128)} %copy.24, f32[3,132,2,128]{1,3,2,0:T(8,128)} %copy-done.1, f32[3,132,2,128]{1,3,2,0:T(8,128)} %copy-done), kind=kLoop, calls=%fused_computation.27 | loop fusion | flops 12582912 | bytes 26738688 | tf_op jit(solution)/shard_map/div | solution.py:24
  55.5 5.1 %fusion.7 = f32[3,128,16,128]{1,3,2,0:T(8,128)S(1)} fusion(f32[3,132,20,2]{1,3,2,0:T(2,128)S(1)} %collective-permute-done.3, f32[3,132,2,128]{1,3,2,0:T(8,128)} %copy-done.1, f32[3,132,16,128]{1,3,2,0:T(8,128)S(1)} %bitcast.28, f32[3,132,2,128]{1,3,2,0:T(8,128)} %copy-done, f32[3,132,20,2]{1,3,2,0:T(2,128)S(1)} %collective-permute-done.2), kind=kLoop, calls=%fused_computation.8 | loop fusion | flops 14155776 | bytes 7327488 | tf_op jit(solution)/shard_map/div | solution.py:24
  60.6 4.2 %fusion.23 = (f32[128,16,128]{0,2,1:T(8,128)}, f32[1,128,16,128]{1,3,2,0:T(8,128)}, f32[1,128,16,128]{1,3,2,0:T(8,128)}, f32[1,128,16,128]{1,3,2,0:T(8,128)}, f3...) fusion(f32[3,128,16,128]{1,3,2,0:T(8,128)S(1)} %fusion.7, ...), kind=kLoop, calls=%fused_computation.48 | loop fusion | flops 7340032 | bytes 18874368 | tf_op jit(solution)/shard_map/add | solution.py:39
  64.8 2.6 %copy.45 = f32[1,128,2048]{2,1,0:T(8,128)} copy(f32[1,128,2048]{1,2,0:T(8,128)} %bitcast.35) | data formatting | bytes 2097152 | tf_op jit(solution)/shard_map/sub | solution.py:36
  67.4 2.7 %copy.46 = f32[1,128,2048]{2,1,0:T(8,128)} copy(f32[1,128,2048]{1,2,0:T(8,128)} %bitcast.34) | data formatting | bytes 2097152 | tf_op jit(solution)/shard_map/sub | solution.py:36
  70.1 1.3 copy.47
  71.4 2.6 %copy.48 = f32[1,128,2048]{2,1,0:T(8,128)} copy(f32[1,128,2048]{1,2,0:T(8,128)} %bitcast.32) | data formatting | bytes 2097152 | tf_op jit(solution)/shard_map/add | solution.py:30
  74.0 1.3 copy.49
  75.4 1.3 copy.50
  77.0 3.4 %fusion.25 = (f32[1,128,2048]{2,1,0:T(8,128)S(1)}, f32[1,128,2048]{2,1,0:T(8,128)S(1)}) fusion(f32[1,128,2048]{2,1,0:T(8,128)S(1)} %copy-done.7, f32[1,128,2048]{2,1,0:T(8,128)} %copy.46, f32[1,128,2048]{2,1,0:T(8,128)} %copy.47, f32[1,128,2048]{2,1,0:T(8,128)S(1)} %copy.51, f32[1,128,2048]{2,1,0:T(8,128)} %copy.50, f32[1,128,2048]{2,1,0:T(8,128)} %copy.48, ...), kind=kLoop, calls=%fused_computation.50 | loop fusion | flops 4456448 | bytes 9437184 | tf_op jit(solution)/shard_map/add | solution.py:38
  80.5 5.6 %fusion = f32[5,128,128]{2,1,0:T(8,128)} fusion(f32[1,128,2048]{2,1,0:T(8,128)S(1)} %get-tuple-element.29, f32[1,128,2048]{2,1,0:T(8,128)S(1)} %get-tuple-element.28, f32[3,128,2048]{2,1,0:T(8,128)S(1)} %copy-done.9), kind=kOutput, calls=%fused_computation | convolution fusion | flops 2015887360 | bytes 5570560 | tf_op jit(solution)/shard_map/fxc,fyc->fxy/dot_general | solution.py:78
  86.1 1.4 copy.43
  87.5 1.4 copy.44
  88.9 121.6 %all-reduce.2.cloned.1.call-done = f32[5,128,128]{2,1,0:T(8,128)} async-done(((f32[5,128,128]{2,1,0:T(8,128)}), f32[5,128,128]{2,1,0:T(8,128)}) %all-reduce.2.cloned.1.call-update) | async-done | bytes 327696 | tf_op jit(solution)/shard_map/psum | solution.py:86
  212.9 11.7 %cholesky.20 = f32[128,128]{1,0:T(8,128)S(1)} custom-call(f32[128,128]{1,0:T(8,128)S(1)} %fusion.31), custom_call_target="Cholesky" | custom-call | tf_op jit(solution)/shard_map/jit(cholesky)/cholesky | solution.py:90
  (44 shorter events, 6.4 us)
Async XLA Ops:
  7.2 203.4 %all-reduce.2.cloned.1.call-start = ((), (), s32[]{:S(2)}) async-start(), calls=%async_computation | async-start | bytes 655360 | tf_op jit(solution)/shard_map/psum | solution.py:86
  10.2 13.3 %collective-permute-start = (f32[3,132,2,128]{3,2,1,0:T(2,128)}, f32[3,132,2,128]{3,2,1,0:T(2,128)}, u32[]{:S(2)}, u32[]{:S(2)}) collective-permute-start(f32[3,132,2,128]{3,2,1,0:T(2,128)} %get-tuple-element.26), channel_id=1, source_target_pairs={{0,8},{8,16},{16,24},{24,0},{1,9},{9,17},{17,25},{25,1},{2,10},{10... | collective-permute-start | bytes 1216520 | tf_op jit(solution)/shard_map/ppermute | solution.py:14
  10.6 14.2 %collective-permute-start.1 = (f32[3,132,2,128]{3,2,1,0:T(2,128)S(1)}, f32[3,132,2,128]{3,2,1,0:T(2,128)}, u32[]{:S(2)}, u32[]{:S(2)}) collective-permute-start(f32[3,132,2,128]{3,2,1,0:T(2,128)S(1)} %get-tuple-element.27), channel_id=1, source_target_pairs={{8,0},{16,8},{24,16},{0,24},{9,1},{17,9},{25,17},{1,25},{10,2},{18... | collective-permute-start | bytes 1216520 | tf_op jit(solution)/shard_map/ppermute | solution.py:16
  19.2 1.9 slice-start.2
  24.8 3.2 %copy-start = (f32[3,132,2,128]{1,3,2,0:T(8,128)}, f32[3,132,2,128]{1,3,2,0:T(8,128)S(1)}, u32[]{:S(2)}) copy-start(f32[3,132,2,128]{1,3,2,0:T(8,128)S(1)} %copy.28) | copy-start | bytes 1216516
  26.4 1.6 copy-start.1
  26.4 29.1 %slice-start = ((s8[6291456]{0:T(1024)(128)(4,1)}), s8[4194304]{0:T(1024)(128)(4,1)S(1)}, s32[]{:S(2)}) async-start(s8[6291456]{0:T(1024)(128)(4,1)} %bitcast.27), calls=%async_computation.1 | async-start | bytes 8388608
  28.0 27.5 %collective-permute-start.2 = (f32[3,132,20,2]{1,3,2,0:T(2,128)S(1)}, f32[3,132,20,2]{1,3,2,0:T(2,128)S(1)}, u32[]{:S(2)}, u32[]{:S(2)}) collective-permute-start(f32[3,132,20,2]{1,3,2,0:T(2,128)S(1)} %get-tuple-element.22), channel_id=1, source_target_pairs={{0,1},{1,2},{2,3},{3,4},{4,5},{5,6},{6,7},{7,0},{8,9},{9,10},{10,1... | collective-permute-start | bytes 190088 | tf_op jit(solution)/shard_map/ppermute | solution.py:14
  30.3 25.2 %slice-start.1 = ((s8[6291456]{0:T(1024)(128)(4,1)}), s8[2097152]{0:T(1024)(128)(4,1)S(1)}, s32[]{:S(2)}) async-start(s8[6291456]{0:T(1024)(128)(4,1)} %bitcast.27), calls=%async_computation.2 | async-start | bytes 4194304
  30.3 25.2 %collective-permute-start.3 = (f32[3,132,20,2]{1,3,2,0:T(2,128)S(1)}, f32[3,132,20,2]{1,3,2,0:T(2,128)S(1)}, u32[]{:S(2)}, u32[]{:S(2)}) collective-permute-start(f32[3,132,20,2]{1,3,2,0:T(2,128)S(1)} %get-tuple-element.23), channel_id=1, source_target_pairs={{1,0},{2,1},{3,2},{4,3},{5,4},{6,5},{7,6},{0,7},{9,8},{10,9},{11,1... | collective-permute-start | bytes 190088 | tf_op jit(solution)/shard_map/ppermute | solution.py:16
  64.8 5.3 %copy-start.8 = (f32[1,128,16,128]{1,3,2,0:T(8,128)S(1)}, f32[1,128,16,128]{1,3,2,0:T(8,128)}, u32[]{:S(2)}) copy-start(f32[1,128,16,128]{1,3,2,0:T(8,128)} %get-tuple-element.19) | copy-start | bytes 3145732
  67.4 6.6 %copy-start.6 = (f32[1,128,16,128]{1,3,2,0:T(8,128)S(1)}, f32[1,128,16,128]{1,3,2,0:T(8,128)}, u32[]{:S(2)}) copy-start(f32[1,128,16,128]{1,3,2,0:T(8,128)} %get-tuple-element.11) | copy-start | bytes 3145732
  70.1 5.3 %copy-start.5 = (f32[1,128,16,128]{1,3,2,0:T(8,128)S(1)}, f32[1,128,16,128]{1,3,2,0:T(8,128)}, u32[]{:S(2)}) copy-start(f32[1,128,16,128]{1,3,2,0:T(8,128)} %get-tuple-element.12) | copy-start | bytes 3145732
  71.4 5.3 %copy-start.4 = (f32[1,128,16,128]{1,3,2,0:T(8,128)S(1)}, f32[1,128,16,128]{1,3,2,0:T(8,128)}, u32[]{:S(2)}) copy-start(f32[1,128,16,128]{1,3,2,0:T(8,128)} %get-tuple-element.13) | copy-start | bytes 3145732
  75.3 1.7 copy-start.7
  77.0 3.5 %copy-start.9 = (f32[3,128,2048]{2,1,0:T(8,128)S(1)}, f32[3,128,2048]{2,1,0:T(8,128)}, u32[]{:S(2)}) copy-start(f32[3,128,2048]{2,1,0:T(8,128)} %reshape.233) | copy-start | bytes 9437188
  80.5 5.7 %copy-start.3 = (f32[128,16,128]{0,2,1:T(8,128)S(1)}, f32[128,16,128]{0,2,1:T(8,128)}, u32[]{:S(2)}) copy-start(f32[128,16,128]{0,2,1:T(8,128)} %get-tuple-element.18) | copy-start | bytes 3145732
  86.1 1.4 copy-start.2
Sparse Core Ops, SparseCore 0:
  86.2 124.2 all-reduce.1
where the time goes:
time: 234 us; the launch traced here: 233 us
  waiting for transfers between devices  122 us (52%)
  other arithmetic  52.1 us (22%)
  local copies, waits for them, and re-layouts  31.8 us (14%)
  between operations  14.2 us (6%)
  starting transfers between devices  7.89 us (3%)
  matrix products  5.6 us (2%)
    psum x1, waiting for transfers between devices, per_device(): grams = lax.psum(local_grams, ('gy', 'gz'))  122 us
    div x2, other arithmetic, stencil(): return (minus_two - 8.0 * minus_one + 8.0 * plus_one - plus_two) / 12.0  27.2 us
    another operation x4, other arithmetic, per_device(): factor = jnp.linalg.cholesky(cross)  12.4 us
    unnamed x27, local copies, waits for them, and re-layouts  9.46 us
    sub x3, local copies, waits for them, and re-layouts, invariants(): gradient[source_axis][target_axis] - gradient[target_axis][source_axis]  6.56 us
    dot_general x1, matrix products, per_device(): jnp.einsum('fxc,fyc->fxy', stacked, stacked, precision=lax.Precision.HIGH...  5.6 us
    ppermute x2, starting transfers between devices, with_halo(): lax.ppermute(head, axis, [((i + 1) % count, i) for i in range(count)])  5.07 us
  transfers between devices with their start and end apart: 5, of which 1 were waited for; matrix products, arithmetic and copies ran while one was open for 15% of the time, Pallas kernels for 0%

commit v1 on v0

--- a/solution.py
+++ b/solution.py
@@ -18,6 +18,19 @@
             axis=dim,
         )
     return cells
+
+
+def butterfly_sum(values, axes):
+    for axis in axes:
+        count = lax.axis_size(axis)
+        if count & (count - 1):
+            values = lax.psum(values, axis)
+            continue
+        step = 1
+        while step < count:
+            values = values + lax.ppermute(values, axis, [(i, i ^ step) for i in range(count)])
+            step *= 2
+    return values
 
 
 def stencil(minus_two, minus_one, plus_one, plus_two):
@@ -83,7 +96,7 @@
         preferred_element_type=jnp.float32,
     )
     total_cells = cells * lax.axis_size("gy") * lax.axis_size("gz")
-    grams = lax.psum(local_grams, ("gy", "gz"))
+    grams = butterfly_sum(local_grams, ("gy", "gz"))
     squares = jnp.trace(grams, axis1=1, axis2=2)
     denominators = 5.0 * total_cells * (squares / (planes * total_cells) + 1e-06)
     cross = jnp.sum(grams / denominators[:, None, None], axis=0)

time: 234 us -> 138 us (0.59)
  waiting for transfers between devices: 122 us -> 37.9 us
  between operations: 14.2 us -> 0.9 us
  starting transfers between devices: 7.89 us -> 10.7 us
    psum x1 -> x0, waiting for transfers between devices: 122 us -> none  [per_device(): grams = lax.psum(local_grams, ('gy', 'gz'))]
    ppermute x0 -> x5, waiting for transfers between devices: none -> 37.9 us  [butterfly_sum(): lax.ppermute(values, axis, [(i, i ^ step) for i in range(count)])]
    ppermute x0 -> x5, starting transfers between devices: none -> 2.89 us  [butterfly_sum(): lax.ppermute(values, axis, [(i, i ^ step) for i in range(count)])]
  transfers between devices with their start and end apart: 5 -> 9, of which waited for: 1 -> 5; matrix products, arithmetic and copies ran while one was open for 15% -> 26% of each run, Pallas kernels for 0% -> 0%
where the time goes in v1:
time: 138 us; the launch traced here: 137 us
  other arithmetic  51 us (37%)
  waiting for transfers between devices  37.9 us (27%)
  local copies, waits for them, and re-layouts  31.7 us (23%)
  starting transfers between devices  10.7 us (8%)
  matrix products  4.88 us (4%)
    ppermute x5, waiting for transfers between devices, butterfly_sum(): lax.ppermute(values, axis, [(i, i ^ step) for i in range(count)])  37.9 us
    div x2, other arithmetic, stencil(): return (minus_two - 8.0 * minus_one + 8.0 * plus_one - plus_two) / 12.0  27.5 us
    another operation x4, other arithmetic, per_device(): factor = jnp.linalg.cholesky(cross)  12.7 us
    unnamed x27, local copies, waits for them, and re-layouts  9.46 us
    sub x3, local copies, waits for them, and re-layouts, invariants(): gradient[source_axis][target_axis] - gradient[target_axis][source_axis]  6.59 us
    ppermute x2, starting transfers between devices, with_halo(): lax.ppermute(head, axis, [((i + 1) % count, i) for i in range(count)])  5.07 us
    dot_general x1, matrix products, per_device(): jnp.einsum('fxc,fyc->fxy', stacked, stacked, precision=lax.Precision.HIGH...  4.88 us
    add x1, other arithmetic, invariants(): strain_rate = strain_rate + 0.5 * shearing * shearing  4.16 us
  transfers between devices with their start and end apart: 9, of which 5 were waited for; matrix products, arithmetic and copies ran while one was open for 26% of the time, Pallas kernels for 0%

profile of v1, /device:TPU:0, one launch (start us, length us, event | category | flops | bytes accessed | tf_op | source)
XLA Modules:
  0.0 137.2 jit_solution(2012296382970654470)
XLA Ops:
  0.6 2.9 %fusion.34 = (f32[3,132,2,128]{3,2,1,0:T(2,128)}, f32[3,132,2,128]{3,2,1,0:T(2,128)S(1)}) fusion(f32[3,132,16,128]{3,2,1,0:T(8,128)} %param.1), kind=kLoop, calls=%fused_computation.79 | loop fusion | bytes 1622016 | tf_op jit(solution)/shard_map/slice | solution.py:11
  4.0 2.0 %collective-permute-start.1 = (f32[3,132,2,128]{3,2,1,0:T(2,128)S(1)}, f32[3,132,2,128]{3,2,1,0:T(2,128)}, u32[]{:S(2)}, u32[]{:S(2)}) collective-permute-start(f32[3,132,2,128]{3,2,1,0:T(2,128)S(1)} %get-tuple-element.29), channel_id=1, source_target_pairs={{8,0},{16,8},{24,16},{0,24},{9,1},{17,9},{25,17},{1,25},{10,2},{18... | collective-permute-start | bytes 1216520 | tf_op jit(solution)/shard_map/ppermute | solution.py:16
  6.0 6.7 %copy.24 = f32[3,132,16,128]{1,3,2,0:T(8,128)} copy(f32[3,132,16,128]{3,2,1,0:T(8,128)} %param.1) | data formatting | bytes 6488064 | tf_op args[0]
  12.6 1.9 %slice-done.2 = f32[3,128,16,128]{3,2,1,0:T(8,128)S(1)} async-done(((f32[3,132,16,128]{3,2,1,0:T(8,128)}), f32[3,128,16,128]{3,2,1,0:T(8,128)S(1)}, s32[]{:S(2)}) %slice-start.2) | async-done | bytes 3145752 | tf_op jit(solution)/shard_map/slice | solution.py:85
  14.5 2.4 %reshape.233 = f32[3,128,2048]{2,1,0:T(8,128)} reshape(f32[3,128,16,128]{3,2,1,0:T(8,128)S(1)} %slice-done.2) | data formatting | bytes 6291456 | tf_op jit(solution)/shard_map/reshape | solution.py:85
  18.2 1.6 %copy.31 = f32[3,132,2,128]{1,3,2,0:T(8,128)S(1)} copy(f32[3,132,2,128]{3,2,1,0:T(2,128)} %collective-permute-done.1) | data formatting | bytes 811008 | tf_op jit(solution)/shard_map/ppermute | solution.py:16
  19.8 1.5 %pad_maximum_fusion.10 = (f32[3,132,20,2]{1,3,2,0:T(2,128)S(1)}, f32[3,132,20,2]{1,3,2,0:T(2,128)S(1)}) fusion(f32[3,132,2,128]{1,3,2,0:T(8,128)S(1)} %copy.31, f32[3,132,16,128]{1,3,2,0:T(8,128)} %copy.24, f32[3,132,2,128]{1,3,2,0:T(8,128)S(1)} %copy.28), kind=kLoop, calls=%fused_computation.69 | loop fusion | flops 63360 | bytes 4181760 | tf_op jit(solution)/shard_map/slice | solution.py:11
  21.3 2.3 %collective-permute-start.2 = (f32[3,132,20,2]{1,3,2,0:T(2,128)S(1)}, f32[3,132,20,2]{1,3,2,0:T(2,128)S(1)}, u32[]{:S(2)}, u32[]{:S(2)}) collective-permute-start(f32[3,132,20,2]{1,3,2,0:T(2,128)S(1)} %get-tuple-element.24), channel_id=1, source_target_pairs={{0,1},{1,2},{2,3},{3,4},{4,5},{5,6},{6,7},{7,0},{8,9},{9,10},{10,1... | collective-permute-start | bytes 190088 | tf_op jit(solution)/shard_map/ppermute | solution.py:14
  23.7 3.1 %collective-permute-start.3 = (f32[3,132,20,2]{1,3,2,0:T(2,128)S(1)}, f32[3,132,20,2]{1,3,2,0:T(2,128)S(1)}, u32[]{:S(2)}, u32[]{:S(2)}) collective-permute-start(f32[3,132,20,2]{1,3,2,0:T(2,128)S(1)} %get-tuple-element.25), channel_id=1, source_target_pairs={{1,0},{2,1},{3,2},{4,3},{5,4},{6,5},{7,6},{0,7},{9,8},{10,9},{11,1... | collective-permute-start | bytes 190088 | tf_op jit(solution)/shard_map/ppermute | solution.py:16
  26.8 22.4 %fusion.16 = (f32[3,128,16,128]{1,3,2,0:T(8,128)S(1)}, f32[3,128,16,128]{1,3,2,0:T(8,128)S(1)}) fusion(f32[3,132,16,128]{1,3,2,0:T(8,128)} %copy.24, f32[3,132,2,128]{1,3,2,0:T(8,128)} %copy-done.1, f32[3,132,2,128]{1,3,2,0:T(8,128)} %copy-done), kind=kLoop, calls=%fused_computation.27 | loop fusion | flops 12582912 | bytes 26738688 | tf_op jit(solution)/shard_map/div | solution.py:37
  49.2 5.1 %fusion.7 = f32[3,128,16,128]{1,3,2,0:T(8,128)S(1)} fusion(f32[3,132,20,2]{1,3,2,0:T(2,128)S(1)} %collective-permute-done.3, f32[3,132,2,128]{1,3,2,0:T(8,128)} %copy-done.1, f32[3,132,16,128]{1,3,2,0:T(8,128)S(1)} %bitcast.28, f32[3,132,2,128]{1,3,2,0:T(8,128)} %copy-done, f32[3,132,20,2]{1,3,2,0:T(2,128)S(1)} %collective-permute-done.2), kind=kLoop, calls=%fused_computation.8 | loop fusion | flops 14155776 | bytes 7327488 | tf_op jit(solution)/shard_map/div | solution.py:37
  54.3 4.2 %fusion.23 = (f32[128,16,128]{0,2,1:T(8,128)}, f32[1,128,16,128]{1,3,2,0:T(8,128)}, f32[1,128,16,128]{1,3,2,0:T(8,128)}, f32[1,128,16,128]{1,3,2,0:T(8,128)}, f3...) fusion(f32[3,128,16,128]{1,3,2,0:T(8,128)S(1)} %fusion.7, ...), kind=kLoop, calls=%fused_computation.48 | loop fusion | flops 7340032 | bytes 18874368 | tf_op jit(solution)/shard_map/add | solution.py:52
  58.5 2.6 %copy.45 = f32[1,128,2048]{2,1,0:T(8,128)} copy(f32[1,128,2048]{1,2,0:T(8,128)} %bitcast.35) | data formatting | bytes 2097152 | tf_op jit(solution)/shard_map/sub | solution.py:49
  61.1 2.7 %copy.46 = f32[1,128,2048]{2,1,0:T(8,128)} copy(f32[1,128,2048]{1,2,0:T(8,128)} %bitcast.34) | data formatting | bytes 2097152 | tf_op jit(solution)/shard_map/sub | solution.py:49
  65.1 2.6 %copy.48 = f32[1,128,2048]{2,1,0:T(8,128)} copy(f32[1,128,2048]{1,2,0:T(8,128)} %bitcast.32) | data formatting | bytes 2097152 | tf_op jit(solution)/shard_map/add | solution.py:43
  70.7 3.4 %fusion.25 = (f32[1,128,2048]{2,1,0:T(8,128)S(1)}, f32[1,128,2048]{2,1,0:T(8,128)S(1)}) fusion(f32[1,128,2048]{2,1,0:T(8,128)S(1)} %copy-done.7, f32[1,128,2048]{2,1,0:T(8,128)} %copy.46, f32[1,128,2048]{2,1,0:T(8,128)} %copy.47, f32[1,128,2048]{2,1,0:T(8,128)S(1)} %copy.51, f32[1,128,2048]{2,1,0:T(8,128)} %copy.50, f32[1,128,2048]{2,1,0:T(8,128)} %copy.48, ...), kind=kLoop, calls=%fused_computation.50 | loop fusion | flops 4456448 | bytes 9437184 | tf_op jit(solution)/shard_map/add | solution.py:51
  74.2 4.9 %fusion = f32[5,128,128]{2,1,0:T(8,128)S(1)} fusion(f32[1,128,2048]{2,1,0:T(8,128)S(1)} %get-tuple-element.31, f32[1,128,2048]{2,1,0:T(8,128)S(1)} %get-tuple-element.30, f32[3,128,2048]{2,1,0:T(8,128)S(1)} %copy-done.9), kind=kOutput, calls=%fused_computation | convolution fusion | flops 2015887360 | bytes 5570560 | tf_op jit(solution)/shard_map/fxc,fyc->fxy/dot_general | solution.py:91
  79.1 1.6 %collective-permute-done.4 = f32[5,128,128]{2,1,0:T(8,128)S(1)} collective-permute-done((f32[5,128,128]{2,1,0:T(8,128)S(1)}, f32[5,128,128]{2,1,0:T(8,128)S(1)}, u32[]{:S(2)}, u32[]{:S(2)}) %collective-permute-start.4) | collective-permute-done | bytes 327712 | tf_op jit(solution)/shard_map/ppermute | solution.py:31
  80.8 1.7 %collective-permute-start.5 = (f32[5,128,128]{2,1,0:T(8,128)S(1)}, f32[5,128,128]{2,1,0:T(8,128)S(1)}, u32[]{:S(2)}, u32[]{:S(2)}) collective-permute-start(f32[5,128,128]{2,1,0:T(8,128)S(1)} %add.202), channel_id=1, source_target_pairs={{0,16},{8,24},{16,0},{24,8},{1,17},{9,25},{17,1},{25,9},{2,18},{10... | collective-permute-start | bytes 983048 | tf_op jit(solution)/shard_map/ppermute | solution.py:31
  82.5 8.1 %collective-permute-done.5 = f32[5,128,128]{2,1,0:T(8,128)S(1)} collective-permute-done((f32[5,128,128]{2,1,0:T(8,128)S(1)}, f32[5,128,128]{2,1,0:T(8,128)S(1)}, u32[]{:S(2)}, u32[]{:S(2)}) %collective-permute-start.5) | collective-permute-done | bytes 327712 | tf_op jit(solution)/shard_map/ppermute | solution.py:31
  90.7 8.9 %collective-permute-done.6 = f32[5,128,128]{2,1,0:T(8,128)S(1)} collective-permute-done((f32[5,128,128]{2,1,0:T(8,128)S(1)}, f32[5,128,128]{2,1,0:T(8,128)S(1)}, u32[]{:S(2)}, u32[]{:S(2)}) %collective-permute-start.6) | collective-permute-done | bytes 327712 | tf_op jit(solution)/shard_map/ppermute | solution.py:31
  99.8 8.0 %collective-permute-done.7 = f32[5,128,128]{2,1,0:T(8,128)S(1)} collective-permute-done((f32[5,128,128]{2,1,0:T(8,128)S(1)}, f32[5,128,128]{2,1,0:T(8,128)S(1)}, u32[]{:S(2)}, u32[]{:S(2)}) %collective-permute-start.7) | collective-permute-done | bytes 327712 | tf_op jit(solution)/shard_map/ppermute | solution.py:31
  111.6 11.3 %collective-permute-done.8 = f32[5,128,128]{2,1,0:T(8,128)S(1)} collective-permute-done((f32[5,128,128]{2,1,0:T(8,128)S(1)}, f32[5,128,128]{2,1,0:T(8,128)S(1)}, u32[]{:S(2)}, u32[]{:S(2)}) %collective-permute-start.8) | collective-permute-done | bytes 327712 | tf_op jit(solution)/shard_map/ppermute | solution.py:31
  123.2 11.9 %cholesky.20 = f32[128,128]{1,0:T(8,128)S(1)} custom-call(f32[128,128]{1,0:T(8,128)S(1)} %fusion.31), custom_call_target="Cholesky" | custom-call | tf_op jit(solution)/shard_map/jit(cholesky)/cholesky | solution.py:103
  (55 shorter events, 12.6 us)
Async XLA Ops:
  3.6 13.3 %collective-permute-start = (f32[3,132,2,128]{3,2,1,0:T(2,128)}, f32[3,132,2,128]{3,2,1,0:T(2,128)}, u32[]{:S(2)}, u32[]{:S(2)}) collective-permute-start(f32[3,132,2,128]{3,2,1,0:T(2,128)} %get-tuple-element.28), channel_id=1, source_target_pairs={{0,8},{8,16},{16,24},{24,0},{1,9},{9,17},{17,25},{25,1},{2,10},{10... | collective-permute-start | bytes 1216520 | tf_op jit(solution)/shard_map/ppermute | solution.py:14
  4.0 14.2 %collective-permute-start.1 = (f32[3,132,2,128]{3,2,1,0:T(2,128)S(1)}, f32[3,132,2,128]{3,2,1,0:T(2,128)}, u32[]{:S(2)}, u32[]{:S(2)}) collective-permute-start(f32[3,132,2,128]{3,2,1,0:T(2,128)S(1)} %get-tuple-element.29), channel_id=1, source_target_pairs={{8,0},{16,8},{24,16},{0,24},{9,1},{17,9},{25,17},{1,25},{10,2},{18... | collective-permute-start | bytes 1216520 | tf_op jit(solution)/shard_map/ppermute | solution.py:16
  12.6 1.9 %slice-start.2 = ((f32[3,132,16,128]{3,2,1,0:T(8,128)}), f32[3,128,16,128]{3,2,1,0:T(8,128)S(1)}, s32[]{:S(2)}) async-start(f32[3,132,16,128]{3,2,1,0:T(8,128)} %param.1), calls=%async_computation.2 | async-start | bytes 6291456 | tf_op jit(solution)/shard_map/slice | solution.py:85
  18.2 3.2 %copy-start = (f32[3,132,2,128]{1,3,2,0:T(8,128)}, f32[3,132,2,128]{1,3,2,0:T(8,128)S(1)}, u32[]{:S(2)}) copy-start(f32[3,132,2,128]{1,3,2,0:T(8,128)S(1)} %copy.28) | copy-start | bytes 1216516
  19.8 1.6 %copy-start.1 = (f32[3,132,2,128]{1,3,2,0:T(8,128)}, f32[3,132,2,128]{1,3,2,0:T(8,128)S(1)}, u32[]{:S(2)}) copy-start(f32[3,132,2,128]{1,3,2,0:T(8,128)S(1)} %copy.31) | copy-start | bytes 1216516
  19.8 29.4 %slice-start = ((s8[6291456]{0:T(1024)(128)(4,1)}), s8[4194304]{0:T(1024)(128)(4,1)S(1)}, s32[]{:S(2)}) async-start(s8[6291456]{0:T(1024)(128)(4,1)} %bitcast.27), calls=%async_computation | async-start | bytes 8388608
  21.3 27.8 %collective-permute-start.2 = (f32[3,132,20,2]{1,3,2,0:T(2,128)S(1)}, f32[3,132,20,2]{1,3,2,0:T(2,128)S(1)}, u32[]{:S(2)}, u32[]{:S(2)}) collective-permute-start(f32[3,132,20,2]{1,3,2,0:T(2,128)S(1)} %get-tuple-element.24), channel_id=1, source_target_pairs={{0,1},{1,2},{2,3},{3,4},{4,5},{5,6},{6,7},{7,0},{8,9},{9,10},{10,1... | collective-permute-start | bytes 190088 | tf_op jit(solution)/shard_map/ppermute | solution.py:14
  23.7 25.5 %slice-start.1 = ((s8[6291456]{0:T(1024)(128)(4,1)}), s8[2097152]{0:T(1024)(128)(4,1)S(1)}, s32[]{:S(2)}) async-start(s8[6291456]{0:T(1024)(128)(4,1)} %bitcast.27), calls=%async_computation.1 | async-start | bytes 4194304
  23.7 25.5 %collective-permute-start.3 = (f32[3,132,20,2]{1,3,2,0:T(2,128)S(1)}, f32[3,132,20,2]{1,3,2,0:T(2,128)S(1)}, u32[]{:S(2)}, u32[]{:S(2)}) collective-permute-start(f32[3,132,20,2]{1,3,2,0:T(2,128)S(1)} %get-tuple-element.25), channel_id=1, source_target_pairs={{1,0},{2,1},{3,2},{4,3},{5,4},{6,5},{7,6},{0,7},{9,8},{10,9},{11,1... | collective-permute-start | bytes 190088 | tf_op jit(solution)/shard_map/ppermute | solution.py:16
  58.5 5.3 %copy-start.8 = (f32[1,128,16,128]{1,3,2,0:T(8,128)S(1)}, f32[1,128,16,128]{1,3,2,0:T(8,128)}, u32[]{:S(2)}) copy-start(f32[1,128,16,128]{1,3,2,0:T(8,128)} %get-tuple-element.21) | copy-start | bytes 3145732
  61.1 6.6 %copy-start.6 = (f32[1,128,16,128]{1,3,2,0:T(8,128)S(1)}, f32[1,128,16,128]{1,3,2,0:T(8,128)}, u32[]{:S(2)}) copy-start(f32[1,128,16,128]{1,3,2,0:T(8,128)} %get-tuple-element.13) | copy-start | bytes 3145732
  63.8 5.3 %copy-start.5 = (f32[1,128,16,128]{1,3,2,0:T(8,128)S(1)}, f32[1,128,16,128]{1,3,2,0:T(8,128)}, u32[]{:S(2)}) copy-start(f32[1,128,16,128]{1,3,2,0:T(8,128)} %get-tuple-element.14) | copy-start | bytes 3145732
  65.1 5.3 %copy-start.4 = (f32[1,128,16,128]{1,3,2,0:T(8,128)S(1)}, f32[1,128,16,128]{1,3,2,0:T(8,128)}, u32[]{:S(2)}) copy-start(f32[1,128,16,128]{1,3,2,0:T(8,128)} %get-tuple-element.15) | copy-start | bytes 3145732
  69.0 1.7 %copy-start.7 = (f32[1,128,2048]{2,1,0:T(8,128)S(1)}, f32[1,128,2048]{2,1,0:T(8,128)}, u32[]{:S(2)}) copy-start(f32[1,128,2048]{2,1,0:T(8,128)} %copy.45) | copy-start | bytes 3145732
  70.7 3.5 %copy-start.9 = (f32[3,128,2048]{2,1,0:T(8,128)S(1)}, f32[3,128,2048]{2,1,0:T(8,128)}, u32[]{:S(2)}) copy-start(f32[3,128,2048]{2,1,0:T(8,128)} %reshape.233) | copy-start | bytes 9437188
  79.0 29.7 %copy-start.3 = (f32[128,16,128]{0,2,1:T(8,128)S(1)}, f32[128,16,128]{0,2,1:T(8,128)}, u32[]{:S(2)}) copy-start(f32[128,16,128]{0,2,1:T(8,128)} %get-tuple-element.20) | copy-start | bytes 3145732
  79.1 31.1 %copy-start.2 = (f32[128,16,128]{0,2,1:T(8,128)S(1)}, f32[128,16,128]{0,2,1:T(8,128)}, u32[]{:S(2)}) copy-start(f32[128,16,128]{0,2,1:T(8,128)} %get-tuple-element.11) | copy-start | bytes 3145732
  79.1 1.7 %collective-permute-start.4 = (f32[5,128,128]{2,1,0:T(8,128)S(1)}, f32[5,128,128]{2,1,0:T(8,128)S(1)}, u32[]{:S(2)}, u32[]{:S(2)}) collective-permute-start(f32[5,128,128]{2,1,0:T(8,128)S(1)} %fusion), channel_id=1, source_target_pairs={{0,8},{8,0},{16,24},{24,16},{1,9},{9,1},{17,25},{25,17},{2,10},{10... | collective-permute-start | bytes 983048 | tf_op jit(solution)/shard_map/ppermute | solution.py:31
  80.8 9.8 %collective-permute-start.5 = (f32[5,128,128]{2,1,0:T(8,128)S(1)}, f32[5,128,128]{2,1,0:T(8,128)S(1)}, u32[]{:S(2)}, u32[]{:S(2)}) collective-permute-start(f32[5,128,128]{2,1,0:T(8,128)S(1)} %add.202), channel_id=1, source_target_pairs={{0,16},{8,24},{16,0},{24,8},{1,17},{9,25},{17,1},{25,9},{2,18},{10... | collective-permute-start | bytes 983048 | tf_op jit(solution)/shard_map/ppermute | solution.py:31
  90.7 9.0 %collective-permute-start.6 = (f32[5,128,128]{2,1,0:T(8,128)S(1)}, f32[5,128,128]{2,1,0:T(8,128)S(1)}, u32[]{:S(2)}, u32[]{:S(2)}) collective-permute-start(f32[5,128,128]{2,1,0:T(8,128)S(1)} %add.203), channel_id=1, source_target_pairs={{0,1},{1,0},{2,3},{3,2},{4,5},{5,4},{6,7},{7,6},{8,9},{9,8},{10,11... | collective-permute-start | bytes 983048 | tf_op jit(solution)/shard_map/ppermute | solution.py:31
  99.7 8.1 %collective-permute-start.7 = (f32[5,128,128]{2,1,0:T(8,128)S(1)}, f32[5,128,128]{2,1,0:T(8,128)S(1)}, u32[]{:S(2)}, u32[]{:S(2)}) collective-permute-start(f32[5,128,128]{2,1,0:T(8,128)S(1)} %add.204), channel_id=1, source_target_pairs={{0,2},{1,3},{2,0},{3,1},{4,6},{5,7},{6,4},{7,5},{8,10},{9,11},{10,... | collective-permute-start | bytes 983048 | tf_op jit(solution)/shard_map/ppermute | solution.py:31
  107.8 15.1 %collective-permute-start.8 = (f32[5,128,128]{2,1,0:T(8,128)S(1)}, f32[5,128,128]{2,1,0:T(8,128)S(1)}, u32[]{:S(2)}, u32[]{:S(2)}) collective-permute-start(f32[5,128,128]{2,1,0:T(8,128)S(1)} %add.205), channel_id=1, source_target_pairs={{0,4},{1,5},{2,6},{3,7},{4,0},{5,1},{6,2},{7,3},{8,12},{9,13},{10,... | collective-permute-start | bytes 983048 | tf_op jit(solution)/shard_map/ppermute | solution.py:31

commit v2 on v1

v2 whole, which is shorter than its diff:
```python
import functools

import jax
import jax.numpy as jnp
from jax import lax
from jax.experimental import pallas as pl
from jax.experimental.pallas import tpu as pltpu
from jax.sharding import PartitionSpec as P

TILE = 16
VMEM = pl.BlockSpec(memory_space=pltpu.VMEM)
DIMS_NT = (((1,), (1,)), ((), ()))


def params(**more):
    return pltpu.CompilerParams(vmem_limit_bytes=32 * 1024 * 1024, **more)


def lanes(shape):
    return lax.broadcasted_iota(jnp.int32, shape, 1)


def split(values):
    high = values.astype(jnp.bfloat16)
    low = (values - high.astype(jnp.float32)).astype(jnp.bfloat16)
    return high, low


def gram_of(product):
    size = product.shape[0]
    mixed = product[:, size:]
    return product[:, :size] + (mixed + mixed.T)


def halves(size):
    row = lax.broadcasted_iota(jnp.int32, (size, size), 0)
    col = lax.broadcasted_iota(jnp.int32, (size, size), 1)
    return row, col


def pack_pair(first, second):
    row, col = halves(first.shape[0])
    return jnp.where(row >= col, first, second)


def diagonal(matrix):
    row, col = halves(matrix.shape[0])
    return jnp.sum(jnp.where(row == col, matrix, 0.0), axis=0, keepdims=True)


def faces_kernel(rows, planes, fields, near, far, behind, ahead):
    odd = lax.axis_index("gy") % 2
    size = fields.shape[2]
    near_row = (1 - odd) * (rows - 2)
    far_row = odd * (rows - 2)
    for c in range(3):
        for layer in range(2):
            near[c, layer] = fields[c, pl.ds(2 * rows + near_row + layer, planes, stride=rows), :]
            far[c, layer] = fields[c, pl.ds(2 * rows + far_row + layer, planes, stride=rows), :]
    lane = lanes((TILE, size))

    @pl.loop(0, planes // TILE)
    def _(t):
        tail = jnp.zeros((TILE, size), jnp.float32)
        head = jnp.zeros((TILE, size), jnp.float32)
        for c in range(3):
            for y in range(rows):
                k = c * rows + y
                cells = fields[c, pl.ds((2 + t * TILE) * rows + y, TILE, stride=rows), :]
                turned = pltpu.roll(cells, (2 * k + 2) % size, 1)
                tail = jnp.where((lane == 2 * k) | (lane == 2 * k + 1), turned, tail)
                head = jnp.where((lane == 2 * k + 2) | (lane == 2 * k + 3), turned, head)
        at = pl.ds(pl.multiple_of(t * TILE, TILE), TILE)
        ahead[at, :] = tail
        behind[at, :] = head


def invariants_of(fields, left, right, t, y, rows, row_at):
    size = fields.shape[2]
    lane = lanes((TILE, size))
    first = 2 + t * TILE
    at = pl.ds(t * TILE, TILE)

    def derivative(minus_two, minus_one, plus_one, plus_two):
        return minus_two - 8.0 * minus_one + 8.0 * plus_one - plus_two

    along_x, along_y, along_z = [], [], []
    halo_left = left[at, :]
    halo_right = right[at, :]
    for c in range(3):
        shifted = [fields[c, pl.ds((first + k) * rows + y, TILE, stride=rows), :] for k in (-2, -1, 1, 2)]
        along_x.append(derivative(*shifted))
        along_y.append(derivative(*[row_at(c, y, k, first, at) for k in (-2, -1, 1, 2)]))
        cells = fields[c, pl.ds(first * rows + y, TILE, stride=rows), :]
        k = c * rows + y
        halo = jnp.where((lane == 2 * k) | (lane == 2 * k + 1), halo_left, halo_right)
        halo = pltpu.roll(halo, (2 * size - 2 - 2 * k) % size, 1)
        along_z.append(
            derivative(
                pltpu.roll(jnp.where(lane >= size - 2, halo, cells), 2, 1),
                pltpu.roll(jnp.where(lane >= size - 1, halo, cells), 1, 1),
                pltpu.roll(jnp.where(lane < 1, halo, cells), size - 1, 1),
                pltpu.roll(jnp.where(lane < 2, halo, cells), size - 2, 1),
            )
        )
    gradient = (along_x, along_y, along_z)
    normal = [gradient[a][a] * gradient[a][a] for a in range(3)]
    rotation, shearing = [], []
    for a, b in ((0, 1), (0, 2), (1, 2)):
        turn = gradient[a][b] - gradient[b][a]
        shear = gradient[a][b] + gradient[b][a]
        rotation.append(turn * turn)
        shearing.append(shear * shear)
    enstrophy = (rotation[0] + rotation[1] + rotation[2]) * (1.0 / 288.0)
    strain = (normal[0] + normal[1] + normal[2]) * (1.0 / 144.0)
    strain = strain + (shearing[0] + shearing[1] + shearing[2]) * (1.0 / 288.0)
    return enstrophy, strain


def velocity_kernel(rows, planes, fields, message, pieces, total):
    size = fields.shape[2]
    for c in range(3):

        @pl.loop(0, rows // 2)
        def _(pair):
            for half in range(2):
                plane = fields[c, pl.ds(2 * rows + 2 * pair + half, planes, stride=rows), :]
                high, low = split(plane)
                pieces[0:planes, half * size : (half + 1) * size] = high
                pieces[planes : 2 * planes, half * size : (half + 1) * size] = low
            product = lax.dot_general(pieces[0:planes, :], pieces[...], DIMS_NT, preferred_element_type=jnp.float32)

            @pl.when(pair == 0)
            def _():
                total[c] = product

            @pl.when(pair > 0)
            def _():
                total[c] += product

    grams = [gram_of(total[c]) for c in range(3)]
    message[0:planes, :] = pack_pair(grams[0], grams[1])
    message[planes : 2 * planes, :] = grams[2]
    message[2 * planes : 2 * planes + 8, :] = jnp.broadcast_to(diagonal(grams[1]), (8, planes))


def interior_kernel(rows, planes, fields, left, right, out, total, pieces):
    size = fields.shape[2]

    def row_at(c, y, k, first, at):
        return fields[c, pl.ds(first * rows + y + k, TILE, stride=rows), :]

    @pl.loop(0, rows // 2 - 2)
    def _(pair):
        for half in range(2):
            index = 2 * pair + half
            for t in range(planes // TILE):
                results = invariants_of(fields, left, right, t, index + 2, rows, row_at)
                for f in range(2):
                    out[f, index, t * TILE : (t + 1) * TILE, :] = results[f]
                    high, low = split(results[f])
                    pieces[f, t * TILE : (t + 1) * TILE, half * size : (half + 1) * size] = high
                    pieces[f, planes + t * TILE : planes + (t + 1) * TILE, half * size : (half + 1) * size] = low
        for f in range(2):
            product = lax.dot_general(
                pieces[f, 0:planes, :], pieces[f], DIMS_NT, preferred_element_type=jnp.float32
            )

            @pl.when(pair == 0)
            def _():
                total[f] = product

            @pl.when(pair > 0)
            def _():
                total[f] += product


def border_kernel(rows, planes, fields, near, far, left, right, part, out, message, pieces, total):
    size = fields.shape[2]
    odd = lax.axis_index("gy") % 2 == 1

    def row_at(c, y, k, first, at):
        if 0 <= y + k < rows:
            return fields[c, pl.ds(first * rows + y + k, TILE, stride=rows), :]
        if y + k < 0:
            layer = y + k + 2
            return jnp.where(odd, near[c, layer, at, :], far[c, layer, at, :])
        layer = y + k - rows
        return jnp.where(odd, far[c, layer, at, :], near[c, layer, at, :])

    for index, y in enumerate((0, 1, rows - 2, rows - 1)):
        half = index % 2
        for t in range(planes // TILE):
            results = invariants_of(fields, left, right, t, y, rows, row_at)
            for f in range(2):
                out[f, index, t * TILE : (t + 1) * TILE, :] = results[f]
                high, low = split(results[f])
                pieces[f, t * TILE : (t + 1) * TILE, half * size : (half + 1) * size] = high
                pieces[f, planes + t * TILE : planes + (t + 1) * TILE, half * size : (half + 1) * size] = low
        if half == 1:
            for f in range(2):
                product = lax.dot_general(
                    pieces[f, 0:planes, :], pieces[f], DIMS_NT, preferred_element_type=jnp.float32
                )
                total[f] = (part[f] if index == 1 else total[f]) + product
    grams = [gram_of(total[f]) for f in range(2)]
    message[0:planes, :] = pack_pair(grams[0], grams[1])
    message[planes : planes + 8, :] = jnp.broadcast_to(diagonal(grams[1]), (8, planes))


def assemble_kernel(rows, planes, inner, border, enstrophy, strain):
    for f, out in enumerate((enstrophy, strain)):
        for y in range(rows):
            if 2 <= y < rows - 2:
                plane = inner[f, y - 2]
            else:
                plane = border[f, y if y < 2 else y - rows + 4]
            out[pl.ds(y, planes, stride=rows), :] = plane


def combine_kernel(cells, planes, velocity, derived, cross):
    row, col = halves(planes)
    eye = row == col

    def scale(squares):
        return 1.0 / (5.0 * cells * (squares / (planes * cells) + 1e-06))

    def unpack(packed, second_diagonal):
        first_scale = scale(jnp.sum(jnp.where(eye, packed, 0.0)))
        second_scale = scale(jnp.sum(second_diagonal))
        lower = jnp.where(row > col, packed * first_scale, jnp.where(row < col, packed * second_scale, 0.0))
        both = jnp.where(eye, packed * first_scale + second_diagonal * second_scale, 0.0)
        return lower, both

    low_a, both_a = unpack(velocity[0:planes, :], velocity[2 * planes : 2 * planes + 1, :])
    low_b, both_b = unpack(derived[0:planes, :], derived[planes : planes + 1, :])
    third = velocity[planes : 2 * planes, :]
    third = third * scale(jnp.sum(jnp.where(eye, third, 0.0)))
    triangles = low_a + low_b
    cross[...] = triangles + triangles.T + (both_a + both_b) + third


def butterfly_sum(values, axes):
    for axis in axes:
        count = lax.axis_size(axis)
        if count & (count - 1):
            values = lax.psum(values, axis)
            continue
        step = 1
        while step < count:
            values = values + lax.ppermute(values, axis, [(i, i ^ step) for i in range(count)])
            step *= 2
    return values


def f32(*shape):
    return jax.ShapeDtypeStruct(shape, jnp.float32)


def per_device(fields):
    planes = fields.shape[1] - 4
    rows, cols = fields.shape[2], fields.shape[3]
    count_y, count_z = lax.axis_size("gy"), lax.axis_size("gz")
    flat = fields.reshape(3, fields.shape[1] * rows, cols)

    near, far, behind, ahead = pl.pallas_call(
        functools.partial(faces_kernel, rows, planes),
        out_shape=(f32(3, 2, planes, cols), f32(3, 2, planes, cols), f32(planes, cols), f32(planes, cols)),
        in_specs=[VMEM],
        out_specs=(VMEM, VMEM, VMEM, VMEM),
        compiler_params=params(),
        name="faces",
    )(flat)
    far = lax.ppermute(far, "gy", [(i, (i + 1 if i % 2 else i - 1) % count_y) for i in range(count_y)])
    near = lax.ppermute(near, "gy", [(i, i ^ 1) for i in range(count_y)])
    left = lax.ppermute(ahead, "gz", [(i, (i + 1) % count_z) for i in range(count_z)])
    right = lax.ppermute(behind, "gz", [(i, (i - 1) % count_z) for i in range(count_z)])

    velocity = pl.pallas_call(
        functools.partial(velocity_kernel, rows, planes),
        out_shape=f32(2 * planes + 8, planes),
        in_specs=[VMEM],
        out_specs=VMEM,
        scratch_shapes=[pltpu.VMEM((2 * planes, 2 * cols), jnp.bfloat16), pltpu.VMEM((3, planes, 2 * planes), jnp.float32)],
        compiler_params=params(),
        name="velocity_grams",
    )(flat)
    pieces = pltpu.VMEM((2, 2 * planes, 2 * cols), jnp.bfloat16)
    inner, part = pl.pallas_call(
        functools.partial(interior_kernel, rows, planes),
        out_shape=(f32(2, rows - 4, planes, cols), f32(2, planes, 2 * planes)),
        in_specs=[VMEM] * 3,
        out_specs=(VMEM, VMEM),
        scratch_shapes=[pieces],
        compiler_params=params(),
        name="interior",
    )(flat, left, right)
    border, derived = pl.pallas_call(
        functools.partial(border_kernel, rows, planes),
        out_shape=(f32(2, 4, planes, cols), f32(planes + 8, planes)),
        in_specs=[VMEM] * 6,
        out_specs=(VMEM, VMEM),
        scratch_shapes=[pieces, pltpu.VMEM((2, planes, 2 * planes), jnp.float32)],
        compiler_params=params(),
        name="border",
    )(flat, near, far, left, right, part)
    enstrophy, strain_rate = pl.pallas_call(
        functools.partial(assemble_kernel, rows, planes),
        out_shape=(f32(planes * rows, cols), f32(planes * rows, cols)),
        in_specs=[VMEM] * 2,
        out_specs=(VMEM, VMEM),
        compiler_params=params(),
        name="assemble",
    )(inner, border)

    velocity = butterfly_sum(velocity, ("gy", "gz"))
    derived = butterfly_sum(derived, ("gy", "gz"))
    cells = rows * cols * count_y * count_z
    cross = pl.pallas_call(
        functools.partial(combine_kernel, float(cells), planes),
        out_shape=f32(planes, planes),
        in_specs=[VMEM] * 2,
        out_specs=VMEM,
        compiler_params=params(),
        name="combine",
    )(velocity, derived)
    factor = jnp.linalg.cholesky(cross)
    shape = (planes, rows, cols)
    return (enstrophy.reshape(shape), strain_rate.reshape(shape), factor)


def solution(mesh):
    return jax.shard_map(
        per_device,
        mesh=mesh,
        in_specs=(P(None, None, "gy", "gz"),),
        out_specs=(P(None, "gy", "gz"), P(None, "gy", "gz"), P()),
        check_vma=False,
    )
```

time: 138 us -> 77.8 us (0.56)
  other arithmetic: 51 us -> 13.7 us
  Pallas kernels: 0 us -> 30 us
  local copies, waits for them, and re-layouts: 31.7 us -> 2 us
  waiting for transfers between devices: 37.9 us -> 10.9 us
  starting transfers between devices: 10.7 us -> 20.2 us
  matrix products: 4.88 us -> 0 us
    pallas_call x0 -> x6, Pallas kernels: none -> 30 us  [the longest x1 13.5 us: per_device(): pl.pallas_call(functools.partial(interior_kernel, rows, planes), out_shap...]
    div x2 -> x0, other arithmetic: 27.5 us -> none  [stencil(): return (minus_two - 8.0 * minus_one + 8.0 * plus_one - plus_two) / 12.0]
    ppermute x5 -> x10, waiting for transfers between devices: 37.9 us -> 10.5 us  [butterfly_sum(): lax.ppermute(values, axis, [(i, i ^ step) for i in range(count)])]
    ppermute x5 -> x10, starting transfers between devices: 2.89 us -> 12 us  [butterfly_sum(): lax.ppermute(values, axis, [(i, i ^ step) for i in range(count)])]
    add x2 -> x0, other arithmetic: 7.61 us -> none  [the longest x1 4.16 us: invariants(): strain_rate = strain_rate + 0.5 * shearing * shearing]
    unnamed x27 -> x2, local copies, waits for them, and re-layouts: 9.46 us -> 1.91 us
    sub x3 -> x0, local copies, waits for them, and re-layouts: 6.59 us -> none  [invariants(): gradient[source_axis][target_axis] - gradient[target_axis][source_axis]]
    add x4 -> x0, local copies, waits for them, and re-layouts: 5.58 us -> none  [the longest x3 2.97 us: invariants(): gradient[source_axis][target_axis] + gradient[target_axis][source_axis]]
  transfers between devices with their start and end apart: 9 -> 14, of which waited for: 5 -> 10; matrix products, arithmetic and copies ran while one was open for 26% -> 0% of each run, Pallas kernels for 0% -> 36%
where the time goes in v2:
time: 77.8 us; the launch traced here: 77.6 us
  Pallas kernels  30 us (39%)
  starting transfers between devices  20.2 us (26%)
  other arithmetic  13.7 us (18%)
  waiting for transfers between devices  10.9 us (14%)
  local copies, waits for them, and re-layouts  2 us (3%)
    pallas_call x1, Pallas kernels, per_device(): pl.pallas_call(functools.partial(interior_kernel, rows, planes), out_shap...  13.5 us
    another operation x3, other arithmetic, per_device(): factor = jnp.linalg.cholesky(cross)  12.4 us
    ppermute x10, starting transfers between devices, butterfly_sum(): lax.ppermute(values, axis, [(i, i ^ step) for i in range(count)])  12 us
    ppermute x10, waiting for transfers between devices, butterfly_sum(): lax.ppermute(values, axis, [(i, i ^ step) for i in range(count)])  10.5 us
    pallas_call x1, Pallas kernels, per_device(): pl.pallas_call(functools.partial(velocity_kernel, rows, planes), out_shap...  6.07 us
    pallas_call x1, Pallas kernels, per_device(): pl.pallas_call(functools.partial(border_kernel, rows, planes), out_shape=...  5.92 us
    ppermute x1, starting transfers between devices, per_device(): lax.ppermute(behind, 'gz', [(i, (i - 1) % count_z) for i in range(count_z)])  3.04 us
    ppermute x1, starting transfers between devices, per_device(): lax.ppermute(far, 'gy', [(i, (i + 1 if i % 2 else i - 1) % count_y) for i...  2.64 us
  transfers between devices with their start and end apart: 14, of which 10 were waited for; matrix products, arithmetic and copies ran while one was open for 0% of the time, Pallas kernels for 36%

profile of v2, /device:TPU:0, one launch (start us, length us, event | category | flops | bytes accessed | tf_op | source)
XLA Modules:
  0.0 77.6 jit_solution(4774123411434260243)
XLA Ops:
  0.6 1.9 %copy-done = f32[3,132,16,128]{3,2,1,0:T(8,128)S(1)} copy-done((f32[3,132,16,128]{3,2,1,0:T(8,128)S(1)}, f32[3,132,16,128]{3,2,1,0:T(8,128)}, u32[]{:S(2)}) %copy-start) | copy-done | bytes 3244056
  2.5 1.8 %faces.1 = (f32[3,2,128,128]{3,2,1,0:T(8,128)S(1)}, f32[3,2,128,128]{3,2,1,0:T(8,128)S(1)}, f32[128,128]{1,0:T(8,128)S(1)}, f32[128,128]{1,0:T(8,128)S(1)}) custom-call(f32[3,2112,128]{2,1,0:T(8,128)S(1)} %bitcast.7), custom_call_target="tpu_custom_call" | custom-call | tf_op jit(solution)/shard_map/faces/pallas_call | solution.py:266
  4.8 2.6 %collective-permute-start.3 = (f32[3,2,128,128]{3,2,1,0:T(8,128)S(1)}, f32[3,2,128,128]{3,2,1,0:T(8,128)S(1)}, u32[]{:S(2)}, u32[]{:S(2)}) collective-permute-start(f32[3,2,128,128]{3,2,1,0:T(8,128)S(1)} %get-tuple-element.17), channel_id=1, source_target_pairs={{0,24},{8,16},{16,8},{24,0},{1,25},{9,17},{17,9},{25,1},{2,26},{10... | collective-permute-start | bytes 1179656 | tf_op jit(solution)/shard_map/ppermute | solution.py:274
  7.5 6.1 %velocity_grams.1 = f32[264,128]{1,0:T(8,128)S(1)} custom-call(f32[3,2112,128]{2,1,0:T(8,128)S(1)} %bitcast.8), custom_call_target="tpu_custom_call" | custom-call | tf_op jit(solution)/shard_map/velocity_grams/pallas_call | solution.py:279
  13.7 1.3 %collective-permute-done.4 = f32[264,128]{1,0:T(8,128)S(1)} collective-permute-done((f32[264,128]{1,0:T(8,128)S(1)}, f32[264,128]{1,0:T(8,128)S(1)}, u32[]{:S(2)}, u32[]{:S(2)}) %collective-permute-start.4) | collective-permute-done | bytes 135200 | tf_op jit(solution)/shard_map/ppermute | solution.py:251
  15.1 2.0 %collective-permute-start = (f32[128,128]{1,0:T(8,128)S(1)}, f32[128,128]{1,0:T(8,128)S(1)}, u32[]{:S(2)}, u32[]{:S(2)}) collective-permute-start(f32[128,128]{1,0:T(8,128)S(1)} %get-tuple-element.13), channel_id=1, source_target_pairs={{0,1},{1,2},{2,3},{3,4},{4,5},{5,6},{6,7},{7,0},{8,9},{9,10},{10,1... | collective-permute-start | bytes 196616 | tf_op jit(solution)/shard_map/ppermute | solution.py:276
  17.1 3.0 %collective-permute-start.1 = (f32[128,128]{1,0:T(8,128)S(1)}, f32[128,128]{1,0:T(8,128)S(1)}, u32[]{:S(2)}, u32[]{:S(2)}) collective-permute-start(f32[128,128]{1,0:T(8,128)S(1)} %get-tuple-element.14), channel_id=1, source_target_pairs={{0,7},{1,0},{2,1},{3,2},{4,3},{5,4},{6,5},{7,6},{8,15},{9,8},{10,9... | collective-permute-start | bytes 196616 | tf_op jit(solution)/shard_map/ppermute | solution.py:277
  20.7 1.6 %collective-permute-start.6 = (f32[264,128]{1,0:T(8,128)S(1)}, f32[264,128]{1,0:T(8,128)S(1)}, u32[]{:S(2)}, u32[]{:S(2)}) collective-permute-start(f32[264,128]{1,0:T(8,128)S(1)} %add.40), channel_id=1, source_target_pairs={{0,1},{1,0},{2,3},{3,2},{4,5},{5,4},{6,7},{7,6},{8,9},{9,8},{10,11... | collective-permute-start | bytes 405512 | tf_op jit(solution)/shard_map/ppermute | solution.py:251
  22.7 13.5 %interior.1 = (f32[2,12,128,128]{3,2,1,0:T(8,128)S(1)}, f32[2,128,256]{2,1,0:T(8,128)S(1)}) custom-call(f32[3,2112,128]{2,1,0:T(8,128)S(1)} %bitcast.9, f32[128,128]{1,0:T(8,128)S(1)} %collective-permute-done.left, f32[128,128]{1,0:T(8,128)S(1)} %collective-permute-done.1.right), custom_call_target="tpu_custom_call" | custom-call | tf_op jit(solution)/shard_map/interior/pallas_call | solution.py:289
  36.2 5.9 %border.1 = (f32[2,4,128,128]{3,2,1,0:T(8,128)S(1)}, f32[136,128]{1,0:T(8,128)S(1)}) custom-call(f32[3,2112,128]{2,1,0:T(8,128)S(1)} %bitcast.10, f32[3,2,128,128]{3,2,1,0:T(8,128)S(1)} %collective-permute-done.2.near, f32[3,2,128,128]{3,2,1,0:T(8,128)S(1)} %collective-permute-done.3.far, f32[128,128]{1,0:T(8,128)S(1)} %collective-permute-done.left, ...), custom_call_target="tpu_custom_call" | custom-call | tf_op jit(solution)/shard_map/border/pallas_call | solution.py:298
  42.2 1.2 %collective-permute-done.9 = f32[136,128]{1,0:T(8,128)S(1)} collective-permute-done((f32[136,128]{1,0:T(8,128)S(1)}, f32[136,128]{1,0:T(8,128)S(1)}, u32[]{:S(2)}, u32[]{:S(2)}) %collective-permute-start.9) | collective-permute-done | bytes 69664 | tf_op jit(solution)/shard_map/ppermute | solution.py:251
  43.5 1.7 %collective-permute-start.10 = (f32[136,128]{1,0:T(8,128)S(1)}, f32[136,128]{1,0:T(8,128)S(1)}, u32[]{:S(2)}, u32[]{:S(2)}) collective-permute-start(f32[136,128]{1,0:T(8,128)S(1)} %add.44), channel_id=1, source_target_pairs={{0,16},{8,24},{16,0},{24,8},{1,17},{9,25},{17,1},{25,9},{2,18},{10... | collective-permute-start | bytes 208904 | tf_op jit(solution)/shard_map/ppermute | solution.py:251
  45.2 0.6 collective-permute-start.7
  45.8 2.0 %collective-permute-done.10 = f32[136,128]{1,0:T(8,128)S(1)} collective-permute-done((f32[136,128]{1,0:T(8,128)S(1)}, f32[136,128]{1,0:T(8,128)S(1)}, u32[]{:S(2)}, u32[]{:S(2)}) %collective-permute-start.10) | collective-permute-done | bytes 69664 | tf_op jit(solution)/shard_map/ppermute | solution.py:251
  47.9 1.1 %collective-permute-start.11 = (f32[136,128]{1,0:T(8,128)S(1)}, f32[136,128]{1,0:T(8,128)S(1)}, u32[]{:S(2)}, u32[]{:S(2)}) collective-permute-start(f32[136,128]{1,0:T(8,128)S(1)} %add.45), channel_id=1, source_target_pairs={{0,1},{1,0},{2,3},{3,2},{4,5},{5,4},{6,7},{7,6},{8,9},{9,8},{10,11... | collective-permute-start | bytes 208904 | tf_op jit(solution)/shard_map/ppermute | solution.py:251
  49.0 3.3 %collective-permute-done.11 = f32[136,128]{1,0:T(8,128)S(1)} collective-permute-done((f32[136,128]{1,0:T(8,128)S(1)}, f32[136,128]{1,0:T(8,128)S(1)}, u32[]{:S(2)}, u32[]{:S(2)}) %collective-permute-start.11) | collective-permute-done | bytes 69664 | tf_op jit(solution)/shard_map/ppermute | solution.py:251
  52.3 1.2 %collective-permute-start.12 = (f32[136,128]{1,0:T(8,128)S(1)}, f32[136,128]{1,0:T(8,128)S(1)}, u32[]{:S(2)}, u32[]{:S(2)}) collective-permute-start(f32[136,128]{1,0:T(8,128)S(1)} %add.46), channel_id=1, source_target_pairs={{0,2},{1,3},{2,0},{3,1},{4,6},{5,7},{6,4},{7,5},{8,10},{9,11},{10,... | collective-permute-start | bytes 208904 | tf_op jit(solution)/shard_map/ppermute | solution.py:251
  53.5 2.7 %collective-permute-start.8 = (f32[264,128]{1,0:T(8,128)S(1)}, f32[264,128]{1,0:T(8,128)S(1)}, u32[]{:S(2)}, u32[]{:S(2)}) collective-permute-start(f32[264,128]{1,0:T(8,128)S(1)} %add.42), channel_id=1, source_target_pairs={{0,4},{1,5},{2,6},{3,7},{4,0},{5,1},{6,2},{7,3},{8,12},{9,13},{10,... | collective-permute-start | bytes 405512 | tf_op jit(solution)/shard_map/ppermute | solution.py:251
  56.7 2.9 %collective-permute-start.13 = (f32[136,128]{1,0:T(8,128)S(1)}, f32[136,128]{1,0:T(8,128)S(1)}, u32[]{:S(2)}, u32[]{:S(2)}) collective-permute-start(f32[136,128]{1,0:T(8,128)S(1)} %add.47), channel_id=1, source_target_pairs={{0,4},{1,5},{2,6},{3,7},{4,0},{5,1},{6,2},{7,3},{8,12},{9,13},{10,... | collective-permute-start | bytes 208904 | tf_op jit(solution)/shard_map/ppermute | solution.py:251
  59.5 2.4 %assemble.1 = (f32[2048,128]{1,0:T(8,128)}, f32[2048,128]{1,0:T(8,128)}) custom-call(f32[2,12,128,128]{3,2,1,0:T(8,128)S(1)} %get-tuple-element.15.inner, f32[2,4,128,128]{3,2,1,0:T(8,128)S(1)} %get-tuple-element.19.border), custom_call_target="tpu_custom_call" | custom-call | tf_op jit(solution)/shard_map/assemble/pallas_call | solution.py:307
  62.0 1.5 %collective-permute-done.13 = f32[136,128]{1,0:T(8,128)S(1)} collective-permute-done((f32[136,128]{1,0:T(8,128)S(1)}, f32[136,128]{1,0:T(8,128)S(1)}, u32[]{:S(2)}, u32[]{:S(2)}) %collective-permute-start.13) | collective-permute-done | bytes 69664 | tf_op jit(solution)/shard_map/ppermute | solution.py:251
  64.0 11.7 %cholesky.18 = f32[128,128]{1,0:T(8,128)S(1)} custom-call(f32[128,128]{1,0:T(8,128)S(1)} %fusion), custom_call_target="Cholesky" | custom-call | tf_op jit(solution)/shard_map/jit(cholesky)/cholesky | solution.py:327
  75.8 0.6 compare_reduce_fusion
  76.4 1.2 %select_select_fusion = f32[128,128]{1,0:T(8,128)} fusion(f32[128,128]{1,0:T(8,128)S(1)} %cholesky.18, pred[]{:T(512)} %compare_reduce_fusion), kind=kLoop, calls=%fused_computation.2 | loop fusion | flops 49152 | bytes 131073 | tf_op jit(solution)/shard_map/jit(cholesky)/select_n | solution.py:327
  (28 shorter events, 3.1 us)
Async XLA Ops:
  0.6 1.9 %copy-start = (f32[3,132,16,128]{3,2,1,0:T(8,128)S(1)}, f32[3,132,16,128]{3,2,1,0:T(8,128)}, u32[]{:S(2)}) copy-start(f32[3,132,16,128]{3,2,1,0:T(8,128)} %param.1) | copy-start | bytes 9732100
  4.3 31.9 %collective-permute-start.2 = (f32[3,2,128,128]{3,2,1,0:T(8,128)S(1)}, f32[3,2,128,128]{3,2,1,0:T(8,128)S(1)}, u32[]{:S(2)}, u32[]{:S(2)}) collective-permute-start(f32[3,2,128,128]{3,2,1,0:T(8,128)S(1)} %get-tuple-element.16), channel_id=1, source_target_pairs={{0,8},{8,0},{16,24},{24,16},{1,9},{9,1},{17,25},{25,17},{2,10},{10... | collective-permute-start | bytes 1179656 | tf_op jit(solution)/shard_map/ppermute | solution.py:275
  4.8 31.4 %collective-permute-start.3 = (f32[3,2,128,128]{3,2,1,0:T(8,128)S(1)}, f32[3,2,128,128]{3,2,1,0:T(8,128)S(1)}, u32[]{:S(2)}, u32[]{:S(2)}) collective-permute-start(f32[3,2,128,128]{3,2,1,0:T(8,128)S(1)} %get-tuple-element.17), channel_id=1, source_target_pairs={{0,24},{8,16},{16,8},{24,0},{1,25},{9,17},{17,9},{25,1},{2,26},{10... | collective-permute-start | bytes 1179656 | tf_op jit(solution)/shard_map/ppermute | solution.py:274
  13.6 1.4 %collective-permute-start.4 = (f32[264,128]{1,0:T(8,128)S(1)}, f32[264,128]{1,0:T(8,128)S(1)}, u32[]{:S(2)}, u32[]{:S(2)}) collective-permute-start(f32[264,128]{1,0:T(8,128)S(1)} %velocity_grams.1), channel_id=1, source_target_pairs={{0,8},{8,0},{16,24},{24,16},{1,9},{9,1},{17,25},{25,17},{2,10},{10... | collective-permute-start | bytes 405512 | tf_op jit(solution)/shard_map/ppermute | solution.py:251
  15.0 5.7 %collective-permute-start.5 = (f32[264,128]{1,0:T(8,128)S(1)}, f32[264,128]{1,0:T(8,128)S(1)}, u32[]{:S(2)}, u32[]{:S(2)}) collective-permute-start(f32[264,128]{1,0:T(8,128)S(1)} %add.39), channel_id=1, source_target_pairs={{0,16},{8,24},{16,0},{24,8},{1,17},{9,25},{17,1},{25,9},{2,18},{10... | collective-permute-start | bytes 405512 | tf_op jit(solution)/shard_map/ppermute | solution.py:251
  15.1 7.3 %collective-permute-start = (f32[128,128]{1,0:T(8,128)S(1)}, f32[128,128]{1,0:T(8,128)S(1)}, u32[]{:S(2)}, u32[]{:S(2)}) collective-permute-start(f32[128,128]{1,0:T(8,128)S(1)} %get-tuple-element.13), channel_id=1, source_target_pairs={{0,1},{1,2},{2,3},{3,4},{4,5},{5,6},{6,7},{7,0},{8,9},{9,10},{10,1... | collective-permute-start | bytes 196616 | tf_op jit(solution)/shard_map/ppermute | solution.py:276
  17.1 5.7 %collective-permute-start.1 = (f32[128,128]{1,0:T(8,128)S(1)}, f32[128,128]{1,0:T(8,128)S(1)}, u32[]{:S(2)}, u32[]{:S(2)}) collective-permute-start(f32[128,128]{1,0:T(8,128)S(1)} %get-tuple-element.14), channel_id=1, source_target_pairs={{0,7},{1,0},{2,1},{3,2},{4,3},{5,4},{6,5},{7,6},{8,15},{9,8},{10,9... | collective-permute-start | bytes 196616 | tf_op jit(solution)/shard_map/ppermute | solution.py:277
  20.7 24.4 %collective-permute-start.6 = (f32[264,128]{1,0:T(8,128)S(1)}, f32[264,128]{1,0:T(8,128)S(1)}, u32[]{:S(2)}, u32[]{:S(2)}) collective-permute-start(f32[264,128]{1,0:T(8,128)S(1)} %add.40), channel_id=1, source_target_pairs={{0,1},{1,0},{2,3},{3,2},{4,5},{5,4},{6,7},{7,6},{8,9},{9,8},{10,11... | collective-permute-start | bytes 405512 | tf_op jit(solution)/shard_map/ppermute | solution.py:251
  42.2 1.3 %collective-permute-start.9 = (f32[136,128]{1,0:T(8,128)S(1)}, f32[136,128]{1,0:T(8,128)S(1)}, u32[]{:S(2)}, u32[]{:S(2)}) collective-permute-start(f32[136,128]{1,0:T(8,128)S(1)} %get-tuple-element.22), channel_id=1, source_target_pairs={{0,8},{8,0},{16,24},{24,16},{1,9},{9,1},{17,25},{25,17},{2,10},{10... | collective-permute-start | bytes 208904 | tf_op jit(solution)/shard_map/ppermute | solution.py:251
  43.5 4.4 %collective-permute-start.10 = (f32[136,128]{1,0:T(8,128)S(1)}, f32[136,128]{1,0:T(8,128)S(1)}, u32[]{:S(2)}, u32[]{:S(2)}) collective-permute-start(f32[136,128]{1,0:T(8,128)S(1)} %add.44), channel_id=1, source_target_pairs={{0,16},{8,24},{16,0},{24,8},{1,17},{9,25},{17,1},{25,9},{2,18},{10... | collective-permute-start | bytes 208904 | tf_op jit(solution)/shard_map/ppermute | solution.py:251
  45.2 8.3 %collective-permute-start.7 = (f32[264,128]{1,0:T(8,128)S(1)}, f32[264,128]{1,0:T(8,128)S(1)}, u32[]{:S(2)}, u32[]{:S(2)}) collective-permute-start(f32[264,128]{1,0:T(8,128)S(1)} %add.41), channel_id=1, source_target_pairs={{0,2},{1,3},{2,0},{3,1},{4,6},{5,7},{6,4},{7,5},{8,10},{9,11},{10,... | collective-permute-start | bytes 405512 | tf_op jit(solution)/shard_map/ppermute | solution.py:251
  47.9 4.4 %collective-permute-start.11 = (f32[136,128]{1,0:T(8,128)S(1)}, f32[136,128]{1,0:T(8,128)S(1)}, u32[]{:S(2)}, u32[]{:S(2)}) collective-permute-start(f32[136,128]{1,0:T(8,128)S(1)} %add.45), channel_id=1, source_target_pairs={{0,1},{1,0},{2,3},{3,2},{4,5},{5,4},{6,7},{7,6},{8,9},{9,8},{10,11... | collective-permute-start | bytes 208904 | tf_op jit(solution)/shard_map/ppermute | solution.py:251
  52.3 4.4 %collective-permute-start.12 = (f32[136,128]{1,0:T(8,128)S(1)}, f32[136,128]{1,0:T(8,128)S(1)}, u32[]{:S(2)}, u32[]{:S(2)}) collective-permute-start(f32[136,128]{1,0:T(8,128)S(1)} %add.46), channel_id=1, source_target_pairs={{0,2},{1,3},{2,0},{3,1},{4,6},{5,7},{6,4},{7,5},{8,10},{9,11},{10,... | collective-permute-start | bytes 208904 | tf_op jit(solution)/shard_map/ppermute | solution.py:251
  53.5 8.5 %collective-permute-start.8 = (f32[264,128]{1,0:T(8,128)S(1)}, f32[264,128]{1,0:T(8,128)S(1)}, u32[]{:S(2)}, u32[]{:S(2)}) collective-permute-start(f32[264,128]{1,0:T(8,128)S(1)} %add.42), channel_id=1, source_target_pairs={{0,4},{1,5},{2,6},{3,7},{4,0},{5,1},{6,2},{7,3},{8,12},{9,13},{10,... | collective-permute-start | bytes 405512 | tf_op jit(solution)/shard_map/ppermute | solution.py:251
  56.7 6.8 %collective-permute-start.13 = (f32[136,128]{1,0:T(8,128)S(1)}, f32[136,128]{1,0:T(8,128)S(1)}, u32[]{:S(2)}, u32[]{:S(2)}) collective-permute-start(f32[136,128]{1,0:T(8,128)S(1)} %add.47), channel_id=1, source_target_pairs={{0,4},{1,5},{2,6},{3,7},{4,0},{5,1},{6,2},{7,3},{8,12},{9,13},{10,... | collective-permute-start | bytes 208904 | tf_op jit(solution)/shard_map/ppermute | solution.py:251

commit v3 on v2

v3 whole, which is shorter than its diff:
```python
import functools

import jax
import jax.numpy as jnp
from jax import lax
from jax.experimental import pallas as pl
from jax.experimental.pallas import tpu as pltpu
from jax.sharding import PartitionSpec as P

TILE = 16
BLOCK = 8
CHUNKS = 2
VMEM = pl.BlockSpec(memory_space=pltpu.VMEM)
DIMS_NT = (((1,), (1,)), ((), ()))


def params(mebibytes=20):
    return pltpu.CompilerParams(vmem_limit_bytes=mebibytes * 1024 * 1024)


def lanes(shape):
    return lax.broadcasted_iota(jnp.int32, shape, 1)


def split(values):
    high = values.astype(jnp.bfloat16)
    low = (values - high.astype(jnp.float32)).astype(jnp.bfloat16)
    return high, low


def gram_of(product):
    size = product.shape[0]
    mixed = product[:, size:]
    return product[:, :size] + (mixed + mixed.T)


def halves(size):
    row = lax.broadcasted_iota(jnp.int32, (size, size), 0)
    col = lax.broadcasted_iota(jnp.int32, (size, size), 1)
    return row, col


def pack_pair(first, second):
    row, col = halves(first.shape[0])
    return jnp.where(row >= col, first, second)


def diagonal(matrix):
    row, col = halves(matrix.shape[0])
    return jnp.sum(jnp.where(row == col, matrix, 0.0), axis=0, keepdims=True)


def faces_kernel(rows, planes, fields, turned_fields, near, far, behind, ahead, landed, tails, heads, arrived):
    odd = lax.axis_index("gy") % 2
    size = fields.shape[3]
    depth = planes + 4
    cuts = [depth * i // CHUNKS for i in range(CHUNKS + 1)]
    cuts = [cut - cut % 8 for cut in cuts[:-1]] + [depth]
    copies = []
    for c in range(3):
        for i in range(CHUNKS):
            part = pl.ds(cuts[i], cuts[i + 1] - cuts[i])
            copies.append(pltpu.make_async_copy(fields.at[c, part], landed.at[c, part], arrived.at[c, i]))
            copies[-1].start()
    lane = lanes((8, size))
    near_row = (1 - odd) * (rows - 2)
    far_row = odd * (rows - 2)

    def turn(c, first):
        at = pl.ds(first, 8)
        tail = tails[at, :]
        head = heads[at, :]
        for base in range(0, rows, 8):
            block = jnp.swapaxes(landed[c, at, base : base + 8, :], 0, 1)
            for j in range(8):
                y = base + j
                k = c * rows + y
                turned_fields[c, y, at, :] = block[j]
                moved = pltpu.roll(block[j], (2 * k + 2) % size, 1)
                tail = jnp.where(lane >= 2 * k, moved, tail)
                head = jnp.where(lane >= 2 * k + 2, moved, head)
        tails[at, :] = tail
        heads[at, :] = head

    for c in range(3):
        for i in range(CHUNKS):
            copies[c * CHUNKS + i].wait()

            @pl.loop(cuts[i] // 8, cuts[i + 1] // 8)
            def _(t):
                turn(c, pl.multiple_of(t * 8, 8))

        if depth % 8:
            turn(c, depth - 8)
        for layer in range(2):
            near[c, layer] = turned_fields[c, near_row + layer, 2 : planes + 2, :]
            far[c, layer] = turned_fields[c, far_row + layer, 2 : planes + 2, :]
    ahead[...] = tails[2 : planes + 2, :]
    behind[...] = heads[2 : planes + 2, :]


def derivative(minus_two, minus_one, plus_one, plus_two):
    return minus_two - 8.0 * minus_one + 8.0 * plus_one - plus_two


def velocity_kernel(rows, planes, fields, message, along_z, thirds, band):
    size = fields.shape[3]
    row = lax.broadcasted_iota(jnp.int32, (3 * size, size), 0) % size
    col = lax.broadcasted_iota(jnp.int32, (3 * size, size), 1)
    far_side = jnp.where(row == col - 2, 1.0, jnp.where(row == col + 2, -1.0, 0.0))
    near_side = jnp.where(row == col - 1, -8.0, jnp.where(row == col + 1, 8.0, 0.0))
    band[...] = (far_side + near_side).astype(jnp.bfloat16)
    grams = []
    for c in range(3):
        total = None
        for y in range(rows):
            for t in range(planes // TILE):
                cells = fields[c, y, 2 + t * TILE : 2 + (t + 1) * TILE, :]
                high = cells.astype(jnp.bfloat16)
                rest = cells - high.astype(jnp.float32)
                middle = rest.astype(jnp.bfloat16)
                low = (rest - middle.astype(jnp.float32)).astype(jnp.bfloat16)
                for part, piece in enumerate((high, middle, low)):
                    thirds[y, t * TILE : (t + 1) * TILE, part * size : (part + 1) * size] = piece
            high, middle = thirds[y, :, 0:size], thirds[y, :, size : 2 * size]
            product = lax.dot_general(
                high, jnp.concatenate([high, middle], axis=0), DIMS_NT, preferred_element_type=jnp.float32
            )
            total = product if y == 0 else total + product
        grams.append(gram_of(total))
        derivatives = jnp.dot(
            thirds[...].reshape(rows * planes, 3 * size), band[...], preferred_element_type=jnp.float32
        )
        along_z[c] = derivatives.reshape(rows, planes, size)
    message[0:planes, :] = pack_pair(grams[0], grams[1])
    message[planes : 2 * planes, :] = grams[2]
    message[2 * planes : 2 * planes + 8, :] = jnp.broadcast_to(diagonal(grams[1]), (8, planes))


def edge_terms(left, right):
    size = left.shape[1]
    even = lanes(left.shape) % 2 == 0
    left = pltpu.roll(left, 2, 1)
    right = pltpu.roll(right, size - 2, 1)
    to_last = jnp.where(even, -right, 8.0 * pltpu.roll(right, 1, 1) - right)
    to_first = jnp.where(even, left - 8.0 * pltpu.roll(left, size - 1, 1), left)
    return to_last, to_first


def invariants_of(fields, own_z, to_last, to_first, t, y, rows, row_at):
    size = fields.shape[3]
    lane = lanes((TILE, size))
    edge = (lane < 2) | (lane >= size - 2)
    at = pl.ds(t * TILE, TILE)
    along_x, along_y, along_z = [], [], []
    for c in range(3):
        along_x.append(derivative(*[fields[c, y, pl.ds(2 + t * TILE + k, TILE), :] for k in (-2, -1, 1, 2)]))
        along_y.append(derivative(*[row_at(c, y, k, t) for k in (-2, -1, 1, 2)]))
        k = c * rows + y
        terms = jnp.where(lane < 2 * k + 2, to_last[at, :], to_first[at, :])
        terms = pltpu.roll(terms, (2 * size - 2 - 2 * k) % size, 1)
        along_z.append(own_z[c, y, at, :] + jnp.where(edge, terms, 0.0))
    gradient = (along_x, along_y, along_z)
    normal = [gradient[a][a] * gradient[a][a] for a in range(3)]
    rotation, shearing = [], []
    for a, b in ((0, 1), (0, 2), (1, 2)):
        turn = gradient[a][b] - gradient[b][a]
        shear = gradient[a][b] + gradient[b][a]
        rotation.append(turn * turn)
        shearing.append(shear * shear)
    enstrophy = (rotation[0] + rotation[1] + rotation[2]) * (1.0 / 288.0)
    strain = (normal[0] + normal[1] + normal[2]) * (1.0 / 144.0)
    strain = strain + (shearing[0] + shearing[1] + shearing[2]) * (1.0 / 288.0)
    return enstrophy, strain


def store_results(results, out, index, pieces, half, t, planes, size):
    tile = slice(t * TILE, (t + 1) * TILE)
    lower = slice(planes + t * TILE, planes + (t + 1) * TILE)
    for f in range(2):
        out[f, index, tile, :] = results[f]
        high, low = split(results[f])
        pieces[f, tile, half * size : (half + 1) * size] = high
        pieces[f, lower, half * size : (half + 1) * size] = low


def interior_kernel(rows, planes, fields, own_z, left, right, out, total, pieces, to_last, to_first):
    size = fields.shape[3]
    to_last[...], to_first[...] = edge_terms(left[...], right[...])

    def row_at(c, y, k, t):
        return fields[c, y + k, pl.ds(2 + t * TILE, TILE), :]

    @pl.loop(0, rows // 2 - 2)
    def _(pair):
        for half in range(2):
            index = 2 * pair + half
            for t in range(planes // TILE):
                results = invariants_of(fields, own_z, to_last, to_first, t, index + 2, rows, row_at)
                store_results(results, out, index, pieces, half, t, planes, size)
        for f in range(2):
            product = lax.dot_general(
                pieces[f, 0:planes, :], pieces[f], DIMS_NT, preferred_element_type=jnp.float32
            )

            @pl.when(pair == 0)
            def _():
                total[f] = product

            @pl.when(pair > 0)
            def _():
                total[f] += product


def border_kernel(
    rows, planes, fields, own_z, near, far, left, right, part, out, message, pieces, total, to_last, to_first
):
    size = fields.shape[3]
    odd = lax.axis_index("gy") % 2 == 1
    to_last[...], to_first[...] = edge_terms(left[...], right[...])

    def row_at(c, y, k, t):
        at = pl.ds(t * TILE, TILE)
        if 0 <= y + k < rows:
            return fields[c, y + k, pl.ds(2 + t * TILE, TILE), :]
        if y + k < 0:
            layer = y + k + 2
            return jnp.where(odd, near[c, layer, at, :], far[c, layer, at, :])
        layer = y + k - rows
        return jnp.where(odd, far[c, layer, at, :], near[c, layer, at, :])

    for index, y in enumerate((0, 1, rows - 2, rows - 1)):
        half = index % 2
        for t in range(planes // TILE):
            results = invariants_of(fields, own_z, to_last, to_first, t, y, rows, row_at)
            store_results(results, out, index, pieces, half, t, planes, size)
        if half == 1:
            for f in range(2):
                product = lax.dot_general(
                    pieces[f, 0:planes, :], pieces[f], DIMS_NT, preferred_element_type=jnp.float32
                )
                total[f] = (part[f] if index == 1 else total[f]) + product
    grams = [gram_of(total[f]) for f in range(2)]
    message[0:planes, :] = pack_pair(grams[0], grams[1])
    message[planes : planes + 8, :] = jnp.broadcast_to(diagonal(grams[1]), (8, planes))


def assemble_kernel(rows, planes, inner, border, enstrophy, strain):
    def plane_of(f, y):
        if 2 <= y < rows - 2:
            return inner.at[f, y - 2]
        return border.at[f, y if y < 2 else y - rows + 4]

    for f, out in enumerate((enstrophy, strain)):

        @pl.loop(0, planes // 8)
        def _(t):
            at = pl.ds(pl.multiple_of(t * 8, 8), 8)
            for base in range(0, rows, 8):
                block = jnp.stack([plane_of(f, y)[at, :] for y in range(base, base + 8)], axis=0)
                out[at, base : base + 8, :] = jnp.swapaxes(block, 0, 1)


def thirds_of(values):
    high = values.astype(jnp.bfloat16).astype(jnp.float32)
    rest = values - high
    middle = rest.astype(jnp.bfloat16).astype(jnp.float32)
    return high, middle, rest - middle

def splat_row(block, j):
    return jnp.broadcast_to(block[j : j + 1, :], block.shape)

def eliminate(rows, first):
    count, size = rows.shape
    columns = [jnp.broadcast_to(rows[:, first + j : first + j + 1], rows.shape) for j in range(count)]
    entry = {(i, j): splat_row(columns[j], i) for j in range(count) for i in range(j, count)}
    row = [splat_row(rows, j) for j in range(count)]
    sub = lax.broadcasted_iota(jnp.int32, rows.shape, 0)
    lane = lax.broadcasted_iota(jnp.int32, rows.shape, 1)
    out = jnp.zeros_like(rows)
    for j in range(count):
        root = lax.rsqrt(entry[j, j])
        lower = {i: entry[i, j] * root for i in range(j + 1, count)}
        row[j] = row[j] * root
        for i in range(j + 1, count):
            for m in range(i, count):
                entry[m, i] = entry[m, i] - lower[m] * lower[i]
            row[i] = row[i] - lower[i] * row[j]
        out = jnp.where(sub == j, row[j], out)
    return jnp.where(lane >= first + sub, out, 0.0)


def factor_kernel(cells, planes, velocity, derived, factor, work, upper):
    row, col = halves(planes)
    eye = row == col

    def scale(squares):
        return 1.0 / (5.0 * cells * (squares / (planes * cells) + 1e-06))

    def unpack(packed, second_diagonal):
        first_scale = scale(jnp.sum(jnp.where(eye, packed, 0.0)))
        second_scale = scale(jnp.sum(second_diagonal))
        lower = jnp.where(row > col, packed * first_scale, jnp.where(row < col, packed * second_scale, 0.0))
        both = jnp.where(eye, packed * first_scale + second_diagonal * second_scale, 0.0)
        return lower, both

    low_a, both_a = unpack(velocity[0:planes, :], velocity[2 * planes : 2 * planes + 1, :])
    low_b, both_b = unpack(derived[0:planes, :], derived[planes : planes + 1, :])
    third = velocity[planes : 2 * planes, :]
    third = third * scale(jnp.sum(jnp.where(eye, third, 0.0)))
    triangles = low_a + low_b
    work[...] = triangles + triangles.T + (both_a + both_b) + third
    for first in range(0, planes, BLOCK):
        rows = eliminate(work[first : first + BLOCK, :], first)
        upper[first : first + BLOCK, :] = rows
        if first + BLOCK < planes:
            high, middle, low = thirds_of(rows)
            one = jnp.concatenate([high, high, middle, high, low, middle], axis=0).astype(jnp.bfloat16)
            two = jnp.concatenate([high, middle, high, low, high, middle], axis=0).astype(jnp.bfloat16)
            update = lax.dot_general(one, two, (((0,), (0,)), ((), ())), preferred_element_type=jnp.float32)
            work[first + BLOCK :, :] -= update[first + BLOCK :, :]
    factor[...] = upper[...].T


def butterfly_sum(values, axes):
    for axis in axes:
        count = lax.axis_size(axis)
        if count & (count - 1):
            values = lax.psum(values, axis)
            continue
        step = 1
        while step < count:
            values = values + lax.ppermute(values, axis, [(i, i ^ step) for i in range(count)])
            step *= 2
    return values


def f32(*shape):
    return jax.ShapeDtypeStruct(shape, jnp.float32)


def per_device(fields):
    planes = fields.shape[1] - 4
    rows, cols = fields.shape[2], fields.shape[3]
    count_y, count_z = lax.axis_size("gy"), lax.axis_size("gz")

    turned, near, far, behind, ahead = pl.pallas_call(
        functools.partial(faces_kernel, rows, planes),
        out_shape=(
            pltpu.VMEM((3, rows, planes + 4, cols), jnp.float32),
            f32(3, 2, planes, cols),
            f32(3, 2, planes, cols),
            f32(planes, cols),
            f32(planes, cols),
        ),
        in_specs=[pl.BlockSpec(memory_space=pl.ANY)],
        out_specs=(VMEM, VMEM, VMEM, VMEM, VMEM),
        scratch_shapes=[
            pltpu.VMEM(fields.shape, jnp.float32),
            pltpu.VMEM((planes + 4, cols), jnp.float32),
            pltpu.VMEM((planes + 4, cols), jnp.float32),
            pltpu.SemaphoreType.DMA((3, CHUNKS)),
        ],
        compiler_params=params(),
        name="faces",
    )(pltpu.with_memory_space_constraint(fields, pltpu.HBM))
    far = lax.ppermute(far, "gy", [(i, (i + 1 if i % 2 else i - 1) % count_y) for i in range(count_y)])
    near = lax.ppermute(near, "gy", [(i, i ^ 1) for i in range(count_y)])
    left = lax.ppermute(ahead, "gz", [(i, (i + 1) % count_z) for i in range(count_z)])
    right = lax.ppermute(behind, "gz", [(i, (i - 1) % count_z) for i in range(count_z)])

    velocity, own_z = pl.pallas_call(
        functools.partial(velocity_kernel, rows, planes),
        out_shape=(f32(2 * planes + 8, planes), pltpu.VMEM((3, rows, planes, cols), jnp.float32)),
        in_specs=[VMEM],
        out_specs=(VMEM, VMEM),
        scratch_shapes=[
            pltpu.VMEM((rows, planes, 3 * cols), jnp.bfloat16),
            pltpu.VMEM((3 * cols, cols), jnp.bfloat16),
        ],
        compiler_params=params(),
        name="velocity_grams",
    )(turned)
    pieces = pltpu.VMEM((2, 2 * planes, 2 * cols), jnp.bfloat16)
    edges = [pltpu.VMEM((planes, cols), jnp.float32)] * 2
    inner, part = pl.pallas_call(
        functools.partial(interior_kernel, rows, planes),
        out_shape=(f32(2, rows - 4, planes, cols), f32(2, planes, 2 * planes)),
        in_specs=[VMEM] * 4,
        out_specs=(VMEM, VMEM),
        scratch_shapes=[pieces, *edges],
        compiler_params=params(),
        name="interior",
    )(turned, own_z, left, right)
    border, derived = pl.pallas_call(
        functools.partial(border_kernel, rows, planes),
        out_shape=(f32(2, 4, planes, cols), f32(planes + 8, planes)),
        in_specs=[VMEM] * 7,
        out_specs=(VMEM, VMEM),
        scratch_shapes=[pieces, pltpu.VMEM((2, planes, 2 * planes), jnp.float32), *edges],
        compiler_params=params(),
        name="border",
    )(turned, own_z, near, far, left, right, part)
    enstrophy, strain_rate = pl.pallas_call(
        functools.partial(assemble_kernel, rows, planes),
        out_shape=(f32(planes, rows, cols), f32(planes, rows, cols)),
        in_specs=[VMEM] * 2,
        out_specs=(VMEM, VMEM),
        compiler_params=params(),
        name="assemble",
    )(inner, border)

    velocity = butterfly_sum(velocity, ("gy", "gz"))
    derived = butterfly_sum(derived, ("gy", "gz"))
    cells = rows * cols * count_y * count_z
    factor = pl.pallas_call(
        functools.partial(factor_kernel, float(cells), planes),
        out_shape=f32(planes, planes),
        in_specs=[VMEM] * 2,
        out_specs=VMEM,
        scratch_shapes=[pltpu.VMEM((planes, planes), jnp.float32)] * 2,
        compiler_params=params(),
        name="factor",
    )(velocity, derived)
    return (enstrophy, strain_rate, factor)


def solution(mesh):
    return jax.shard_map(
        per_device,
        mesh=mesh,
        in_specs=(P(None, None, "gy", "gz"),),
        out_specs=(P(None, "gy", "gz"), P(None, "gy", "gz"), P()),
        check_vma=False,
    )
```

time: 77.8 us -> 58.4 us (0.75)
  other arithmetic: 13.7 us -> 0.14 us
  Pallas kernels: 30 us -> 22.6 us
  waiting for transfers between devices: 10.9 us -> 13.7 us
  local copies, waits for them, and re-layouts: 2 us -> 0 us
  starting transfers between devices: 20.2 us -> 21.2 us
    another operation x3 -> x0, other arithmetic: 12.4 us -> none  [per_device(): factor = jnp.linalg.cholesky(cross)]
    pallas_call x1, Pallas kernels: 13.5 us -> 4.34 us  [per_device(): pl.pallas_call(functools.partial(interior_kernel, rows, planes), out_shap...]
    pallas_call x1, Pallas kernels: 0.42 us -> 6.86 us  [per_device(): pl.pallas_call(functools.partial(factor_kernel, float(cells), planes), ou...]
    pallas_call x1, Pallas kernels: 5.92 us -> 1.15 us  [per_device(): pl.pallas_call(functools.partial(border_kernel, rows, planes), out_shape=...]
    pallas_call x1, Pallas kernels: 1.78 us -> 5.77 us  [per_device(): pl.pallas_call(functools.partial(faces_kernel, rows, planes), out_shape=(...]
    pallas_call x1, Pallas kernels: 6.07 us -> 2.55 us  [per_device(): pl.pallas_call(functools.partial(velocity_kernel, rows, planes), out_shap...]
    ppermute x10, waiting for transfers between devices: 10.5 us -> 13.7 us  [butterfly_sum(): lax.ppermute(values, axis, [(i, i ^ step) for i in range(count)])]
    unnamed x2 -> x0, local copies, waits for them, and re-layouts: 1.91 us -> none
  transfers between devices with their start and end apart: 14 -> 14, of which waited for: 10 -> 8; matrix products, arithmetic and copies ran while one was open for 0% -> 0% of each run, Pallas kernels for 36% -> 17%
where the time goes in v3:
time: 58.4 us; the launch traced here: 58.3 us
  Pallas kernels  22.6 us (39%)
  starting transfers between devices  21.2 us (36%)
  waiting for transfers between devices  13.7 us (23%)
  between operations  0.71 us (1%)
    ppermute x10, waiting for transfers between devices, butterfly_sum(): lax.ppermute(values, axis, [(i, i ^ step) for i in range(count)])  13.7 us
    ppermute x10, starting transfers between devices, butterfly_sum(): lax.ppermute(values, axis, [(i, i ^ step) for i in range(count)])  13 us
    pallas_call x1, Pallas kernels, per_device(): pl.pallas_call(functools.partial(factor_kernel, float(cells), planes), ou...  6.86 us
    pallas_call x1, Pallas kernels, per_device(): pl.pallas_call(functools.partial(faces_kernel, rows, planes), out_shape=(...  5.77 us
    pallas_call x1, Pallas kernels, per_device(): pl.pallas_call(functools.partial(interior_kernel, rows, planes), out_shap...  4.34 us
    ppermute x1, starting transfers between devices, per_device(): lax.ppermute(behind, 'gz', [(i, (i - 1) % count_z) for i in range(count_z)])  3.04 us
    ppermute x1, starting transfers between devices, per_device(): lax.ppermute(far, 'gy', [(i, (i + 1 if i % 2 else i - 1) % count_y) for i...  2.65 us
    pallas_call x1, Pallas kernels, per_device(): pl.pallas_call(functools.partial(velocity_kernel, rows, planes), out_shap...  2.55 us
  transfers between devices with their start and end apart: 14, of which 8 were waited for; matrix products, arithmetic and copies ran while one was open for 0% of the time, Pallas kernels for 17%

profile of v3, /device:TPU:0, one launch (start us, length us, event | category | flops | bytes accessed | tf_op | source)
XLA Modules:
  0.0 58.3 jit_solution(7078622200091534353)
XLA Ops:
  0.6 5.8 %faces.1 = (f32[3,16,132,128]{3,2,1,0:T(8,128)S(1)}, f32[3,2,128,128]{3,2,1,0:T(8,128)S(1)}, f32[3,2,128,128]{3,2,1,0:T(8,128)S(1)}, f32[128,128]{1,0:T(8,128)S(1)}, f32[128,128]{1,0:T(8,128)S(1)}) custom-call(f32[3,132,16,128]{3,2,1,0:T(8,128)} %fields.1), custom_call_target="tpu_custom_call" | custom-call | tf_op jit(solution)/shard_map/faces/pallas_call | solution.py:347
  6.4 0.5 collective-permute-start.2
  6.9 2.6 %collective-permute-start.3 = (f32[3,2,128,128]{3,2,1,0:T(8,128)S(1)}, f32[3,2,128,128]{3,2,1,0:T(8,128)S(1)}, u32[]{:S(2)}, u32[]{:S(2)}) collective-permute-start(f32[3,2,128,128]{3,2,1,0:T(8,128)S(1)} %get-tuple-element.22), channel_id=1, source_target_pairs={{0,24},{8,16},{16,8},{24,0},{1,25},{9,17},{17,9},{25,1},{2,26},{10... | collective-permute-start | bytes 1179656 | tf_op jit(solution)/shard_map/ppermute | solution.py:367
  9.6 2.5 %velocity_grams.1 = (f32[264,128]{1,0:T(8,128)S(1)}, f32[3,16,128,128]{3,2,1,0:T(8,128)S(1)}) custom-call(f32[3,16,132,128]{3,2,1,0:T(8,128)S(1)} %get-tuple-element.16.fields), custom_call_target="tpu_custom_call" | custom-call | tf_op jit(solution)/shard_map/velocity_grams/pallas_call | solution.py:372
  12.3 1.3 %collective-permute-done.4 = f32[264,128]{1,0:T(8,128)S(1)} collective-permute-done((f32[264,128]{1,0:T(8,128)S(1)}, f32[264,128]{1,0:T(8,128)S(1)}, u32[]{:S(2)}, u32[]{:S(2)}) %collective-permute-start.4) | collective-permute-done | bytes 135200 | tf_op jit(solution)/shard_map/ppermute | solution.py:333
  13.7 2.0 %collective-permute-start = (f32[128,128]{1,0:T(8,128)S(1)}, f32[128,128]{1,0:T(8,128)S(1)}, u32[]{:S(2)}, u32[]{:S(2)}) collective-permute-start(f32[128,128]{1,0:T(8,128)S(1)} %get-tuple-element.18), channel_id=1, source_target_pairs={{0,1},{1,2},{2,3},{3,4},{4,5},{5,6},{6,7},{7,0},{8,9},{9,10},{10,1... | collective-permute-start | bytes 196616 | tf_op jit(solution)/shard_map/ppermute | solution.py:369
  15.6 3.0 %collective-permute-start.1 = (f32[128,128]{1,0:T(8,128)S(1)}, f32[128,128]{1,0:T(8,128)S(1)}, u32[]{:S(2)}, u32[]{:S(2)}) collective-permute-start(f32[128,128]{1,0:T(8,128)S(1)} %get-tuple-element.19), channel_id=1, source_target_pairs={{0,7},{1,0},{2,1},{3,2},{4,3},{5,4},{6,5},{7,6},{8,15},{9,8},{10,9... | collective-permute-start | bytes 196616 | tf_op jit(solution)/shard_map/ppermute | solution.py:370
  18.7 3.5 %collective-permute-done.5 = f32[264,128]{1,0:T(8,128)S(1)} collective-permute-done((f32[264,128]{1,0:T(8,128)S(1)}, f32[264,128]{1,0:T(8,128)S(1)}, u32[]{:S(2)}, u32[]{:S(2)}) %collective-permute-start.5) | collective-permute-done | bytes 135200 | tf_op jit(solution)/shard_map/ppermute | solution.py:333
  22.1 1.7 %collective-permute-start.6 = (f32[264,128]{1,0:T(8,128)S(1)}, f32[264,128]{1,0:T(8,128)S(1)}, u32[]{:S(2)}, u32[]{:S(2)}) collective-permute-start(f32[264,128]{1,0:T(8,128)S(1)} %add.31), channel_id=1, source_target_pairs={{0,1},{1,0},{2,3},{3,2},{4,5},{5,4},{6,7},{7,6},{8,9},{9,8},{10,11... | collective-permute-start | bytes 405512 | tf_op jit(solution)/shard_map/ppermute | solution.py:333
  23.9 4.3 %interior.1 = (f32[2,12,128,128]{3,2,1,0:T(8,128)S(1)}, f32[2,128,256]{2,1,0:T(8,128)S(1)}) custom-call(f32[3,16,132,128]{3,2,1,0:T(8,128)S(1)} %get-tuple-element.16.fields, f32[3,16,128,128]{3,2,1,0:T(8,128)S(1)} %get-tuple-element.17.own_z, f32[128,128]{1,0:T(8,128)S(1)} %collective-permute-done.left, f32[128,128]{1,0:T(8,128)S(1)} %collective-permute-done.1.right), custom_call_target="tpu_custom_call" | custom-call | tf_op jit(solution)/shard_map/interior/pallas_call | solution.py:386
  28.3 1.2 %border.1 = (f32[2,4,128,128]{3,2,1,0:T(8,128)S(1)}, f32[136,128]{1,0:T(8,128)S(1)}) custom-call(f32[3,16,132,128]{3,2,1,0:T(8,128)S(1)} %get-tuple-element.16.fields, f32[3,16,128,128]{3,2,1,0:T(8,128)S(1)} %get-tuple-element.17.own_z, f32[3,2,128,128]{3,2,1,0:T(8,128)S(1)} %collective-permute-done.2.near, ...), custom_call_target="tpu_custom_call" | custom-call | tf_op jit(solution)/shard_map/border/pallas_call | solution.py:395
  29.5 1.2 %collective-permute-done.9 = f32[136,128]{1,0:T(8,128)S(1)} collective-permute-done((f32[136,128]{1,0:T(8,128)S(1)}, f32[136,128]{1,0:T(8,128)S(1)}, u32[]{:S(2)}, u32[]{:S(2)}) %collective-permute-start.9) | collective-permute-done | bytes 69664 | tf_op jit(solution)/shard_map/ppermute | solution.py:333
  30.8 1.6 %collective-permute-start.10 = (f32[136,128]{1,0:T(8,128)S(1)}, f32[136,128]{1,0:T(8,128)S(1)}, u32[]{:S(2)}, u32[]{:S(2)}) collective-permute-start(f32[136,128]{1,0:T(8,128)S(1)} %add.35), channel_id=1, source_target_pairs={{0,16},{8,24},{16,0},{24,8},{1,17},{9,25},{17,1},{25,9},{2,18},{10... | collective-permute-start | bytes 208904 | tf_op jit(solution)/shard_map/ppermute | solution.py:333
  32.4 1.6 %collective-permute-start.7 = (f32[264,128]{1,0:T(8,128)S(1)}, f32[264,128]{1,0:T(8,128)S(1)}, u32[]{:S(2)}, u32[]{:S(2)}) collective-permute-start(f32[264,128]{1,0:T(8,128)S(1)} %add.32), channel_id=1, source_target_pairs={{0,2},{1,3},{2,0},{3,1},{4,6},{5,7},{6,4},{7,5},{8,10},{9,11},{10,... | collective-permute-start | bytes 405512 | tf_op jit(solution)/shard_map/ppermute | solution.py:333
  34.0 1.1 %collective-permute-done.10 = f32[136,128]{1,0:T(8,128)S(1)} collective-permute-done((f32[136,128]{1,0:T(8,128)S(1)}, f32[136,128]{1,0:T(8,128)S(1)}, u32[]{:S(2)}, u32[]{:S(2)}) %collective-permute-start.10) | collective-permute-done | bytes 69664 | tf_op jit(solution)/shard_map/ppermute | solution.py:333
  35.1 0.4 collective-permute-start.11
  35.6 4.0 %collective-permute-done.11 = f32[136,128]{1,0:T(8,128)S(1)} collective-permute-done((f32[136,128]{1,0:T(8,128)S(1)}, f32[136,128]{1,0:T(8,128)S(1)}, u32[]{:S(2)}, u32[]{:S(2)}) %collective-permute-start.11) | collective-permute-done | bytes 69664 | tf_op jit(solution)/shard_map/ppermute | solution.py:333
  39.5 1.6 %collective-permute-start.12 = (f32[136,128]{1,0:T(8,128)S(1)}, f32[136,128]{1,0:T(8,128)S(1)}, u32[]{:S(2)}, u32[]{:S(2)}) collective-permute-start(f32[136,128]{1,0:T(8,128)S(1)} %add.37), channel_id=1, source_target_pairs={{0,2},{1,3},{2,0},{3,1},{4,6},{5,7},{6,4},{7,5},{8,10},{9,11},{10,... | collective-permute-start | bytes 208904 | tf_op jit(solution)/shard_map/ppermute | solution.py:333
  41.2 2.7 %collective-permute-start.8 = (f32[264,128]{1,0:T(8,128)S(1)}, f32[264,128]{1,0:T(8,128)S(1)}, u32[]{:S(2)}, u32[]{:S(2)}) collective-permute-start(f32[264,128]{1,0:T(8,128)S(1)} %add.33), channel_id=1, source_target_pairs={{0,4},{1,5},{2,6},{3,7},{4,0},{5,1},{6,2},{7,3},{8,12},{9,13},{10,... | collective-permute-start | bytes 405512 | tf_op jit(solution)/shard_map/ppermute | solution.py:333
  44.0 3.0 %collective-permute-start.13 = (f32[136,128]{1,0:T(8,128)S(1)}, f32[136,128]{1,0:T(8,128)S(1)}, u32[]{:S(2)}, u32[]{:S(2)}) collective-permute-start(f32[136,128]{1,0:T(8,128)S(1)} %add.38), channel_id=1, source_target_pairs={{0,4},{1,5},{2,6},{3,7},{4,0},{5,1},{6,2},{7,3},{8,12},{9,13},{10,... | collective-permute-start | bytes 208904 | tf_op jit(solution)/shard_map/ppermute | solution.py:333
  47.0 1.9 %assemble.1 = (f32[128,16,128]{2,1,0:T(8,128)}, f32[128,16,128]{2,1,0:T(8,128)}) custom-call(f32[2,12,128,128]{3,2,1,0:T(8,128)S(1)} %get-tuple-element.20.inner, f32[2,4,128,128]{3,2,1,0:T(8,128)S(1)} %get-tuple-element.24.border), custom_call_target="tpu_custom_call" | custom-call | tf_op jit(solution)/shard_map/assemble/pallas_call | solution.py:404
  48.9 1.0 %collective-permute-done.8 = f32[264,128]{1,0:T(8,128)S(1)} collective-permute-done((f32[264,128]{1,0:T(8,128)S(1)}, f32[264,128]{1,0:T(8,128)S(1)}, u32[]{:S(2)}, u32[]{:S(2)}) %collective-permute-start.8) | collective-permute-done | bytes 135200 | tf_op jit(solution)/shard_map/ppermute | solution.py:333
  49.9 1.5 %collective-permute-done.13 = f32[136,128]{1,0:T(8,128)S(1)} collective-permute-done((f32[136,128]{1,0:T(8,128)S(1)}, f32[136,128]{1,0:T(8,128)S(1)}, u32[]{:S(2)}, u32[]{:S(2)}) %collective-permute-start.13) | collective-permute-done | bytes 69664 | tf_op jit(solution)/shard_map/ppermute | solution.py:333
  51.4 6.9 %factor.1 = f32[128,128]{1,0:T(8,128)} custom-call(f32[264,128]{1,0:T(8,128)S(1)} %add.34.velocity, f32[136,128]{1,0:T(8,128)S(1)} %add.39.derived), custom_call_target="tpu_custom_call" | custom-call | tf_op jit(solution)/shard_map/factor/pallas_call | solution.py:416
  (20 shorter events, 0.6 us)
Async XLA Ops:
  6.4 21.8 %collective-permute-start.2 = (f32[3,2,128,128]{3,2,1,0:T(8,128)S(1)}, f32[3,2,128,128]{3,2,1,0:T(8,128)S(1)}, u32[]{:S(2)}, u32[]{:S(2)}) collective-permute-start(f32[3,2,128,128]{3,2,1,0:T(8,128)S(1)} %get-tuple-element.21), channel_id=1, source_target_pairs={{0,8},{8,0},{16,24},{24,16},{1,9},{9,1},{17,25},{25,17},{2,10},{10... | collective-permute-start | bytes 1179656 | tf_op jit(solution)/shard_map/ppermute | solution.py:368
  6.9 21.3 %collective-permute-start.3 = (f32[3,2,128,128]{3,2,1,0:T(8,128)S(1)}, f32[3,2,128,128]{3,2,1,0:T(8,128)S(1)}, u32[]{:S(2)}, u32[]{:S(2)}) collective-permute-start(f32[3,2,128,128]{3,2,1,0:T(8,128)S(1)} %get-tuple-element.22), channel_id=1, source_target_pairs={{0,24},{8,16},{16,8},{24,0},{1,25},{9,17},{17,9},{25,1},{2,26},{10... | collective-permute-start | bytes 1179656 | tf_op jit(solution)/shard_map/ppermute | solution.py:367
  12.1 1.4 %collective-permute-start.4 = (f32[264,128]{1,0:T(8,128)S(1)}, f32[264,128]{1,0:T(8,128)S(1)}, u32[]{:S(2)}, u32[]{:S(2)}) collective-permute-start(f32[264,128]{1,0:T(8,128)S(1)} %get-tuple-element.27), channel_id=1, source_target_pairs={{0,8},{8,0},{16,24},{24,16},{1,9},{9,1},{17,25},{25,17},{2,10},{10... | collective-permute-start | bytes 405512 | tf_op jit(solution)/shard_map/ppermute | solution.py:333
  13.6 8.6 %collective-permute-start.5 = (f32[264,128]{1,0:T(8,128)S(1)}, f32[264,128]{1,0:T(8,128)S(1)}, u32[]{:S(2)}, u32[]{:S(2)}) collective-permute-start(f32[264,128]{1,0:T(8,128)S(1)} %add.30), channel_id=1, source_target_pairs={{0,16},{8,24},{16,0},{24,8},{1,17},{9,25},{17,1},{25,9},{2,18},{10... | collective-permute-start | bytes 405512 | tf_op jit(solution)/shard_map/ppermute | solution.py:333
  13.7 10.2 %collective-permute-start = (f32[128,128]{1,0:T(8,128)S(1)}, f32[128,128]{1,0:T(8,128)S(1)}, u32[]{:S(2)}, u32[]{:S(2)}) collective-permute-start(f32[128,128]{1,0:T(8,128)S(1)} %get-tuple-element.18), channel_id=1, source_target_pairs={{0,1},{1,2},{2,3},{3,4},{4,5},{5,6},{6,7},{7,0},{8,9},{9,10},{10,1... | collective-permute-start | bytes 196616 | tf_op jit(solution)/shard_map/ppermute | solution.py:369
  15.6 8.3 %collective-permute-start.1 = (f32[128,128]{1,0:T(8,128)S(1)}, f32[128,128]{1,0:T(8,128)S(1)}, u32[]{:S(2)}, u32[]{:S(2)}) collective-permute-start(f32[128,128]{1,0:T(8,128)S(1)} %get-tuple-element.19), channel_id=1, source_target_pairs={{0,7},{1,0},{2,1},{3,2},{4,3},{5,4},{6,5},{7,6},{8,15},{9,8},{10,9... | collective-permute-start | bytes 196616 | tf_op jit(solution)/shard_map/ppermute | solution.py:370
  22.1 10.2 %collective-permute-start.6 = (f32[264,128]{1,0:T(8,128)S(1)}, f32[264,128]{1,0:T(8,128)S(1)}, u32[]{:S(2)}, u32[]{:S(2)}) collective-permute-start(f32[264,128]{1,0:T(8,128)S(1)} %add.31), channel_id=1, source_target_pairs={{0,1},{1,0},{2,3},{3,2},{4,5},{5,4},{6,7},{7,6},{8,9},{9,8},{10,11... | collective-permute-start | bytes 405512 | tf_op jit(solution)/shard_map/ppermute | solution.py:333
  29.4 1.3 %collective-permute-start.9 = (f32[136,128]{1,0:T(8,128)S(1)}, f32[136,128]{1,0:T(8,128)S(1)}, u32[]{:S(2)}, u32[]{:S(2)}) collective-permute-start(f32[136,128]{1,0:T(8,128)S(1)} %get-tuple-element.28), channel_id=1, source_target_pairs={{0,8},{8,0},{16,24},{24,16},{1,9},{9,1},{17,25},{25,17},{2,10},{10... | collective-permute-start | bytes 208904 | tf_op jit(solution)/shard_map/ppermute | solution.py:333
  30.8 4.4 %collective-permute-start.10 = (f32[136,128]{1,0:T(8,128)S(1)}, f32[136,128]{1,0:T(8,128)S(1)}, u32[]{:S(2)}, u32[]{:S(2)}) collective-permute-start(f32[136,128]{1,0:T(8,128)S(1)} %add.35), channel_id=1, source_target_pairs={{0,16},{8,24},{16,0},{24,8},{1,17},{9,25},{17,1},{25,9},{2,18},{10... | collective-permute-start | bytes 208904 | tf_op jit(solution)/shard_map/ppermute | solution.py:333
  32.4 8.8 %collective-permute-start.7 = (f32[264,128]{1,0:T(8,128)S(1)}, f32[264,128]{1,0:T(8,128)S(1)}, u32[]{:S(2)}, u32[]{:S(2)}) collective-permute-start(f32[264,128]{1,0:T(8,128)S(1)} %add.32), channel_id=1, source_target_pairs={{0,2},{1,3},{2,0},{3,1},{4,6},{5,7},{6,4},{7,5},{8,10},{9,11},{10,... | collective-permute-start | bytes 405512 | tf_op jit(solution)/shard_map/ppermute | solution.py:333
  35.1 4.4 %collective-permute-start.11 = (f32[136,128]{1,0:T(8,128)S(1)}, f32[136,128]{1,0:T(8,128)S(1)}, u32[]{:S(2)}, u32[]{:S(2)}) collective-permute-start(f32[136,128]{1,0:T(8,128)S(1)} %add.36), channel_id=1, source_target_pairs={{0,1},{1,0},{2,3},{3,2},{4,5},{5,4},{6,7},{7,6},{8,9},{9,8},{10,11... | collective-permute-start | bytes 208904 | tf_op jit(solution)/shard_map/ppermute | solution.py:333
  39.5 4.4 %collective-permute-start.12 = (f32[136,128]{1,0:T(8,128)S(1)}, f32[136,128]{1,0:T(8,128)S(1)}, u32[]{:S(2)}, u32[]{:S(2)}) collective-permute-start(f32[136,128]{1,0:T(8,128)S(1)} %add.37), channel_id=1, source_target_pairs={{0,2},{1,3},{2,0},{3,1},{4,6},{5,7},{6,4},{7,5},{8,10},{9,11},{10,... | collective-permute-start | bytes 208904 | tf_op jit(solution)/shard_map/ppermute | solution.py:333
  41.2 8.7 %collective-permute-start.8 = (f32[264,128]{1,0:T(8,128)S(1)}, f32[264,128]{1,0:T(8,128)S(1)}, u32[]{:S(2)}, u32[]{:S(2)}) collective-permute-start(f32[264,128]{1,0:T(8,128)S(1)} %add.33), channel_id=1, source_target_pairs={{0,4},{1,5},{2,6},{3,7},{4,0},{5,1},{6,2},{7,3},{8,12},{9,13},{10,... | collective-permute-start | bytes 405512 | tf_op jit(solution)/shard_map/ppermute | solution.py:333
  44.0 7.4 %collective-permute-start.13 = (f32[136,128]{1,0:T(8,128)S(1)}, f32[136,128]{1,0:T(8,128)S(1)}, u32[]{:S(2)}, u32[]{:S(2)}) collective-permute-start(f32[136,128]{1,0:T(8,128)S(1)} %add.38), channel_id=1, source_target_pairs={{0,4},{1,5},{2,6},{3,7},{4,0},{5,1},{6,2},{7,3},{8,12},{9,13},{10,... | collective-permute-start | bytes 208904 | tf_op jit(solution)/shard_map/ppermute | solution.py:333

commit v4 on v3

--- a/solution.py
+++ b/solution.py
@@ -43,6 +43,11 @@
 def pack_pair(first, second):
     row, col = halves(first.shape[0])
     return jnp.where(row >= col, first, second)
+
+
+def half_starts(length):
+    core = lax.axis_index("gy") % 2
+    return pl.multiple_of(core * length, 8), pl.multiple_of((1 - core) * length, 8)
 
 
 def diagonal(matrix):
@@ -86,7 +91,7 @@
         for i in range(CHUNKS):
             copies[c * CHUNKS + i].wait()
 
-            @pl.loop(cuts[i] // 8, cuts[i + 1] // 8)
+            @pl.loop(cuts[i] // 8, cuts[i + 1] // 8, unroll=8)
             def _(t):
                 turn(c, pl.multiple_of(t * 8, 8))
 
@@ -103,14 +108,13 @@
     return minus_two - 8.0 * minus_one + 8.0 * plus_one - plus_two
 
 
-def velocity_kernel(rows, planes, fields, message, along_z, thirds, band):
+def velocity_kernel(rows, planes, fields, grams, along_z, thirds, band):
     size = fields.shape[3]
     row = lax.broadcasted_iota(jnp.int32, (3 * size, size), 0) % size
     col = lax.broadcasted_iota(jnp.int32, (3 * size, size), 1)
     far_side = jnp.where(row == col - 2, 1.0, jnp.where(row == col + 2, -1.0, 0.0))
     near_side = jnp.where(row == col - 1, -8.0, jnp.where(row == col + 1, 8.0, 0.0))
     band[...] = (far_side + near_side).astype(jnp.bfloat16)
-    grams = []
     for c in range(3):
         total = None
         for y in range(rows):
@@ -127,14 +131,11 @@
                 high, jnp.concatenate([high, middle], axis=0), DIMS_NT, preferred_element_type=jnp.float32
             )
             total = product if y == 0 else total + product
-        grams.append(gram_of(total))
+        grams[c] = gram_of(total)
         derivatives = jnp.dot(
             thirds[...].reshape(rows * planes, 3 * size), band[...], preferred_element_type=jnp.float32
         )
         along_z[c] = derivatives.reshape(rows, planes, size)
-    message[0:planes, :] = pack_pair(grams[0], grams[1])
-    message[planes : 2 * planes, :] = grams[2]
-    message[2 * planes : 2 * planes + 8, :] = jnp.broadcast_to(diagonal(grams[1]), (8, planes))
 
 
 def edge_terms(left, right):
@@ -213,7 +214,7 @@
 
 
 def border_kernel(
-    rows, planes, fields, own_z, near, far, left, right, part, out, message, pieces, total, to_last, to_first
+    rows, planes, fields, own_z, near, far, left, right, part, velocity, out, keep, give, message, pieces, total, to_last, to_first
 ):
     size = fields.shape[3]
     odd = lax.axis_index("gy") % 2 == 1
@@ -240,9 +241,15 @@
                     pieces[f, 0:planes, :], pieces[f], DIMS_NT, preferred_element_type=jnp.float32
                 )
                 total[f] = (part[f] if index == 1 else total[f]) + product
-    grams = [gram_of(total[f]) for f in range(2)]
+    grams = [gram_of(total[f]) for f in range(2)] + [velocity[c] for c in range(3)]
     message[0:planes, :] = pack_pair(grams[0], grams[1])
-    message[planes : planes + 8, :] = jnp.broadcast_to(diagonal(grams[1]), (8, planes))
+    message[planes : 2 * planes, :] = pack_pair(grams[2], grams[3])
+    message[2 * planes : 3 * planes, :] = grams[4]
+    message[3 * planes : 3 * planes + 8, :] = jnp.broadcast_to(diagonal(grams[1]), (8, planes))
+    message[3 * planes + 8 : 3 * planes + 16, :] = jnp.broadcast_to(diagonal(grams[3]), (8, planes))
+    mine, other = half_starts(keep.shape[0])
+    keep[...] = message[pl.ds(mine, keep.shape[0]), :]
+    give[...] = message[pl.ds(other, keep.shape[0]), :]
 
 
 def assemble_kernel(rows, planes, inner, border, enstrophy, strain):
@@ -290,7 +297,10 @@
     return jnp.where(lane >= first + sub, out, 0.0)
 
 
-def factor_kernel(cells, planes, velocity, derived, factor, work, upper):
+def factor_kernel(cells, planes, kept, given, factor, message, work, upper):
+    mine, other = half_starts(kept.shape[0])
+    message[pl.ds(mine, kept.shape[0]), :] = kept[...]
+    message[pl.ds(other, kept.shape[0]), :] = given[...]
     row, col = halves(planes)
     eye = row == col
 
@@ -304,9 +314,9 @@
         both = jnp.where(eye, packed * first_scale + second_diagonal * second_scale, 0.0)
         return lower, both
 
-    low_a, both_a = unpack(velocity[0:planes, :], velocity[2 * planes : 2 * planes + 1, :])
-    low_b, both_b = unpack(derived[0:planes, :], derived[planes : planes + 1, :])
-    third = velocity[planes : 2 * planes, :]
+    low_a, both_a = unpack(message[0:planes, :], message[3 * planes : 3 * planes + 1, :])
+    low_b, both_b = unpack(message[planes : 2 * planes, :], message[3 * planes + 8 : 3 * planes + 9, :])
+    third = message[2 * planes : 3 * planes, :]
     third = third * scale(jnp.sum(jnp.where(eye, third, 0.0)))
     triangles = low_a + low_b
     work[...] = triangles + triangles.T + (both_a + both_b) + third
@@ -322,17 +332,31 @@
     factor[...] = upper[...].T
 
 
-def butterfly_sum(values, axes):
-    for axis in axes:
-        count = lax.axis_size(axis)
-        if count & (count - 1):
-            values = lax.psum(values, axis)
-            continue
-        step = 1
-        while step < count:
-            values = values + lax.ppermute(values, axis, [(i, i ^ step) for i in range(count)])
-            step *= 2
-    return values
+def cost(microseconds):
+    return pl.CostEstimate(flops=0, bytes_accessed=int(microseconds * 3.69e6), transcendentals=0)
+
+
+AXES = ("gy", "gz")
+
+
+def exchange(values, even, odd):
+    count_z = lax.axis_size("gz")
+    count = lax.axis_size("gy") * count_z
+    return lax.ppermute(values, AXES, [(i, i ^ (odd if i // count_z % 2 else even)) for i in range(count)])
+
+
+def rounds():
+    count_y, count_z = lax.axis_size("gy"), lax.axis_size("gz")
+    assert count_y & (count_y - 1) == 0 and count_z & (count_z - 1) == 0
+    bits = [count_z << i for i in range(1, count_y.bit_length() - 1)] + [1 << i for i in range(count_z.bit_length() - 1)]
+    groups = [bits[i : i + 2] for i in range(0, len(bits), 2)]
+    return [[group[0]] if len(group) == 1 else [group[0], group[1], group[0] ^ group[1]] for group in groups]
+
+
+def add_terms(terms):
+    while len(terms) > 1:
+        terms = [terms[i] + terms[i + 1] for i in range(0, len(terms), 2)]
+    return terms[0]
 
 
 def f32(*shape):
@@ -362,6 +386,7 @@
             pltpu.SemaphoreType.DMA((3, CHUNKS)),
         ],
         compiler_params=params(),
+        cost_estimate=cost(5),
         name="faces",
     )(pltpu.with_memory_space_constraint(fields, pltpu.HBM))
     far = lax.ppermute(far, "gy", [(i, (i + 1 if i % 2 else i - 1) % count_y) for i in range(count_y)])
@@ -371,7 +396,7 @@
 
     velocity, own_z = pl.pallas_call(
         functools.partial(velocity_kernel, rows, planes),
-        out_shape=(f32(2 * planes + 8, planes), pltpu.VMEM((3, rows, planes, cols), jnp.float32)),
+        out_shape=(f32(3, planes, planes), pltpu.VMEM((3, rows, planes, cols), jnp.float32)),
         in_specs=[VMEM],
         out_specs=(VMEM, VMEM),
         scratch_shapes=[
@@ -379,6 +404,7 @@
             pltpu.VMEM((3 * cols, cols), jnp.bfloat16),
         ],
         compiler_params=params(),
+        cost_estimate=cost(2.5),
         name="velocity_grams",
     )(turned)
     pieces = pltpu.VMEM((2, 2 * planes, 2 * cols), jnp.bfloat16)
@@ -390,38 +416,48 @@
         out_specs=(VMEM, VMEM),
         scratch_shapes=[pieces, *edges],
         compiler_params=params(),
+        cost_estimate=cost(4),
         name="interior",
     )(turned, own_z, left, right)
-    border, derived = pl.pallas_call(
+    half = 3 * planes // 2 + 8
+    message = pltpu.VMEM((2 * half, planes), jnp.float32)
+    border, keep, give = pl.pallas_call(
         functools.partial(border_kernel, rows, planes),
-        out_shape=(f32(2, 4, planes, cols), f32(planes + 8, planes)),
-        in_specs=[VMEM] * 7,
-        out_specs=(VMEM, VMEM),
-        scratch_shapes=[pieces, pltpu.VMEM((2, planes, 2 * planes), jnp.float32), *edges],
-        compiler_params=params(),
+        out_shape=(f32(2, 4, planes, cols), f32(half, planes), f32(half, planes)),
+        in_specs=[VMEM] * 8,
+        out_specs=(VMEM, VMEM, VMEM),
+        scratch_shapes=[message, pieces, pltpu.VMEM((2, planes, 2 * planes), jnp.float32), *edges],
+        compiler_params=params(),
+        cost_estimate=cost(1),
         name="border",
-    )(turned, own_z, near, far, left, right, part)
+    )(turned, own_z, near, far, left, right, part, velocity)
     enstrophy, strain_rate = pl.pallas_call(
         functools.partial(assemble_kernel, rows, planes),
         out_shape=(f32(planes, rows, cols), f32(planes, rows, cols)),
         in_specs=[VMEM] * 2,
         out_specs=(VMEM, VMEM),
         compiler_params=params(),
+        cost_estimate=cost(2),
         name="assemble",
     )(inner, border)
 
-    velocity = butterfly_sum(velocity, ("gy", "gz"))
-    derived = butterfly_sum(derived, ("gy", "gz"))
+    core = count_z
+    kept = keep + exchange(give, core, core)
+    masks = rounds()
+    for even, odd in zip(masks, masks[::-1]):
+        kept = add_terms([kept] + [exchange(kept, *pair) for pair in zip(even, odd)])
+    given = exchange(kept, core, core)
     cells = rows * cols * count_y * count_z
     factor = pl.pallas_call(
         functools.partial(factor_kernel, float(cells), planes),
         out_shape=f32(planes, planes),
         in_specs=[VMEM] * 2,
         out_specs=VMEM,
-        scratch_shapes=[pltpu.VMEM((planes, planes), jnp.float32)] * 2,
-        compiler_params=params(),
+        scratch_shapes=[message] + [pltpu.VMEM((planes, planes), jnp.float32)] * 2,
+        compiler_params=params(),
+        cost_estimate=cost(6),
         name="factor",
-    )(velocity, derived)
+    )(kept, given)
     return (enstrophy, strain_rate, factor)
 
 

time: 58.4 us -> 46.5 us (0.80)
  starting transfers between devices: 21.2 us -> 15.4 us
  waiting for transfers between devices: 13.7 us -> 10.5 us
  Pallas kernels: 22.6 us -> 19.6 us
    ppermute x10 -> x8, starting transfers between devices: 13 us -> 7.47 us  [exchange(): lax.ppermute(values, AXES, [(i, i ^ (odd if i // count_z % 2 else even))...]
    pallas_call x1, Pallas kernels: 5.77 us -> 2.49 us  [per_device(): pl.pallas_call(functools.partial(faces_kernel, rows, planes), out_shape=(...]
    ppermute x10 -> x8, waiting for transfers between devices: 13.7 us -> 10.5 us  [exchange(): lax.ppermute(values, AXES, [(i, i ^ (odd if i // count_z % 2 else even))...]
  transfers between devices with their start and end apart: 14 -> 12, of which waited for: 8 -> 7; matrix products, arithmetic and copies ran while one was open for 0% -> 0% of each run, Pallas kernels for 17% -> 19%
where the time goes in v4:
time: 46.5 us; the launch traced here: 46.3 us
  Pallas kernels  19.6 us (42%)
  starting transfers between devices  15.4 us (33%)
  waiting for transfers between devices  10.5 us (23%)
  between operations  0.71 us (2%)
    ppermute x8, waiting for transfers between devices, exchange(): lax.ppermute(values, AXES, [(i, i ^ (odd if i // count_z % 2 else even))...  10.5 us
    ppermute x8, starting transfers between devices, exchange(): lax.ppermute(values, AXES, [(i, i ^ (odd if i // count_z % 2 else even))...  7.47 us
    pallas_call x1, Pallas kernels, per_device(): pl.pallas_call(functools.partial(factor_kernel, float(cells), planes), ou...  6.88 us
    pallas_call x1, Pallas kernels, per_device(): pl.pallas_call(functools.partial(interior_kernel, rows, planes), out_shap...  4.34 us
    ppermute x1, starting transfers between devices, per_device(): lax.ppermute(behind, 'gz', [(i, (i - 1) % count_z) for i in range(count_z)])  3.23 us
    ppermute x1, starting transfers between devices, per_device(): lax.ppermute(far, 'gy', [(i, (i + 1 if i % 2 else i - 1) % count_y) for i...  2.65 us
    pallas_call x1, Pallas kernels, per_device(): pl.pallas_call(functools.partial(velocity_kernel, rows, planes), out_shap...  2.65 us
    pallas_call x1, Pallas kernels, per_device(): pl.pallas_call(functools.partial(faces_kernel, rows, planes), out_shape=(...  2.49 us
  transfers between devices with their start and end apart: 12, of which 7 were waited for; matrix products, arithmetic and copies ran while one was open for 0% of the time, Pallas kernels for 19%

profile of v4, /device:TPU:0, one launch (start us, length us, event | category | flops | bytes accessed | tf_op | source)
XLA Modules:
  0.0 46.3 jit_solution(11885294504304593486)
XLA Ops:
  0.6 2.5 %faces.1 = (f32[3,16,132,128]{3,2,1,0:T(8,128)S(1)}, f32[3,2,128,128]{3,2,1,0:T(8,128)S(1)}, f32[3,2,128,128]{3,2,1,0:T(8,128)S(1)}, f32[128,128]{1,0:T(8,128)S(1)}, f32[128,128]{1,0:T(8,128)S(1)}) custom-call(f32[3,132,16,128]{3,2,1,0:T(8,128)} %fields.1), custom_call_target="tpu_custom_call" | custom-call | bytes 18450000 | tf_op jit(solution)/shard_map/faces/pallas_call | solution.py:371
  3.1 0.5 %collective-permute-start.2 = (f32[3,2,128,128]{3,2,1,0:T(8,128)S(1)}, f32[3,2,128,128]{3,2,1,0:T(8,128)S(1)}, u32[]{:S(2)}, u32[]{:S(2)}) collective-permute-start(f32[3,2,128,128]{3,2,1,0:T(8,128)S(1)} %get-tuple-element.22), channel_id=1, source_target_pairs={{0,8},{8,0},{16,24},{24,16},{1,9},{9,1},{17,25},{25,17},{2,10},{10... | collective-permute-start | bytes 1179656 | tf_op jit(solution)/shard_map/ppermute | solution.py:393
  3.6 2.6 %collective-permute-start.3 = (f32[3,2,128,128]{3,2,1,0:T(8,128)S(1)}, f32[3,2,128,128]{3,2,1,0:T(8,128)S(1)}, u32[]{:S(2)}, u32[]{:S(2)}) collective-permute-start(f32[3,2,128,128]{3,2,1,0:T(8,128)S(1)} %get-tuple-element.23), channel_id=1, source_target_pairs={{0,24},{8,16},{16,8},{24,0},{1,25},{9,17},{17,9},{25,1},{2,26},{10... | collective-permute-start | bytes 1179656 | tf_op jit(solution)/shard_map/ppermute | solution.py:392
  6.3 1.5 %collective-permute-start = (f32[128,128]{1,0:T(8,128)S(1)}, f32[128,128]{1,0:T(8,128)S(1)}, u32[]{:S(2)}, u32[]{:S(2)}) collective-permute-start(f32[128,128]{1,0:T(8,128)S(1)} %get-tuple-element.19), channel_id=1, source_target_pairs={{0,1},{1,2},{2,3},{3,4},{4,5},{5,6},{6,7},{7,0},{8,9},{9,10},{10,1... | collective-permute-start | bytes 196616 | tf_op jit(solution)/shard_map/ppermute | solution.py:394
  7.8 3.2 %collective-permute-start.1 = (f32[128,128]{1,0:T(8,128)S(1)}, f32[128,128]{1,0:T(8,128)S(1)}, u32[]{:S(2)}, u32[]{:S(2)}) collective-permute-start(f32[128,128]{1,0:T(8,128)S(1)} %get-tuple-element.20), channel_id=1, source_target_pairs={{0,7},{1,0},{2,1},{3,2},{4,3},{5,4},{6,5},{7,6},{8,15},{9,8},{10,9... | collective-permute-start | bytes 196616 | tf_op jit(solution)/shard_map/ppermute | solution.py:395
  11.0 2.6 %velocity_grams.1 = (f32[3,128,128]{2,1,0:T(8,128)S(1)}, f32[3,16,128,128]{3,2,1,0:T(8,128)S(1)}) custom-call(f32[3,16,132,128]{3,2,1,0:T(8,128)S(1)} %get-tuple-element.17.fields), custom_call_target="tpu_custom_call" | custom-call | bytes 9225000 | tf_op jit(solution)/shard_map/velocity_grams/pallas_call | solution.py:397
  13.7 4.3 %interior.1 = (f32[2,12,128,128]{3,2,1,0:T(8,128)S(1)}, f32[2,128,256]{2,1,0:T(8,128)S(1)}) custom-call(f32[3,16,132,128]{3,2,1,0:T(8,128)S(1)} %get-tuple-element.17.fields, f32[3,16,128,128]{3,2,1,0:T(8,128)S(1)} %get-tuple-element.18.own_z, f32[128,128]{1,0:T(8,128)S(1)} %collective-permute-done.left, f32[128,128]{1,0:T(8,128)S(1)} %collective-permute-done.1.right), custom_call_target="tpu_custom_call" | custom-call | bytes 14760000 | tf_op jit(solution)/shard_map/interior/pallas_call | solution.py:412
  18.1 1.3 %border.1 = (f32[2,4,128,128]{3,2,1,0:T(8,128)S(1)}, f32[200,128]{1,0:T(8,128)S(1)}, f32[200,128]{1,0:T(8,128)S(1)}) custom-call(f32[3,16,132,128]{3,2,1,0:T(8,128)S(1)} %get-tuple-element.17.fields, f32[3,16,128,128]{3,2,1,0:T(8,128)S(1)} %get-tuple-element.18.own_z, f32[3,2,128,128]{3,2,1,0:T(8,128)S(1)} %collective-permute-done.2.near, ...), custom_call_target="tpu_custom_call" | custom-call | bytes 3690000 | tf_op jit(solution)/shard_map/border/pallas_call | solution.py:424
  19.4 1.3 %collective-permute-done.4 = f32[200,128]{1,0:T(8,128)S(1)} collective-permute-done((f32[200,128]{1,0:T(8,128)S(1)}, f32[200,128]{1,0:T(8,128)S(1)}, u32[]{:S(2)}, u32[]{:S(2)}) %collective-permute-start.4) | collective-permute-done | bytes 102432 | tf_op jit(solution)/shard_map/ppermute | solution.py:345
  20.8 0.9 %collective-permute-start.6 = (f32[200,128]{1,0:T(8,128)S(1)}, f32[200,128]{1,0:T(8,128)S(1)}, u32[]{:S(2)}, u32[]{:S(2)}) collective-permute-start(f32[200,128]{1,0:T(8,128)S(1)} %add.21), channel_id=1, source_target_pairs={{0,1},{1,0},{2,3},{3,2},{4,5},{5,4},{6,7},{7,6},{8,12},{9,13},{10,... | collective-permute-start | bytes 307208 | tf_op jit(solution)/shard_map/ppermute | solution.py:345
  21.6 1.0 %collective-permute-start.7 = (f32[200,128]{1,0:T(8,128)S(1)}, f32[200,128]{1,0:T(8,128)S(1)}, u32[]{:S(2)}, u32[]{:S(2)}) collective-permute-start(f32[200,128]{1,0:T(8,128)S(1)} %add.21), channel_id=1, source_target_pairs={{0,17},{1,16},{2,19},{3,18},{4,21},{5,20},{6,23},{7,22},{8,14},{9,... | collective-permute-start | bytes 307208 | tf_op jit(solution)/shard_map/ppermute | solution.py:345
  22.6 1.7 %collective-permute-start.5 = (f32[200,128]{1,0:T(8,128)S(1)}, f32[200,128]{1,0:T(8,128)S(1)}, u32[]{:S(2)}, u32[]{:S(2)}) collective-permute-start(f32[200,128]{1,0:T(8,128)S(1)} %add.21), channel_id=1, source_target_pairs={{0,16},{1,17},{2,18},{3,19},{4,20},{5,21},{6,22},{7,23},{8,10},{9,... | collective-permute-start | bytes 307208 | tf_op jit(solution)/shard_map/ppermute | solution.py:345
  24.3 1.2 %collective-permute-done.6 = f32[200,128]{1,0:T(8,128)S(1)} collective-permute-done((f32[200,128]{1,0:T(8,128)S(1)}, f32[200,128]{1,0:T(8,128)S(1)}, u32[]{:S(2)}, u32[]{:S(2)}) %collective-permute-start.6) | collective-permute-done | bytes 102432 | tf_op jit(solution)/shard_map/ppermute | solution.py:345
  25.5 1.8 %collective-permute-done.7 = f32[200,128]{1,0:T(8,128)S(1)} collective-permute-done((f32[200,128]{1,0:T(8,128)S(1)}, f32[200,128]{1,0:T(8,128)S(1)}, u32[]{:S(2)}, u32[]{:S(2)}) %collective-permute-start.7) | collective-permute-done | bytes 102432 | tf_op jit(solution)/shard_map/ppermute | solution.py:345
  27.3 1.0 %collective-permute-done.5 = f32[200,128]{1,0:T(8,128)S(1)} collective-permute-done((f32[200,128]{1,0:T(8,128)S(1)}, f32[200,128]{1,0:T(8,128)S(1)}, u32[]{:S(2)}, u32[]{:S(2)}) %collective-permute-start.5) | collective-permute-done | bytes 102432 | tf_op jit(solution)/shard_map/ppermute | solution.py:345
  28.3 1.9 %collective-permute-start.9 = (f32[200,128]{1,0:T(8,128)S(1)}, f32[200,128]{1,0:T(8,128)S(1)}, u32[]{:S(2)}, u32[]{:S(2)}) collective-permute-start(f32[200,128]{1,0:T(8,128)S(1)} %add_add_fusion.1), channel_id=1, source_target_pairs={{0,4},{1,5},{2,6},{3,7},{4,0},{5,1},{6,2},{7,3},{8,9},{9,8},{10,11... | collective-permute-start | bytes 307208 | tf_op jit(solution)/shard_map/ppermute | solution.py:345
  30.2 1.4 %collective-permute-start.10 = (f32[200,128]{1,0:T(8,128)S(1)}, f32[200,128]{1,0:T(8,128)S(1)}, u32[]{:S(2)}, u32[]{:S(2)}) collective-permute-start(f32[200,128]{1,0:T(8,128)S(1)} %add_add_fusion.1), channel_id=1, source_target_pairs={{0,6},{1,7},{2,4},{3,5},{4,2},{5,3},{6,0},{7,1},{8,25},{9,24},{10,... | collective-permute-start | bytes 307208 | tf_op jit(solution)/shard_map/ppermute | solution.py:345
  31.6 0.5 %collective-permute-start.8 = (f32[200,128]{1,0:T(8,128)S(1)}, f32[200,128]{1,0:T(8,128)S(1)}, u32[]{:S(2)}, u32[]{:S(2)}) collective-permute-start(f32[200,128]{1,0:T(8,128)S(1)} %add_add_fusion.1), channel_id=1, source_target_pairs={{0,2},{1,3},{2,0},{3,1},{4,6},{5,7},{6,4},{7,5},{8,24},{9,25},{10,... | collective-permute-start | bytes 307208 | tf_op jit(solution)/shard_map/ppermute | solution.py:345
  32.1 2.9 %collective-permute-done.9 = f32[200,128]{1,0:T(8,128)S(1)} collective-permute-done((f32[200,128]{1,0:T(8,128)S(1)}, f32[200,128]{1,0:T(8,128)S(1)}, u32[]{:S(2)}, u32[]{:S(2)}) %collective-permute-start.9) | collective-permute-done | bytes 102432 | tf_op jit(solution)/shard_map/ppermute | solution.py:345
  35.0 1.8 %collective-permute-done.10 = f32[200,128]{1,0:T(8,128)S(1)} collective-permute-done((f32[200,128]{1,0:T(8,128)S(1)}, f32[200,128]{1,0:T(8,128)S(1)}, u32[]{:S(2)}, u32[]{:S(2)}) %collective-permute-start.10) | collective-permute-done | bytes 102432 | tf_op jit(solution)/shard_map/ppermute | solution.py:345
  36.8 0.6 %collective-permute-done.8 = f32[200,128]{1,0:T(8,128)S(1)} collective-permute-done((f32[200,128]{1,0:T(8,128)S(1)}, f32[200,128]{1,0:T(8,128)S(1)}, u32[]{:S(2)}, u32[]{:S(2)}) %collective-permute-start.8) | collective-permute-done | bytes 102432 | tf_op jit(solution)/shard_map/ppermute | solution.py:345
  37.4 0.1 collective-permute-start.11
  37.5 1.9 %assemble.1 = (f32[128,16,128]{2,1,0:T(8,128)}, f32[128,16,128]{2,1,0:T(8,128)}) custom-call(f32[2,12,128,128]{3,2,1,0:T(8,128)S(1)} %get-tuple-element.21.inner, f32[2,4,128,128]{3,2,1,0:T(8,128)S(1)} %get-tuple-element.26.border), custom_call_target="tpu_custom_call" | custom-call | bytes 7380000 | tf_op jit(solution)/shard_map/assemble/pallas_call | solution.py:434
  39.4 6.9 %factor.1 = f32[128,128]{1,0:T(8,128)} custom-call(f32[200,128]{1,0:T(8,128)S(1)} %add_add_fusion.kept, f32[200,128]{1,0:T(8,128)S(1)} %collective-permute-done.11.given), custom_call_target="tpu_custom_call" | custom-call | bytes 22140000 | tf_op jit(solution)/shard_map/factor/pallas_call | solution.py:451
  (9 shorter events, 0.1 us)
Async XLA Ops:
  3.1 14.9 %collective-permute-start.2 = (f32[3,2,128,128]{3,2,1,0:T(8,128)S(1)}, f32[3,2,128,128]{3,2,1,0:T(8,128)S(1)}, u32[]{:S(2)}, u32[]{:S(2)}) collective-permute-start(f32[3,2,128,128]{3,2,1,0:T(8,128)S(1)} %get-tuple-element.22), channel_id=1, source_target_pairs={{0,8},{8,0},{16,24},{24,16},{1,9},{9,1},{17,25},{25,17},{2,10},{10... | collective-permute-start | bytes 1179656 | tf_op jit(solution)/shard_map/ppermute | solution.py:393
  3.6 14.4 %collective-permute-start.3 = (f32[3,2,128,128]{3,2,1,0:T(8,128)S(1)}, f32[3,2,128,128]{3,2,1,0:T(8,128)S(1)}, u32[]{:S(2)}, u32[]{:S(2)}) collective-permute-start(f32[3,2,128,128]{3,2,1,0:T(8,128)S(1)} %get-tuple-element.23), channel_id=1, source_target_pairs={{0,24},{8,16},{16,8},{24,0},{1,25},{9,17},{17,9},{25,1},{2,26},{10... | collective-permute-start | bytes 1179656 | tf_op jit(solution)/shard_map/ppermute | solution.py:392
  6.3 7.4 %collective-permute-start = (f32[128,128]{1,0:T(8,128)S(1)}, f32[128,128]{1,0:T(8,128)S(1)}, u32[]{:S(2)}, u32[]{:S(2)}) collective-permute-start(f32[128,128]{1,0:T(8,128)S(1)} %get-tuple-element.19), channel_id=1, source_target_pairs={{0,1},{1,2},{2,3},{3,4},{4,5},{5,6},{6,7},{7,0},{8,9},{9,10},{10,1... | collective-permute-start | bytes 196616 | tf_op jit(solution)/shard_map/ppermute | solution.py:394
  7.8 5.9 %collective-permute-start.1 = (f32[128,128]{1,0:T(8,128)S(1)}, f32[128,128]{1,0:T(8,128)S(1)}, u32[]{:S(2)}, u32[]{:S(2)}) collective-permute-start(f32[128,128]{1,0:T(8,128)S(1)} %get-tuple-element.20), channel_id=1, source_target_pairs={{0,7},{1,0},{2,1},{3,2},{4,3},{5,4},{6,5},{7,6},{8,15},{9,8},{10,9... | collective-permute-start | bytes 196616 | tf_op jit(solution)/shard_map/ppermute | solution.py:395
  19.4 1.4 %collective-permute-start.4 = (f32[200,128]{1,0:T(8,128)S(1)}, f32[200,128]{1,0:T(8,128)S(1)}, u32[]{:S(2)}, u32[]{:S(2)}) collective-permute-start(f32[200,128]{1,0:T(8,128)S(1)} %get-tuple-element.30), channel_id=1, source_target_pairs={{0,8},{1,9},{2,10},{3,11},{4,12},{5,13},{6,14},{7,15},{8,0},{9,1},... | collective-permute-start | bytes 307208 | tf_op jit(solution)/shard_map/ppermute | solution.py:345
  20.8 4.7 %collective-permute-start.6 = (f32[200,128]{1,0:T(8,128)S(1)}, f32[200,128]{1,0:T(8,128)S(1)}, u32[]{:S(2)}, u32[]{:S(2)}) collective-permute-start(f32[200,128]{1,0:T(8,128)S(1)} %add.21), channel_id=1, source_target_pairs={{0,1},{1,0},{2,3},{3,2},{4,5},{5,4},{6,7},{7,6},{8,12},{9,13},{10,... | collective-permute-start | bytes 307208 | tf_op jit(solution)/shard_map/ppermute | solution.py:345
  21.6 5.7 %collective-permute-start.7 = (f32[200,128]{1,0:T(8,128)S(1)}, f32[200,128]{1,0:T(8,128)S(1)}, u32[]{:S(2)}, u32[]{:S(2)}) collective-permute-start(f32[200,128]{1,0:T(8,128)S(1)} %add.21), channel_id=1, source_target_pairs={{0,17},{1,16},{2,19},{3,18},{4,21},{5,20},{6,23},{7,22},{8,14},{9,... | collective-permute-start | bytes 307208 | tf_op jit(solution)/shard_map/ppermute | solution.py:345
  22.6 5.7 %collective-permute-start.5 = (f32[200,128]{1,0:T(8,128)S(1)}, f32[200,128]{1,0:T(8,128)S(1)}, u32[]{:S(2)}, u32[]{:S(2)}) collective-permute-start(f32[200,128]{1,0:T(8,128)S(1)} %add.21), channel_id=1, source_target_pairs={{0,16},{1,17},{2,18},{3,19},{4,20},{5,21},{6,22},{7,23},{8,10},{9,... | collective-permute-start | bytes 307208 | tf_op jit(solution)/shard_map/ppermute | solution.py:345
  28.3 6.7 %collective-permute-start.9 = (f32[200,128]{1,0:T(8,128)S(1)}, f32[200,128]{1,0:T(8,128)S(1)}, u32[]{:S(2)}, u32[]{:S(2)}) collective-permute-start(f32[200,128]{1,0:T(8,128)S(1)} %add_add_fusion.1), channel_id=1, source_target_pairs={{0,4},{1,5},{2,6},{3,7},{4,0},{5,1},{6,2},{7,3},{8,9},{9,8},{10,11... | collective-permute-start | bytes 307208 | tf_op jit(solution)/shard_map/ppermute | solution.py:345
  30.2 6.6 %collective-permute-start.10 = (f32[200,128]{1,0:T(8,128)S(1)}, f32[200,128]{1,0:T(8,128)S(1)}, u32[]{:S(2)}, u32[]{:S(2)}) collective-permute-start(f32[200,128]{1,0:T(8,128)S(1)} %add_add_fusion.1), channel_id=1, source_target_pairs={{0,6},{1,7},{2,4},{3,5},{4,2},{5,3},{6,0},{7,1},{8,25},{9,24},{10,... | collective-permute-start | bytes 307208 | tf_op jit(solution)/shard_map/ppermute | solution.py:345
  31.6 5.8 %collective-permute-start.8 = (f32[200,128]{1,0:T(8,128)S(1)}, f32[200,128]{1,0:T(8,128)S(1)}, u32[]{:S(2)}, u32[]{:S(2)}) collective-permute-start(f32[200,128]{1,0:T(8,128)S(1)} %add_add_fusion.1), channel_id=1, source_target_pairs={{0,2},{1,3},{2,0},{3,1},{4,6},{5,7},{6,4},{7,5},{8,24},{9,25},{10,... | collective-permute-start | bytes 307208 | tf_op jit(solution)/shard_map/ppermute | solution.py:345
  37.4 2.0 %collective-permute-start.11 = (f32[200,128]{1,0:T(8,128)S(1)}, f32[200,128]{1,0:T(8,128)S(1)}, u32[]{:S(2)}, u32[]{:S(2)}) collective-permute-start(f32[200,128]{1,0:T(8,128)S(1)} %add_add_fusion.kept), channel_id=1, source_target_pairs={{0,8},{1,9},{2,10},{3,11},{4,12},{5,13},{6,14},{7,15},{8,0},{9,1},... | collective-permute-start | bytes 307208 | tf_op jit(solution)/shard_map/ppermute | solution.py:345

commit v5 on v4

--- a/solution.py
+++ b/solution.py
@@ -8,7 +8,6 @@
 from jax.sharding import PartitionSpec as P
 
 TILE = 16
-BLOCK = 8
 CHUNKS = 2
 VMEM = pl.BlockSpec(memory_space=pltpu.VMEM)
 DIMS_NT = (((1,), (1,)), ((), ()))
@@ -29,9 +28,13 @@
 
 
 def gram_of(product):
-    size = product.shape[0]
-    mixed = product[:, size:]
-    return product[:, :size] + (mixed + mixed.T)
+    size = product.shape[0] // 2
+    same = product[:size, :size] + product[size:, size:]
+    return same + (product[:size, size:] + product[size:, :size])
+
+
+def square(pieces):
+    return lax.dot_general(pieces, pieces, DIMS_NT, preferred_element_type=jnp.float32)
 
 
 def halves(size):
@@ -105,7 +108,7 @@
 
 
 def derivative(minus_two, minus_one, plus_one, plus_two):
-    return minus_two - 8.0 * minus_one + 8.0 * plus_one - plus_two
+    return 8.0 * (plus_one - minus_one) - (plus_two - minus_two)
 
 
 def velocity_kernel(rows, planes, fields, grams, along_z, thirds, band):
@@ -126,11 +129,13 @@
                 low = (rest - middle.astype(jnp.float32)).astype(jnp.bfloat16)
                 for part, piece in enumerate((high, middle, low)):
                     thirds[y, t * TILE : (t + 1) * TILE, part * size : (part + 1) * size] = piece
-            high, middle = thirds[y, :, 0:size], thirds[y, :, size : 2 * size]
-            product = lax.dot_general(
-                high, jnp.concatenate([high, middle], axis=0), DIMS_NT, preferred_element_type=jnp.float32
-            )
-            total = product if y == 0 else total + product
+            if y % 2 == 1:
+                parts = [
+                    jnp.concatenate([thirds[y - 1, :, at : at + size], thirds[y, :, at : at + size]], axis=1)
+                    for at in (0, size)
+                ]
+                product = square(jnp.concatenate(parts, axis=0))
+                total = product if y == 1 else total + product
         grams[c] = gram_of(total)
         derivatives = jnp.dot(
             thirds[...].reshape(rows * planes, 3 * size), band[...], preferred_element_type=jnp.float32
@@ -192,25 +197,16 @@
     def row_at(c, y, k, t):
         return fields[c, y + k, pl.ds(2 + t * TILE, TILE), :]
 
-    @pl.loop(0, rows // 2 - 2)
-    def _(pair):
+    for pair in range(rows // 2 - 2):
+        buffer = pieces.at[pair % 2]
         for half in range(2):
             index = 2 * pair + half
             for t in range(planes // TILE):
                 results = invariants_of(fields, own_z, to_last, to_first, t, index + 2, rows, row_at)
-                store_results(results, out, index, pieces, half, t, planes, size)
+                store_results(results, out, index, buffer, half, t, planes, size)
         for f in range(2):
-            product = lax.dot_general(
-                pieces[f, 0:planes, :], pieces[f], DIMS_NT, preferred_element_type=jnp.float32
-            )
-
-            @pl.when(pair == 0)
-            def _():
-                total[f] = product
-
-            @pl.when(pair > 0)
-            def _():
-                total[f] += product
+            product = square(buffer[f])
+            total[f] = product if pair == 0 else total[f] + product
 
 
 def border_kernel(
@@ -232,14 +228,13 @@
 
     for index, y in enumerate((0, 1, rows - 2, rows - 1)):
         half = index % 2
+        buffer = pieces.at[index // 2]
         for t in range(planes // TILE):
             results = invariants_of(fields, own_z, to_last, to_first, t, y, rows, row_at)
-            store_results(results, out, index, pieces, half, t, planes, size)
+            store_results(results, out, index, buffer, half, t, planes, size)
         if half == 1:
             for f in range(2):
-                product = lax.dot_general(
-                    pieces[f, 0:planes, :], pieces[f], DIMS_NT, preferred_element_type=jnp.float32
-                )
+                product = square(buffer[f])
                 total[f] = (part[f] if index == 1 else total[f]) + product
     grams = [gram_of(total[f]) for f in range(2)] + [velocity[c] for c in range(3)]
     message[0:planes, :] = pack_pair(grams[0], grams[1])
@@ -252,52 +247,77 @@
     give[...] = message[pl.ds(other, keep.shape[0]), :]
 
 
-def assemble_kernel(rows, planes, inner, border, enstrophy, strain):
-    def plane_of(f, y):
+def assemble_kernel(rows, planes, f, inner, border, out):
+    def plane_of(y):
         if 2 <= y < rows - 2:
             return inner.at[f, y - 2]
         return border.at[f, y if y < 2 else y - rows + 4]
 
-    for f, out in enumerate((enstrophy, strain)):
-
-        @pl.loop(0, planes // 8)
-        def _(t):
-            at = pl.ds(pl.multiple_of(t * 8, 8), 8)
-            for base in range(0, rows, 8):
-                block = jnp.stack([plane_of(f, y)[at, :] for y in range(base, base + 8)], axis=0)
-                out[at, base : base + 8, :] = jnp.swapaxes(block, 0, 1)
-
-
-def thirds_of(values):
-    high = values.astype(jnp.bfloat16).astype(jnp.float32)
-    rest = values - high
-    middle = rest.astype(jnp.bfloat16).astype(jnp.float32)
-    return high, middle, rest - middle
-
-def splat_row(block, j):
-    return jnp.broadcast_to(block[j : j + 1, :], block.shape)
-
-def eliminate(rows, first):
-    count, size = rows.shape
-    columns = [jnp.broadcast_to(rows[:, first + j : first + j + 1], rows.shape) for j in range(count)]
-    entry = {(i, j): splat_row(columns[j], i) for j in range(count) for i in range(j, count)}
-    row = [splat_row(rows, j) for j in range(count)]
-    sub = lax.broadcasted_iota(jnp.int32, rows.shape, 0)
-    lane = lax.broadcasted_iota(jnp.int32, rows.shape, 1)
-    out = jnp.zeros_like(rows)
-    for j in range(count):
-        root = lax.rsqrt(entry[j, j])
-        lower = {i: entry[i, j] * root for i in range(j + 1, count)}
-        row[j] = row[j] * root
-        for i in range(j + 1, count):
-            for m in range(i, count):
-                entry[m, i] = entry[m, i] - lower[m] * lower[i]
-            row[i] = row[i] - lower[i] * row[j]
-        out = jnp.where(sub == j, row[j], out)
-    return jnp.where(lane >= first + sub, out, 0.0)
-
-
-def factor_kernel(cells, planes, kept, given, factor, message, work, upper):
+    @pl.loop(0, planes // 8)
+    def _(t):
+        at = pl.ds(pl.multiple_of(t * 8, 8), 8)
+        for base in range(0, rows, 8):
+            block = jnp.stack([plane_of(y)[at, :] for y in range(base, base + 8)], axis=0)
+            out[at, base : base + 8, :] = jnp.swapaxes(block, 0, 1)
+
+
+def splat(tile, j):
+    return jnp.broadcast_to(tile[j : j + 1, :], tile.shape)
+
+def spread_column(tile, at):
+    return jnp.broadcast_to(tile[:, at : at + 1], tile.shape)
+
+
+def factor_tiles(tiles, widths):
+    count, size = tiles[0].shape
+    sub = lax.broadcasted_iota(jnp.int32, (count, size), 0)
+    lane = lax.broadcasted_iota(jnp.int32, (count, size), 1)
+    tiles = list(tiles)
+    out = []
+    first = 0
+    for width in widths:
+        top = first // count
+        head = width // count
+        spread = [[spread_column(tiles[top + t], first + j) for t in range(head)] for j in range(width)]
+        rows = tiles[top : top + head]
+        results = [jnp.zeros((count, size), jnp.float32)] * head
+        inverses, entries, pivots = [], {}, []
+        pivot = splat(spread[0][0], 0)
+        for j in range(width):
+            t0, s0 = divmod(j, count)
+            inverse = 1.0 / pivot
+            inverses.append(inverse)
+            for m in range(j + 1, width):
+                entries[j, m] = splat(spread[j][m // count], m % count)
+            if j + 1 < width:
+                t1, s1 = divmod(j + 1, count)
+                following = splat(spread[j + 1][t1], s1) - (entries[j, j + 1] * entries[j, j + 1]) * inverse
+            row = splat(rows[t0], s0)
+            pivots.append(row)
+            results[t0] = jnp.where(sub == s0, row * lax.rsqrt(pivot), results[t0])
+            for t in range(t0, head):
+                scaled = spread[j][t] * inverse
+                for m in range(j + 1, width):
+                    spread[m][t] = spread[m][t] - scaled * entries[j, m]
+                rows[t] = rows[t] - scaled * row
+            if j + 1 < width:
+                pivot = following
+        for t in range(head):
+            out.append(jnp.where(lane >= first + t * count + sub, results[t], 0.0))
+        for t in range(top + head, len(tiles)):
+            tile = tiles[t]
+            columns = [spread_column(tile, first + j) for j in range(width)]
+            for j in range(width):
+                scaled = columns[j] * inverses[j]
+                for m in range(j + 1, width):
+                    columns[m] = columns[m] - scaled * entries[j, m]
+                tile = tile - scaled * pivots[j]
+            tiles[t] = tile
+        first += width
+    return out
+
+
+def factor_kernel(cells, planes, kept, given, factor, message):
     mine, other = half_starts(kept.shape[0])
     message[pl.ds(mine, kept.shape[0]), :] = kept[...]
     message[pl.ds(other, kept.shape[0]), :] = given[...]
@@ -319,17 +339,11 @@
     third = message[2 * planes : 3 * planes, :]
     third = third * scale(jnp.sum(jnp.where(eye, third, 0.0)))
     triangles = low_a + low_b
-    work[...] = triangles + triangles.T + (both_a + both_b) + third
-    for first in range(0, planes, BLOCK):
-        rows = eliminate(work[first : first + BLOCK, :], first)
-        upper[first : first + BLOCK, :] = rows
-        if first + BLOCK < planes:
-            high, middle, low = thirds_of(rows)
-            one = jnp.concatenate([high, high, middle, high, low, middle], axis=0).astype(jnp.bfloat16)
-            two = jnp.concatenate([high, middle, high, low, high, middle], axis=0).astype(jnp.bfloat16)
-            update = lax.dot_general(one, two, (((0,), (0,)), ((), ())), preferred_element_type=jnp.float32)
-            work[first + BLOCK :, :] -= update[first + BLOCK :, :]
-    factor[...] = upper[...].T
+    cross = triangles + triangles.T + (both_a + both_b) + third
+    wide = 16 if planes % 32 == 0 else 8
+    widths = [8] * (planes // 16) + [wide] * (planes // 2 // wide)
+    upper = factor_tiles([cross[t : t + 8, :] for t in range(0, planes, 8)], widths)
+    factor[...] = jnp.concatenate(upper, axis=0).T
 
 
 def cost(microseconds):
@@ -350,7 +364,7 @@
     assert count_y & (count_y - 1) == 0 and count_z & (count_z - 1) == 0
     bits = [count_z << i for i in range(1, count_y.bit_length() - 1)] + [1 << i for i in range(count_z.bit_length() - 1)]
     groups = [bits[i : i + 2] for i in range(0, len(bits), 2)]
-    return [[group[0]] if len(group) == 1 else [group[0], group[1], group[0] ^ group[1]] for group in groups]
+    return [[group[0]] if len(group) == 1 else [group[0] ^ group[1], group[0], group[1]] for group in groups]
 
 
 def add_terms(terms):
@@ -407,11 +421,11 @@
         cost_estimate=cost(2.5),
         name="velocity_grams",
     )(turned)
-    pieces = pltpu.VMEM((2, 2 * planes, 2 * cols), jnp.bfloat16)
+    pieces = pltpu.VMEM((2, 2, 2 * planes, 2 * cols), jnp.bfloat16)
     edges = [pltpu.VMEM((planes, cols), jnp.float32)] * 2
     inner, part = pl.pallas_call(
         functools.partial(interior_kernel, rows, planes),
-        out_shape=(f32(2, rows - 4, planes, cols), f32(2, planes, 2 * planes)),
+        out_shape=(f32(2, rows - 4, planes, cols), f32(2, 2 * planes, 2 * planes)),
         in_specs=[VMEM] * 4,
         out_specs=(VMEM, VMEM),
         scratch_shapes=[pieces, *edges],
@@ -426,26 +440,29 @@
         out_shape=(f32(2, 4, planes, cols), f32(half, planes), f32(half, planes)),
         in_specs=[VMEM] * 8,
         out_specs=(VMEM, VMEM, VMEM),
-        scratch_shapes=[message, pieces, pltpu.VMEM((2, planes, 2 * planes), jnp.float32), *edges],
+        scratch_shapes=[message, pieces, pltpu.VMEM((2, 2 * planes, 2 * planes), jnp.float32), *edges],
         compiler_params=params(),
         cost_estimate=cost(1),
         name="border",
     )(turned, own_z, near, far, left, right, part, velocity)
-    enstrophy, strain_rate = pl.pallas_call(
-        functools.partial(assemble_kernel, rows, planes),
-        out_shape=(f32(planes, rows, cols), f32(planes, rows, cols)),
-        in_specs=[VMEM] * 2,
-        out_specs=(VMEM, VMEM),
-        compiler_params=params(),
-        cost_estimate=cost(2),
-        name="assemble",
-    )(inner, border)
-
+    enstrophy, strain_rate = [
+        pl.pallas_call(
+            functools.partial(assemble_kernel, rows, planes, f),
+            out_shape=f32(planes, rows, cols),
+            in_specs=[VMEM] * 2,
+            out_specs=VMEM,
+            compiler_params=params(),
+            cost_estimate=cost(1),
+            name="assemble",
+        )(inner, border)
+        for f in range(2)
+    ]
     core = count_z
     kept = keep + exchange(give, core, core)
     masks = rounds()
     for even, odd in zip(masks, masks[::-1]):
         kept = add_terms([kept] + [exchange(kept, *pair) for pair in zip(even, odd)])
+    kept, enstrophy, strain_rate = lax.optimization_barrier((kept, enstrophy, strain_rate))
     given = exchange(kept, core, core)
     cells = rows * cols * count_y * count_z
     factor = pl.pallas_call(
@@ -453,7 +470,7 @@
         out_shape=f32(planes, planes),
         in_specs=[VMEM] * 2,
         out_specs=VMEM,
-        scratch_shapes=[message] + [pltpu.VMEM((planes, planes), jnp.float32)] * 2,
+        scratch_shapes=[message],
         compiler_params=params(),
         cost_estimate=cost(6),
         name="factor",

time: 46.5 us -> 43.4 us (0.933)
  Pallas kernels: 19.6 us -> 15.6 us
  starting transfers between devices: 15.4 us -> 16 us
    pallas_call x1, Pallas kernels: 6.88 us -> 4.25 us  [per_device(): pl.pallas_call(functools.partial(factor_kernel, float(cells), planes), ou...]
    pallas_call x1, Pallas kernels: 4.34 us -> 2.52 us  [per_device(): pl.pallas_call(functools.partial(interior_kernel, rows, planes), out_shap...]
    ppermute x8, starting transfers between devices: 7.47 us -> 8.14 us  [exchange(): lax.ppermute(values, AXES, [(i, i ^ (odd if i // count_z % 2 else even))...]
    pallas_call x1 -> x2, Pallas kernels: 1.9 us -> 2.52 us  [per_device(): pl.pallas_call(functools.partial(assemble_kernel, rows, planes, f), out_s...]
  transfers between devices with their start and end apart: 12 -> 12, of which waited for: 7 -> 7; matrix products, arithmetic and copies ran while one was open for 0% -> 0% of each run, Pallas kernels for 19% -> 18%
where the time goes in v5:
time: 43.4 us; the launch traced here: 43.2 us
  starting transfers between devices  16 us (37%)
  Pallas kernels  15.6 us (36%)
  waiting for transfers between devices  10.8 us (25%)
  between operations  0.71 us (2%)
    ppermute x8, waiting for transfers between devices, exchange(): lax.ppermute(values, AXES, [(i, i ^ (odd if i // count_z % 2 else even))...  10.8 us
    ppermute x8, starting transfers between devices, exchange(): lax.ppermute(values, AXES, [(i, i ^ (odd if i // count_z % 2 else even))...  8.14 us
    pallas_call x1, Pallas kernels, per_device(): pl.pallas_call(functools.partial(factor_kernel, float(cells), planes), ou...  4.25 us
    ppermute x1, starting transfers between devices, per_device(): lax.ppermute(behind, 'gz', [(i, (i - 1) % count_z) for i in range(count_z)])  3.23 us
    ppermute x1, starting transfers between devices, per_device(): lax.ppermute(far, 'gy', [(i, (i + 1 if i % 2 else i - 1) % count_y) for i...  2.65 us
    pallas_call x1, Pallas kernels, per_device(): pl.pallas_call(functools.partial(velocity_kernel, rows, planes), out_shap...  2.6 us
    pallas_call x1, Pallas kernels, per_device(): pl.pallas_call(functools.partial(interior_kernel, rows, planes), out_shap...  2.52 us
    pallas_call x2, Pallas kernels, per_device(): pl.pallas_call(functools.partial(assemble_kernel, rows, planes, f), out_s...  2.52 us
  transfers between devices with their start and end apart: 12, of which 7 were waited for; matrix products, arithmetic and copies ran while one was open for 0% of the time, Pallas kernels for 18%

profile of v5, /device:TPU:0, one launch (start us, length us, event | category | flops | bytes accessed | tf_op | source)
XLA Modules:
  0.0 43.2 jit_solution(23365520121069233)
XLA Ops:
  0.6 2.5 %faces.1 = (f32[3,16,132,128]{3,2,1,0:T(8,128)S(1)}, f32[3,2,128,128]{3,2,1,0:T(8,128)S(1)}, f32[3,2,128,128]{3,2,1,0:T(8,128)S(1)}, f32[128,128]{1,0:T(8,128)S(1)}, f32[128,128]{1,0:T(8,128)S(1)}) custom-call(f32[3,132,16,128]{3,2,1,0:T(8,128)} %fields.1), custom_call_target="tpu_custom_call" | custom-call | bytes 18450000 | tf_op jit(solution)/shard_map/faces/pallas_call | solution.py:385
  3.1 0.5 %collective-permute-start = (f32[3,2,128,128]{3,2,1,0:T(8,128)S(1)}, f32[3,2,128,128]{3,2,1,0:T(8,128)S(1)}, u32[]{:S(2)}, u32[]{:S(2)}) collective-permute-start(f32[3,2,128,128]{3,2,1,0:T(8,128)S(1)} %get-tuple-element.20), channel_id=1, source_target_pairs={{0,8},{8,0},{16,24},{24,16},{1,9},{9,1},{17,25},{25,17},{2,10},{10... | collective-permute-start | bytes 1179656 | tf_op jit(solution)/shard_map/ppermute | solution.py:407
  3.6 2.6 %collective-permute-start.1 = (f32[3,2,128,128]{3,2,1,0:T(8,128)S(1)}, f32[3,2,128,128]{3,2,1,0:T(8,128)S(1)}, u32[]{:S(2)}, u32[]{:S(2)}) collective-permute-start(f32[3,2,128,128]{3,2,1,0:T(8,128)S(1)} %get-tuple-element.21), channel_id=1, source_target_pairs={{0,24},{8,16},{16,8},{24,0},{1,25},{9,17},{17,9},{25,1},{2,26},{10... | collective-permute-start | bytes 1179656 | tf_op jit(solution)/shard_map/ppermute | solution.py:406
  6.3 1.5 %collective-permute-start.2 = (f32[128,128]{1,0:T(8,128)S(1)}, f32[128,128]{1,0:T(8,128)S(1)}, u32[]{:S(2)}, u32[]{:S(2)}) collective-permute-start(f32[128,128]{1,0:T(8,128)S(1)} %get-tuple-element.22), channel_id=1, source_target_pairs={{0,1},{1,2},{2,3},{3,4},{4,5},{5,6},{6,7},{7,0},{8,9},{9,10},{10,1... | collective-permute-start | bytes 196616 | tf_op jit(solution)/shard_map/ppermute | solution.py:408
  7.8 3.2 %collective-permute-start.3 = (f32[128,128]{1,0:T(8,128)S(1)}, f32[128,128]{1,0:T(8,128)S(1)}, u32[]{:S(2)}, u32[]{:S(2)}) collective-permute-start(f32[128,128]{1,0:T(8,128)S(1)} %get-tuple-element.23), channel_id=1, source_target_pairs={{0,7},{1,0},{2,1},{3,2},{4,3},{5,4},{6,5},{7,6},{8,15},{9,8},{10,9... | collective-permute-start | bytes 196616 | tf_op jit(solution)/shard_map/ppermute | solution.py:409
  11.0 2.6 %velocity_grams.1 = (f32[3,128,128]{2,1,0:T(8,128)S(1)}, f32[3,16,128,128]{3,2,1,0:T(8,128)S(1)}) custom-call(f32[3,16,132,128]{3,2,1,0:T(8,128)S(1)} %get-tuple-element.18.fields), custom_call_target="tpu_custom_call" | custom-call | bytes 9225000 | tf_op jit(solution)/shard_map/velocity_grams/pallas_call | solution.py:411
  13.6 2.5 %interior.1 = (f32[2,12,128,128]{3,2,1,0:T(8,128)S(1)}, f32[2,256,256]{2,1,0:T(8,128)S(1)}) custom-call(f32[3,16,132,128]{3,2,1,0:T(8,128)S(1)} %get-tuple-element.18.fields, f32[3,16,128,128]{3,2,1,0:T(8,128)S(1)} %get-tuple-element.19.own_z, f32[128,128]{1,0:T(8,128)S(1)} %collective-permute-done.2.left, f32[128,128]{1,0:T(8,128)S(1)} %collective-permute-done.3.right), custom_call_target="tpu_custom_call" | custom-call | bytes 14760000 | tf_op jit(solution)/shard_map/interior/pallas_call | solution.py:426
  16.2 1.2 %border.1 = (f32[2,4,128,128]{3,2,1,0:T(8,128)S(1)}, f32[200,128]{1,0:T(8,128)S(1)}, f32[200,128]{1,0:T(8,128)S(1)}) custom-call(f32[3,16,132,128]{3,2,1,0:T(8,128)S(1)} %get-tuple-element.18.fields, f32[3,16,128,128]{3,2,1,0:T(8,128)S(1)} %get-tuple-element.19.own_z, f32[3,2,128,128]{3,2,1,0:T(8,128)S(1)} %collective-permute-done.near, ...), custom_call_target="tpu_custom_call" | custom-call | bytes 3690000 | tf_op jit(solution)/shard_map/border/pallas_call | solution.py:438
  17.5 1.3 %collective-permute-done.4 = f32[200,128]{1,0:T(8,128)S(1)} collective-permute-done((f32[200,128]{1,0:T(8,128)S(1)}, f32[200,128]{1,0:T(8,128)S(1)}, u32[]{:S(2)}, u32[]{:S(2)}) %collective-permute-start.4) | collective-permute-done | bytes 102432 | tf_op jit(solution)/shard_map/ppermute | solution.py:359
  18.8 1.0 %collective-permute-start.7 = (f32[200,128]{1,0:T(8,128)S(1)}, f32[200,128]{1,0:T(8,128)S(1)}, u32[]{:S(2)}, u32[]{:S(2)}) collective-permute-start(f32[200,128]{1,0:T(8,128)S(1)} %add.21), channel_id=1, source_target_pairs={{0,1},{1,0},{2,3},{3,2},{4,5},{5,4},{6,7},{7,6},{8,12},{9,13},{10,... | collective-permute-start | bytes 307208 | tf_op jit(solution)/shard_map/ppermute | solution.py:359
  19.8 1.5 %collective-permute-start.6 = (f32[200,128]{1,0:T(8,128)S(1)}, f32[200,128]{1,0:T(8,128)S(1)}, u32[]{:S(2)}, u32[]{:S(2)}) collective-permute-start(f32[200,128]{1,0:T(8,128)S(1)} %add.21), channel_id=1, source_target_pairs={{0,16},{1,17},{2,18},{3,19},{4,20},{5,21},{6,22},{7,23},{8,10},{9,... | collective-permute-start | bytes 307208 | tf_op jit(solution)/shard_map/ppermute | solution.py:359
  21.3 1.1 %collective-permute-start.5 = (f32[200,128]{1,0:T(8,128)S(1)}, f32[200,128]{1,0:T(8,128)S(1)}, u32[]{:S(2)}, u32[]{:S(2)}) collective-permute-start(f32[200,128]{1,0:T(8,128)S(1)} %add.21), channel_id=1, source_target_pairs={{0,17},{1,16},{2,19},{3,18},{4,21},{5,20},{6,23},{7,22},{8,14},{9,... | collective-permute-start | bytes 307208 | tf_op jit(solution)/shard_map/ppermute | solution.py:359
  22.4 1.2 %collective-permute-done.7 = f32[200,128]{1,0:T(8,128)S(1)} collective-permute-done((f32[200,128]{1,0:T(8,128)S(1)}, f32[200,128]{1,0:T(8,128)S(1)}, u32[]{:S(2)}, u32[]{:S(2)}) %collective-permute-start.7) | collective-permute-done | bytes 102432 | tf_op jit(solution)/shard_map/ppermute | solution.py:359
  23.5 0.9 %collective-permute-done.6 = f32[200,128]{1,0:T(8,128)S(1)} collective-permute-done((f32[200,128]{1,0:T(8,128)S(1)}, f32[200,128]{1,0:T(8,128)S(1)}, u32[]{:S(2)}, u32[]{:S(2)}) %collective-permute-start.6) | collective-permute-done | bytes 102432 | tf_op jit(solution)/shard_map/ppermute | solution.py:359
  24.4 2.4 %collective-permute-done.5 = f32[200,128]{1,0:T(8,128)S(1)} collective-permute-done((f32[200,128]{1,0:T(8,128)S(1)}, f32[200,128]{1,0:T(8,128)S(1)}, u32[]{:S(2)}, u32[]{:S(2)}) %collective-permute-start.5) | collective-permute-done | bytes 102432 | tf_op jit(solution)/shard_map/ppermute | solution.py:359
  26.9 2.7 %collective-permute-start.10 = (f32[200,128]{1,0:T(8,128)S(1)}, f32[200,128]{1,0:T(8,128)S(1)}, u32[]{:S(2)}, u32[]{:S(2)}) collective-permute-start(f32[200,128]{1,0:T(8,128)S(1)} %add_add_fusion.1), channel_id=1, source_target_pairs={{0,4},{1,5},{2,6},{3,7},{4,0},{5,1},{6,2},{7,3},{8,9},{9,8},{10,11... | collective-permute-start | bytes 307208 | tf_op jit(solution)/shard_map/ppermute | solution.py:359
  29.5 1.6 %collective-permute-start.9 = (f32[200,128]{1,0:T(8,128)S(1)}, f32[200,128]{1,0:T(8,128)S(1)}, u32[]{:S(2)}, u32[]{:S(2)}) collective-permute-start(f32[200,128]{1,0:T(8,128)S(1)} %add_add_fusion.1), channel_id=1, source_target_pairs={{0,2},{1,3},{2,0},{3,1},{4,6},{5,7},{6,4},{7,5},{8,24},{9,25},{10,... | collective-permute-start | bytes 307208 | tf_op jit(solution)/shard_map/ppermute | solution.py:359
  31.1 0.2 collective-permute-start.8
  31.3 1.3 %assemble.3 = f32[128,16,128]{2,1,0:T(8,128)} custom-call(f32[2,12,128,128]{3,2,1,0:T(8,128)S(1)} %get-tuple-element.28.inner, f32[2,4,128,128]{3,2,1,0:T(8,128)S(1)} %get-tuple-element.29.border), custom_call_target="tpu_custom_call" | custom-call | bytes 3690000 | tf_op jit(solution)/shard_map/assemble/pallas_call | solution.py:449
  32.6 1.3 %assemble.2 = f32[128,16,128]{2,1,0:T(8,128)} custom-call(f32[2,12,128,128]{3,2,1,0:T(8,128)S(1)} %get-tuple-element.28.inner, f32[2,4,128,128]{3,2,1,0:T(8,128)S(1)} %get-tuple-element.29.border), custom_call_target="tpu_custom_call" | custom-call | bytes 3690000 | tf_op jit(solution)/shard_map/assemble/pallas_call | solution.py:449
  33.8 0.3 collective-permute-done.9
  34.2 3.4 %collective-permute-done.8 = f32[200,128]{1,0:T(8,128)S(1)} collective-permute-done((f32[200,128]{1,0:T(8,128)S(1)}, f32[200,128]{1,0:T(8,128)S(1)}, u32[]{:S(2)}, u32[]{:S(2)}) %collective-permute-start.8) | collective-permute-done | bytes 102432 | tf_op jit(solution)/shard_map/ppermute | solution.py:359
  37.7 1.3 %collective-permute-done.11.given = f32[200,128]{1,0:T(8,128)S(1)} collective-permute-done((f32[200,128]{1,0:T(8,128)S(1)}, f32[200,128]{1,0:T(8,128)S(1)}, u32[]{:S(2)}, u32[]{:S(2)}) %collective-permute-start.11) | collective-permute-done | bytes 102432 | tf_op jit(solution)/shard_map/ppermute | solution.py:359
  39.0 4.2 %factor.1 = f32[128,128]{1,0:T(8,128)} custom-call(f32[200,128]{1,0:T(8,128)S(1)} %add_add_fusion.kept, f32[200,128]{1,0:T(8,128)S(1)} %collective-permute-done.11.given), custom_call_target="tpu_custom_call" | custom-call | bytes 22140000 | tf_op jit(solution)/shard_map/factor/pallas_call | solution.py:468
  (10 shorter events, 0.2 us)
Async XLA Ops:
  3.1 13.0 %collective-permute-start = (f32[3,2,128,128]{3,2,1,0:T(8,128)S(1)}, f32[3,2,128,128]{3,2,1,0:T(8,128)S(1)}, u32[]{:S(2)}, u32[]{:S(2)}) collective-permute-start(f32[3,2,128,128]{3,2,1,0:T(8,128)S(1)} %get-tuple-element.20), channel_id=1, source_target_pairs={{0,8},{8,0},{16,24},{24,16},{1,9},{9,1},{17,25},{25,17},{2,10},{10... | collective-permute-start | bytes 1179656 | tf_op jit(solution)/shard_map/ppermute | solution.py:407
  3.6 12.5 %collective-permute-start.1 = (f32[3,2,128,128]{3,2,1,0:T(8,128)S(1)}, f32[3,2,128,128]{3,2,1,0:T(8,128)S(1)}, u32[]{:S(2)}, u32[]{:S(2)}) collective-permute-start(f32[3,2,128,128]{3,2,1,0:T(8,128)S(1)} %get-tuple-element.21), channel_id=1, source_target_pairs={{0,24},{8,16},{16,8},{24,0},{1,25},{9,17},{17,9},{25,1},{2,26},{10... | collective-permute-start | bytes 1179656 | tf_op jit(solution)/shard_map/ppermute | solution.py:406
  6.3 7.3 %collective-permute-start.2 = (f32[128,128]{1,0:T(8,128)S(1)}, f32[128,128]{1,0:T(8,128)S(1)}, u32[]{:S(2)}, u32[]{:S(2)}) collective-permute-start(f32[128,128]{1,0:T(8,128)S(1)} %get-tuple-element.22), channel_id=1, source_target_pairs={{0,1},{1,2},{2,3},{3,4},{4,5},{5,6},{6,7},{7,0},{8,9},{9,10},{10,1... | collective-permute-start | bytes 196616 | tf_op jit(solution)/shard_map/ppermute | solution.py:408
  7.8 5.9 %collective-permute-start.3 = (f32[128,128]{1,0:T(8,128)S(1)}, f32[128,128]{1,0:T(8,128)S(1)}, u32[]{:S(2)}, u32[]{:S(2)}) collective-permute-start(f32[128,128]{1,0:T(8,128)S(1)} %get-tuple-element.23), channel_id=1, source_target_pairs={{0,7},{1,0},{2,1},{3,2},{4,3},{5,4},{6,5},{7,6},{8,15},{9,8},{10,9... | collective-permute-start | bytes 196616 | tf_op jit(solution)/shard_map/ppermute | solution.py:409
  17.4 1.4 %collective-permute-start.4 = (f32[200,128]{1,0:T(8,128)S(1)}, f32[200,128]{1,0:T(8,128)S(1)}, u32[]{:S(2)}, u32[]{:S(2)}) collective-permute-start(f32[200,128]{1,0:T(8,128)S(1)} %get-tuple-element.27), channel_id=1, source_target_pairs={{0,8},{1,9},{2,10},{3,11},{4,12},{5,13},{6,14},{7,15},{8,0},{9,1},... | collective-permute-start | bytes 307208 | tf_op jit(solution)/shard_map/ppermute | solution.py:359
  18.8 4.7 %collective-permute-start.7 = (f32[200,128]{1,0:T(8,128)S(1)}, f32[200,128]{1,0:T(8,128)S(1)}, u32[]{:S(2)}, u32[]{:S(2)}) collective-permute-start(f32[200,128]{1,0:T(8,128)S(1)} %add.21), channel_id=1, source_target_pairs={{0,1},{1,0},{2,3},{3,2},{4,5},{5,4},{6,7},{7,6},{8,12},{9,13},{10,... | collective-permute-start | bytes 307208 | tf_op jit(solution)/shard_map/ppermute | solution.py:359
  19.8 4.7 %collective-permute-start.6 = (f32[200,128]{1,0:T(8,128)S(1)}, f32[200,128]{1,0:T(8,128)S(1)}, u32[]{:S(2)}, u32[]{:S(2)}) collective-permute-start(f32[200,128]{1,0:T(8,128)S(1)} %add.21), channel_id=1, source_target_pairs={{0,16},{1,17},{2,18},{3,19},{4,20},{5,21},{6,22},{7,23},{8,10},{9,... | collective-permute-start | bytes 307208 | tf_op jit(solution)/shard_map/ppermute | solution.py:359
  21.3 5.6 %collective-permute-start.5 = (f32[200,128]{1,0:T(8,128)S(1)}, f32[200,128]{1,0:T(8,128)S(1)}, u32[]{:S(2)}, u32[]{:S(2)}) collective-permute-start(f32[200,128]{1,0:T(8,128)S(1)} %add.21), channel_id=1, source_target_pairs={{0,17},{1,16},{2,19},{3,18},{4,21},{5,20},{6,23},{7,22},{8,14},{9,... | collective-permute-start | bytes 307208 | tf_op jit(solution)/shard_map/ppermute | solution.py:359
  26.9 7.0 %collective-permute-start.10 = (f32[200,128]{1,0:T(8,128)S(1)}, f32[200,128]{1,0:T(8,128)S(1)}, u32[]{:S(2)}, u32[]{:S(2)}) collective-permute-start(f32[200,128]{1,0:T(8,128)S(1)} %add_add_fusion.1), channel_id=1, source_target_pairs={{0,4},{1,5},{2,6},{3,7},{4,0},{5,1},{6,2},{7,3},{8,9},{9,8},{10,11... | collective-permute-start | bytes 307208 | tf_op jit(solution)/shard_map/ppermute | solution.py:359
  29.5 4.7 %collective-permute-start.9 = (f32[200,128]{1,0:T(8,128)S(1)}, f32[200,128]{1,0:T(8,128)S(1)}, u32[]{:S(2)}, u32[]{:S(2)}) collective-permute-start(f32[200,128]{1,0:T(8,128)S(1)} %add_add_fusion.1), channel_id=1, source_target_pairs={{0,2},{1,3},{2,0},{3,1},{4,6},{5,7},{6,4},{7,5},{8,24},{9,25},{10,... | collective-permute-start | bytes 307208 | tf_op jit(solution)/shard_map/ppermute | solution.py:359
  31.1 6.5 %collective-permute-start.8 = (f32[200,128]{1,0:T(8,128)S(1)}, f32[200,128]{1,0:T(8,128)S(1)}, u32[]{:S(2)}, u32[]{:S(2)}) collective-permute-start(f32[200,128]{1,0:T(8,128)S(1)} %add_add_fusion.1), channel_id=1, source_target_pairs={{0,6},{1,7},{2,4},{3,5},{4,2},{5,3},{6,0},{7,1},{8,25},{9,24},{10,... | collective-permute-start | bytes 307208 | tf_op jit(solution)/shard_map/ppermute | solution.py:359
  37.6 1.4 %collective-permute-start.11 = (f32[200,128]{1,0:T(8,128)S(1)}, f32[200,128]{1,0:T(8,128)S(1)}, u32[]{:S(2)}, u32[]{:S(2)}) collective-permute-start(f32[200,128]{1,0:T(8,128)S(1)} %add_add_fusion.kept), channel_id=1, source_target_pairs={{0,8},{1,9},{2,10},{3,11},{4,12},{5,13},{6,14},{7,15},{8,0},{9,1},... | collective-permute-start | bytes 307208 | tf_op jit(solution)/shard_map/ppermute | solution.py:359

commit v6 on v5

--- a/solution.py
+++ b/solution.py
@@ -8,7 +8,6 @@
 from jax.sharding import PartitionSpec as P
 
 TILE = 16
-CHUNKS = 2
 VMEM = pl.BlockSpec(memory_space=pltpu.VMEM)
 DIMS_NT = (((1,), (1,)), ((), ()))
 
@@ -58,28 +57,31 @@
     return jnp.sum(jnp.where(row == col, matrix, 0.0), axis=0, keepdims=True)
 
 
-def faces_kernel(rows, planes, fields, turned_fields, near, far, behind, ahead, landed, tails, heads, arrived):
+def far_kernel(rows, planes, fields, far, arrived):
+    first = lax.axis_index("gy") % 2 * (rows - 2)
+    copies = []
+    for layer in range(2):
+        for c in range(3):
+            source = fields.at[c, pl.ds(2, planes), first + layer, :]
+            copies.append(pltpu.make_async_copy(source, far.at[c, layer], arrived.at[layer, c]))
+            copies[-1].start()
+    for copy in copies:
+        copy.wait()
+
+
+def faces_kernel(rows, planes, fields, turned_fields, near_0, near_1, behind, ahead, tails, heads):
     odd = lax.axis_index("gy") % 2
     size = fields.shape[3]
     depth = planes + 4
-    cuts = [depth * i // CHUNKS for i in range(CHUNKS + 1)]
-    cuts = [cut - cut % 8 for cut in cuts[:-1]] + [depth]
-    copies = []
-    for c in range(3):
-        for i in range(CHUNKS):
-            part = pl.ds(cuts[i], cuts[i + 1] - cuts[i])
-            copies.append(pltpu.make_async_copy(fields.at[c, part], landed.at[c, part], arrived.at[c, i]))
-            copies[-1].start()
     lane = lanes((8, size))
     near_row = (1 - odd) * (rows - 2)
-    far_row = odd * (rows - 2)
 
     def turn(c, first):
         at = pl.ds(first, 8)
         tail = tails[at, :]
         head = heads[at, :]
         for base in range(0, rows, 8):
-            block = jnp.swapaxes(landed[c, at, base : base + 8, :], 0, 1)
+            block = jnp.swapaxes(fields[c, at, base : base + 8, :], 0, 1)
             for j in range(8):
                 y = base + j
                 k = c * rows + y
@@ -91,18 +93,15 @@
         heads[at, :] = head
 
     for c in range(3):
-        for i in range(CHUNKS):
-            copies[c * CHUNKS + i].wait()
-
-            @pl.loop(cuts[i] // 8, cuts[i + 1] // 8, unroll=8)
-            def _(t):
-                turn(c, pl.multiple_of(t * 8, 8))
+
+        @pl.loop(0, depth // 8, unroll=8)
+        def _(t):
+            turn(c, pl.multiple_of(t * 8, 8))
 
         if depth % 8:
             turn(c, depth - 8)
-        for layer in range(2):
-            near[c, layer] = turned_fields[c, near_row + layer, 2 : planes + 2, :]
-            far[c, layer] = turned_fields[c, far_row + layer, 2 : planes + 2, :]
+        for layer, near in enumerate((near_0, near_1)):
+            near[c] = turned_fields[c, near_row + layer, 2 : planes + 2, :]
     ahead[...] = tails[2 : planes + 2, :]
     behind[...] = heads[2 : planes + 2, :]
 
@@ -111,13 +110,33 @@
     return 8.0 * (plus_one - minus_one) - (plus_two - minus_two)
 
 
-def velocity_kernel(rows, planes, fields, grams, along_z, thirds, band):
+def inner_kernel(rows, planes, fields, grams, along_z, spin, stretch, bend_x, bend_y, thirds, band):
     size = fields.shape[3]
     row = lax.broadcasted_iota(jnp.int32, (3 * size, size), 0) % size
     col = lax.broadcasted_iota(jnp.int32, (3 * size, size), 1)
     far_side = jnp.where(row == col - 2, 1.0, jnp.where(row == col + 2, -1.0, 0.0))
     near_side = jnp.where(row == col - 1, -8.0, jnp.where(row == col + 1, 8.0, 0.0))
     band[...] = (far_side + near_side).astype(jnp.bfloat16)
+
+    def planar(index, t):
+        y = index + 2
+        at = pl.ds(t * TILE, TILE)
+        x, y = [
+            [
+                derivative(*[fields[c, y + k * step, pl.ds(2 + t * TILE + k * (1 - step), TILE), :] for k in (-2, -1, 1, 2)])
+                for c in range(3)
+            ]
+            for step in (0, 1)
+        ]
+        turn = x[1] - y[0]
+        shear = x[1] + y[0]
+        spin[index, at, :] = turn * turn
+        stretch[index, at, :] = 2.0 * (x[0] * x[0] + y[1] * y[1]) + shear * shear
+        bend_x[index, at, :] = x[2]
+        bend_y[index, at, :] = y[2]
+
+    tiles = [(index, t) for index in range(rows - 4) for t in range(planes // TILE)]
+    done = 0
     for c in range(3):
         total = None
         for y in range(rows):
@@ -136,6 +155,10 @@
                 ]
                 product = square(jnp.concatenate(parts, axis=0))
                 total = product if y == 1 else total + product
+            upto = len(tiles) * (c * rows + y + 1) // (3 * rows)
+            for tile in tiles[done:upto]:
+                planar(*tile)
+            done = upto
         grams[c] = gram_of(total)
         derivatives = jnp.dot(
             thirds[...].reshape(rows * planes, 3 * size), band[...], preferred_element_type=jnp.float32
@@ -153,31 +176,26 @@
     return to_last, to_first
 
 
-def invariants_of(fields, own_z, to_last, to_first, t, y, rows, row_at):
-    size = fields.shape[3]
+def z_derivatives(own_z, to_last, to_first, t, y, rows):
+    size = own_z.shape[3]
     lane = lanes((TILE, size))
     edge = (lane < 2) | (lane >= size - 2)
     at = pl.ds(t * TILE, TILE)
-    along_x, along_y, along_z = [], [], []
+    along_z = []
     for c in range(3):
-        along_x.append(derivative(*[fields[c, y, pl.ds(2 + t * TILE + k, TILE), :] for k in (-2, -1, 1, 2)]))
-        along_y.append(derivative(*[row_at(c, y, k, t) for k in (-2, -1, 1, 2)]))
         k = c * rows + y
         terms = jnp.where(lane < 2 * k + 2, to_last[at, :], to_first[at, :])
         terms = pltpu.roll(terms, (2 * size - 2 - 2 * k) % size, 1)
         along_z.append(own_z[c, y, at, :] + jnp.where(edge, terms, 0.0))
-    gradient = (along_x, along_y, along_z)
-    normal = [gradient[a][a] * gradient[a][a] for a in range(3)]
-    rotation, shearing = [], []
-    for a, b in ((0, 1), (0, 2), (1, 2)):
-        turn = gradient[a][b] - gradient[b][a]
-        shear = gradient[a][b] + gradient[b][a]
-        rotation.append(turn * turn)
-        shearing.append(shear * shear)
-    enstrophy = (rotation[0] + rotation[1] + rotation[2]) * (1.0 / 288.0)
-    strain = (normal[0] + normal[1] + normal[2]) * (1.0 / 144.0)
-    strain = strain + (shearing[0] + shearing[1] + shearing[2]) * (1.0 / 288.0)
-    return enstrophy, strain
+    return along_z
+
+
+def finish(spin, stretch, bend_x, bend_y, z):
+    turn_x, turn_y = bend_x - z[0], bend_y - z[1]
+    shear_x, shear_y = bend_x + z[0], bend_y + z[1]
+    enstrophy = spin + turn_x * turn_x + turn_y * turn_y
+    strain = stretch + 2.0 * (z[2] * z[2]) + (shear_x * shear_x + shear_y * shear_y)
+    return enstrophy * (1.0 / 288.0), strain * (1.0 / 288.0)
 
 
 def store_results(results, out, index, pieces, half, t, planes, size):
@@ -190,53 +208,64 @@
         pieces[f, lower, half * size : (half + 1) * size] = low
 
 
-def interior_kernel(rows, planes, fields, own_z, left, right, out, total, pieces, to_last, to_first):
-    size = fields.shape[3]
+def beside_face(rows, planes, fields, own_z, halo, lower, to_last, to_first, t):
+    at = pl.ds(t * TILE, TILE)
+    within = pl.ds(2 + t * TILE, TILE)
+    first = jnp.where(lower, 0, rows - 2)
+
+    def window(c):
+        own = [fields[c, jnp.where(lower, 0, rows - 4) + i, within, :] for i in range(4)]
+        ends = [halo[i][c, at, :] for i in range(2)]
+        before = [jnp.where(lower, ends[i], own[i]) for i in range(2)]
+        centre = [jnp.where(lower, own[i], own[i + 2]) for i in range(2)]
+        after = [jnp.where(lower, own[i + 2], ends[i]) for i in range(2)]
+        return before + centre + after
+
+    windows = [window(c) for c in range(3)]
+    for i in range(2):
+        y = first + i
+        z = z_derivatives(own_z, to_last, to_first, t, y, rows)
+        along_x = [derivative(*[fields[c, y, pl.ds(2 + t * TILE + k, TILE), :] for k in (-2, -1, 1, 2)]) for c in range(3)]
+        along_y = [derivative(*[windows[c][2 + i + k] for k in (-2, -1, 1, 2)]) for c in range(3)]
+        turn = along_x[1] - along_y[0]
+        shear = along_x[1] + along_y[0]
+        stretch = 2.0 * (along_x[0] * along_x[0] + along_y[1] * along_y[1]) + shear * shear
+        yield i, finish(turn * turn, stretch, along_x[2], along_y[2], z)
+
+
+def interior_kernel(
+    rows, planes, fields, own_z, spin, stretch, bend_x, bend_y, near_0, near_1, left, right, out, total, pieces, to_last, to_first
+):
+    size = own_z.shape[3]
+    odd = lax.axis_index("gy") % 2 == 1
     to_last[...], to_first[...] = edge_terms(left[...], right[...])
-
-    def row_at(c, y, k, t):
-        return fields[c, y + k, pl.ds(2 + t * TILE, TILE), :]
-
-    for pair in range(rows // 2 - 2):
+    for pair in range(rows // 2 - 1):
         buffer = pieces.at[pair % 2]
-        for half in range(2):
-            index = 2 * pair + half
-            for t in range(planes // TILE):
-                results = invariants_of(fields, own_z, to_last, to_first, t, index + 2, rows, row_at)
-                store_results(results, out, index, buffer, half, t, planes, size)
+        for t in range(planes // TILE):
+            if pair < rows // 2 - 2:
+                for half in range(2):
+                    index = 2 * pair + half
+                    z = z_derivatives(own_z, to_last, to_first, t, index + 2, rows)
+                    planar = [ref[index, t * TILE : (t + 1) * TILE, :] for ref in (spin, stretch, bend_x, bend_y)]
+                    store_results(finish(*planar, z), out, index, buffer, half, t, planes, size)
+            else:
+                for half, results in beside_face(rows, planes, fields, own_z, [near_0, near_1], odd, to_last, to_first, t):
+                    store_results(results, out, 2 * pair + half, buffer, half, t, planes, size)
         for f in range(2):
             product = square(buffer[f])
             total[f] = product if pair == 0 else total[f] + product
 
 
 def border_kernel(
-    rows, planes, fields, own_z, near, far, left, right, part, velocity, out, keep, give, message, pieces, total, to_last, to_first
+    rows, planes, fields, own_z, far, left, right, part, velocity, out, keep, give, message, pieces, to_last, to_first
 ):
     size = fields.shape[3]
     odd = lax.axis_index("gy") % 2 == 1
     to_last[...], to_first[...] = edge_terms(left[...], right[...])
-
-    def row_at(c, y, k, t):
-        at = pl.ds(t * TILE, TILE)
-        if 0 <= y + k < rows:
-            return fields[c, y + k, pl.ds(2 + t * TILE, TILE), :]
-        if y + k < 0:
-            layer = y + k + 2
-            return jnp.where(odd, near[c, layer, at, :], far[c, layer, at, :])
-        layer = y + k - rows
-        return jnp.where(odd, far[c, layer, at, :], near[c, layer, at, :])
-
-    for index, y in enumerate((0, 1, rows - 2, rows - 1)):
-        half = index % 2
-        buffer = pieces.at[index // 2]
-        for t in range(planes // TILE):
-            results = invariants_of(fields, own_z, to_last, to_first, t, y, rows, row_at)
-            store_results(results, out, index, buffer, half, t, planes, size)
-        if half == 1:
-            for f in range(2):
-                product = square(buffer[f])
-                total[f] = (part[f] if index == 1 else total[f]) + product
-    grams = [gram_of(total[f]) for f in range(2)] + [velocity[c] for c in range(3)]
+    for t in range(planes // TILE):
+        for half, results in beside_face(rows, planes, fields, own_z, [far.at[:, i] for i in range(2)], ~odd, to_last, to_first, t):
+            store_results(results, out, half, pieces, half, t, planes, size)
+    grams = [gram_of(part[f] + square(pieces[f])) for f in range(2)] + [velocity[c] for c in range(3)]
     message[0:planes, :] = pack_pair(grams[0], grams[1])
     message[planes : 2 * planes, :] = pack_pair(grams[2], grams[3])
     message[2 * planes : 3 * planes, :] = grams[4]
@@ -248,16 +277,20 @@
 
 
 def assemble_kernel(rows, planes, f, inner, border, out):
-    def plane_of(y):
+    odd = lax.axis_index("gy") % 2 == 1
+
+    def plane_of(y, at):
         if 2 <= y < rows - 2:
-            return inner.at[f, y - 2]
-        return border.at[f, y if y < 2 else y - rows + 4]
+            return inner[f, y - 2, at, :]
+        layer = y % (rows - 2)
+        beside_near = odd if y < 2 else ~odd
+        return jnp.where(beside_near, inner[f, rows - 4 + layer, at, :], border[f, layer, at, :])
 
     @pl.loop(0, planes // 8)
     def _(t):
         at = pl.ds(pl.multiple_of(t * 8, 8), 8)
         for base in range(0, rows, 8):
-            block = jnp.stack([plane_of(y)[at, :] for y in range(base, base + 8)], axis=0)
+            block = jnp.stack([plane_of(y, at) for y in range(base, base + 8)], axis=0)
             out[at, base : base + 8, :] = jnp.swapaxes(block, 0, 1)
 
 
@@ -364,7 +397,7 @@
     assert count_y & (count_y - 1) == 0 and count_z & (count_z - 1) == 0
     bits = [count_z << i for i in range(1, count_y.bit_length() - 1)] + [1 << i for i in range(count_z.bit_length() - 1)]
     groups = [bits[i : i + 2] for i in range(0, len(bits), 2)]
-    return [[group[0]] if len(group) == 1 else [group[0] ^ group[1], group[0], group[1]] for group in groups]
+    return [[group[0]] if len(group) == 1 else [group[0], group[1], group[0] ^ group[1]] for group in groups]
 
 
 def add_terms(terms):
@@ -382,69 +415,76 @@
     rows, cols = fields.shape[2], fields.shape[3]
     count_y, count_z = lax.axis_size("gy"), lax.axis_size("gz")
 
-    turned, near, far, behind, ahead = pl.pallas_call(
+    far = pl.pallas_call(
+        functools.partial(far_kernel, rows, planes),
+        out_shape=f32(3, 2, planes, cols),
+        in_specs=[pl.BlockSpec(memory_space=pl.ANY)],
+        out_specs=VMEM,
+        scratch_shapes=[pltpu.SemaphoreType.DMA((2, 3))],
+        compiler_params=params(),
+        cost_estimate=cost(1),
+        name="far_face",
+    )(pltpu.with_memory_space_constraint(fields, pltpu.HBM))
+    fields, far = lax.optimization_barrier((fields, far))
+    far = lax.ppermute(far, "gy", [(i, (i + 1 if i % 2 else i - 1) % count_y) for i in range(count_y)])
+    turned, near_0, near_1, behind, ahead = pl.pallas_call(
         functools.partial(faces_kernel, rows, planes),
         out_shape=(
             pltpu.VMEM((3, rows, planes + 4, cols), jnp.float32),
-            f32(3, 2, planes, cols),
-            f32(3, 2, planes, cols),
+            f32(3, planes, cols),
+            f32(3, planes, cols),
             f32(planes, cols),
             f32(planes, cols),
         ),
-        in_specs=[pl.BlockSpec(memory_space=pl.ANY)],
-        out_specs=(VMEM, VMEM, VMEM, VMEM, VMEM),
-        scratch_shapes=[
-            pltpu.VMEM(fields.shape, jnp.float32),
-            pltpu.VMEM((planes + 4, cols), jnp.float32),
-            pltpu.VMEM((planes + 4, cols), jnp.float32),
-            pltpu.SemaphoreType.DMA((3, CHUNKS)),
-        ],
+        in_specs=[VMEM],
+        out_specs=(VMEM,) * 5,
+        scratch_shapes=[pltpu.VMEM((planes + 4, cols), jnp.float32)] * 2,
         compiler_params=params(),
-        cost_estimate=cost(5),
+        cost_estimate=cost(2.5),
         name="faces",
-    )(pltpu.with_memory_space_constraint(fields, pltpu.HBM))
-    far = lax.ppermute(far, "gy", [(i, (i + 1 if i % 2 else i - 1) % count_y) for i in range(count_y)])
-    near = lax.ppermute(near, "gy", [(i, i ^ 1) for i in range(count_y)])
+    )(pltpu.with_memory_space_constraint(fields, pltpu.VMEM))
+    near = [lax.ppermute(layer, "gy", [(i, i ^ 1) for i in range(count_y)]) for layer in (near_0, near_1)]
     left = lax.ppermute(ahead, "gz", [(i, (i + 1) % count_z) for i in range(count_z)])
     right = lax.ppermute(behind, "gz", [(i, (i - 1) % count_z) for i in range(count_z)])
 
-    velocity, own_z = pl.pallas_call(
-        functools.partial(velocity_kernel, rows, planes),
-        out_shape=(f32(3, planes, planes), pltpu.VMEM((3, rows, planes, cols), jnp.float32)),
+    inner_rows = [pltpu.VMEM((rows - 4, planes, cols), jnp.float32)] * 4
+    velocity, own_z, *planar = pl.pallas_call(
+        functools.partial(inner_kernel, rows, planes),
+        out_shape=(f32(3, planes, planes), pltpu.VMEM((3, rows, planes, cols), jnp.float32), *inner_rows),
         in_specs=[VMEM],
-        out_specs=(VMEM, VMEM),
+        out_specs=(VMEM,) * 6,
         scratch_shapes=[
             pltpu.VMEM((rows, planes, 3 * cols), jnp.bfloat16),
             pltpu.VMEM((3 * cols, cols), jnp.bfloat16),
         ],
         compiler_params=params(),
-        cost_estimate=cost(2.5),
-        name="velocity_grams",
+        cost_estimate=cost(3),
+        name="inner",
     )(turned)
     pieces = pltpu.VMEM((2, 2, 2 * planes, 2 * cols), jnp.bfloat16)
     edges = [pltpu.VMEM((planes, cols), jnp.float32)] * 2
     inner, part = pl.pallas_call(
         functools.partial(interior_kernel, rows, planes),
-        out_shape=(f32(2, rows - 4, planes, cols), f32(2, 2 * planes, 2 * planes)),
-        in_specs=[VMEM] * 4,
+        out_shape=(f32(2, rows - 2, planes, cols), f32(2, 2 * planes, 2 * planes)),
+        in_specs=[VMEM] * 10,
         out_specs=(VMEM, VMEM),
         scratch_shapes=[pieces, *edges],
         compiler_params=params(),
-        cost_estimate=cost(4),
+        cost_estimate=cost(1.9),
         name="interior",
-    )(turned, own_z, left, right)
+    )(turned, own_z, *planar, *near, left, right)
     half = 3 * planes // 2 + 8
     message = pltpu.VMEM((2 * half, planes), jnp.float32)
     border, keep, give = pl.pallas_call(
         functools.partial(border_kernel, rows, planes),
-        out_shape=(f32(2, 4, planes, cols), f32(half, planes), f32(half, planes)),
-        in_specs=[VMEM] * 8,
+        out_shape=(f32(2, 2, planes, cols), f32(half, planes), f32(half, planes)),
+        in_specs=[VMEM] * 7,
         out_specs=(VMEM, VMEM, VMEM),
-        scratch_shapes=[message, pieces, pltpu.VMEM((2, 2 * planes, 2 * planes), jnp.float32), *edges],
+        scratch_shapes=[message, pltpu.VMEM((2, 2 * planes, 2 * cols), jnp.bfloat16), *edges],
         compiler_params=params(),
-        cost_estimate=cost(1),
+        cost_estimate=cost(0.7),
         name="border",
-    )(turned, own_z, near, far, left, right, part, velocity)
+    )(turned, own_z, far, left, right, part, velocity)
     enstrophy, strain_rate = [
         pl.pallas_call(
             functools.partial(assemble_kernel, rows, planes, f),

time: 43.4 us -> 40.7 us (0.938)
  waiting for transfers between devices: 10.8 us -> 8.08 us
    ppermute x8, waiting for transfers between devices: 10.8 us -> 8.06 us  [exchange(): lax.ppermute(values, AXES, [(i, i ^ (odd if i // count_z % 2 else even))...]
    pallas_call x1 -> x2, Pallas kernels: 2.6 us -> 4.38 us  [the longest x1 3.12 us: per_device(): pl.pallas_call(functools.partial(inner_kernel, rows, planes), out_shape=(...]
    pallas_call x1, Pallas kernels: 2.49 us -> 1.55 us  [per_device(): pl.pallas_call(functools.partial(faces_kernel, rows, planes), out_shape=(...]
    pallas_call x1, Pallas kernels: 2.52 us -> 2 us  [per_device(): pl.pallas_call(functools.partial(interior_kernel, rows, planes), out_shap...]
  transfers between devices with their start and end apart: 12 -> 13, of which waited for: 7 -> 6; matrix products, arithmetic and copies ran while one was open for 0% -> 0% of each run, Pallas kernels for 18% -> 23%
where the time goes in v6:
time: 40.7 us; the launch traced here: 40.6 us
  starting transfers between devices  16.2 us (40%)
  Pallas kernels  15.5 us (38%)
  waiting for transfers between devices  8.08 us (20%)
  between operations  0.73 us (2%)
    ppermute x8, starting transfers between devices, exchange(): lax.ppermute(values, AXES, [(i, i ^ (odd if i // count_z % 2 else even))...  8.14 us
    ppermute x8, waiting for transfers between devices, exchange(): lax.ppermute(values, AXES, [(i, i ^ (odd if i // count_z % 2 else even))...  8.06 us
    pallas_call x1, Pallas kernels, per_device(): pl.pallas_call(functools.partial(factor_kernel, float(cells), planes), ou...  4.25 us
    ppermute x1, starting transfers between devices, per_device(): lax.ppermute(behind, 'gz', [(i, (i - 1) % count_z) for i in range(count_z)])  3.23 us
    pallas_call x1, Pallas kernels, per_device(): pl.pallas_call(functools.partial(inner_kernel, rows, planes), out_shape=(...  3.12 us
    pallas_call x2, Pallas kernels, per_device(): pl.pallas_call(functools.partial(assemble_kernel, rows, planes, f), out_s...  2.55 us
    ppermute x1, starting transfers between devices, per_device(): lax.ppermute(far, 'gy', [(i, (i + 1 if i % 2 else i - 1) % count_y) for i...  2.47 us
    pallas_call x1, Pallas kernels, per_device(): pl.pallas_call(functools.partial(interior_kernel, rows, planes), out_shap...  2 us
  transfers between devices with their start and end apart: 13, of which 6 were waited for; matrix products, arithmetic and copies ran while one was open for 0% of the time, Pallas kernels for 23%

profile of v6, /device:TPU:0, one launch (start us, length us, event | category | flops | bytes accessed | tf_op | source)
XLA Modules:
  0.0 40.6 jit_solution(9550912931059246787)
XLA Ops:
  0.6 1.3 %far_face.1 = f32[3,2,128,128]{3,2,1,0:T(8,128)S(1)} custom-call(f32[3,132,16,128]{3,2,1,0:T(8,128)} %fields.2), custom_call_target="tpu_custom_call" | custom-call | bytes 3690000 | tf_op jit(solution)/shard_map/far_face/pallas_call | solution.py:418
  1.9 2.5 %collective-permute-start = (f32[3,2,128,128]{3,2,1,0:T(8,128)S(1)}, f32[3,2,128,128]{3,2,1,0:T(8,128)S(1)}, u32[]{:S(2)}, u32[]{:S(2)}) collective-permute-start(f32[3,2,128,128]{3,2,1,0:T(8,128)S(1)} %far_face.1), channel_id=1, source_target_pairs={{0,24},{8,16},{16,8},{24,0},{1,25},{9,17},{17,9},{25,1},{2,26},{10... | collective-permute-start | bytes 1179656 | tf_op jit(solution)/shard_map/ppermute | solution.py:429
  4.4 1.6 %faces.1 = (f32[3,16,132,128]{3,2,1,0:T(8,128)S(1)}, f32[3,128,128]{2,1,0:T(8,128)S(1)}, f32[3,128,128]{2,1,0:T(8,128)S(1)}, f32[128,128]{1,0:T(8,128)S(1)}, f32[128,128]{1,0:T(8,128)S(1)}) custom-call(f32[3,132,16,128]{3,2,1,0:T(8,128)S(1)} %copy-done), custom_call_target="tpu_custom_call" | custom-call | bytes 9225000 | tf_op jit(solution)/shard_map/faces/pallas_call | solution.py:430
  5.9 0.7 %collective-permute-start.3 = (f32[3,128,128]{2,1,0:T(8,128)S(1)}, f32[3,128,128]{2,1,0:T(8,128)S(1)}, u32[]{:S(2)}, u32[]{:S(2)}) collective-permute-start(f32[3,128,128]{2,1,0:T(8,128)S(1)} %get-tuple-element.34), channel_id=1, source_target_pairs={{0,8},{8,0},{16,24},{24,16},{1,9},{9,1},{17,25},{25,17},{2,10},{10... | collective-permute-start | bytes 589832 | tf_op jit(solution)/shard_map/ppermute | solution.py:446
  6.7 0.1 collective-permute-start.4
  6.7 1.5 %collective-permute-start.1 = (f32[128,128]{1,0:T(8,128)S(1)}, f32[128,128]{1,0:T(8,128)S(1)}, u32[]{:S(2)}, u32[]{:S(2)}) collective-permute-start(f32[128,128]{1,0:T(8,128)S(1)} %get-tuple-element.28), channel_id=1, source_target_pairs={{0,1},{1,2},{2,3},{3,4},{4,5},{5,6},{6,7},{7,0},{8,9},{9,10},{10,1... | collective-permute-start | bytes 196616 | tf_op jit(solution)/shard_map/ppermute | solution.py:447
  8.2 3.2 %collective-permute-start.2 = (f32[128,128]{1,0:T(8,128)S(1)}, f32[128,128]{1,0:T(8,128)S(1)}, u32[]{:S(2)}, u32[]{:S(2)}) collective-permute-start(f32[128,128]{1,0:T(8,128)S(1)} %get-tuple-element.29), channel_id=1, source_target_pairs={{0,7},{1,0},{2,1},{3,2},{4,3},{5,4},{6,5},{7,6},{8,15},{9,8},{10,9... | collective-permute-start | bytes 196616 | tf_op jit(solution)/shard_map/ppermute | solution.py:448
  11.5 3.1 %inner.1 = (f32[3,128,128]{2,1,0:T(8,128)S(1)}, f32[3,16,128,128]{3,2,1,0:T(8,128)S(1)}, f32[12,128,128]{2,1,0:T(8,128)S(1)}, f32[12,128,128]{2,1,0:T(8,128)S(1)...) custom-call(f32[3,16,132,128]{3,2,1,0:T(8,128)S(1)} %get-tuple-element.25.fields), custom_call_target="tpu_custom_call" | custom-call | bytes 11070000 | tf_op jit(solution)/shard_map/inner/pallas_call | solution.py:451
  14.6 2.0 %interior.1 = (f32[2,14,128,128]{3,2,1,0:T(8,128)S(1)}, f32[2,256,256]{2,1,0:T(8,128)S(1)}) custom-call(f32[3,16,132,128]{3,2,1,0:T(8,128)S(1)} %get-tuple-element.25.fields, f32[3,16,128,128]{3,2,1,0:T(8,128)S(1)} %get-tuple-element.26.own_z, f32[12,128,128]{2,1,0:T(8,128)S(1)} %get-tuple-element.30.spin, f32[12,128,128]{2,1,0:T(8,128)S(1)} %get-tuple-element.31.stretch, ...), custom_call_target="tpu_custom_call" | custom-call | bytes 7011000 | tf_op jit(solution)/shard_map/interior/pallas_call | solution.py:466
  16.7 0.8 %border.1 = (f32[2,2,128,128]{3,2,1,0:T(8,128)S(1)}, f32[200,128]{1,0:T(8,128)S(1)}, f32[200,128]{1,0:T(8,128)S(1)}) custom-call(f32[3,16,132,128]{3,2,1,0:T(8,128)S(1)} %get-tuple-element.25.fields, f32[3,16,128,128]{3,2,1,0:T(8,128)S(1)} %get-tuple-element.26.own_z, f32[3,2,128,128]{3,2,1,0:T(8,128)S(1)} %collective-permute-done.far, ...), custom_call_target="tpu_custom_call" | custom-call | bytes 2583000 | tf_op jit(solution)/shard_map/border/pallas_call | solution.py:478
  17.5 1.3 %collective-permute-done.5 = f32[200,128]{1,0:T(8,128)S(1)} collective-permute-done((f32[200,128]{1,0:T(8,128)S(1)}, f32[200,128]{1,0:T(8,128)S(1)}, u32[]{:S(2)}, u32[]{:S(2)}) %collective-permute-start.5) | collective-permute-done | bytes 102432 | tf_op jit(solution)/shard_map/ppermute | solution.py:392
  18.8 1.0 %collective-permute-start.8 = (f32[200,128]{1,0:T(8,128)S(1)}, f32[200,128]{1,0:T(8,128)S(1)}, u32[]{:S(2)}, u32[]{:S(2)}) collective-permute-start(f32[200,128]{1,0:T(8,128)S(1)} %add.21), channel_id=1, source_target_pairs={{0,17},{1,16},{2,19},{3,18},{4,21},{5,20},{6,23},{7,22},{8,14},{9,... | collective-permute-start | bytes 307208 | tf_op jit(solution)/shard_map/ppermute | solution.py:392
  19.8 1.7 %collective-permute-start.7 = (f32[200,128]{1,0:T(8,128)S(1)}, f32[200,128]{1,0:T(8,128)S(1)}, u32[]{:S(2)}, u32[]{:S(2)}) collective-permute-start(f32[200,128]{1,0:T(8,128)S(1)} %add.21), channel_id=1, source_target_pairs={{0,1},{1,0},{2,3},{3,2},{4,5},{5,4},{6,7},{7,6},{8,12},{9,13},{10,... | collective-permute-start | bytes 307208 | tf_op jit(solution)/shard_map/ppermute | solution.py:392
  21.5 0.9 %collective-permute-start.6 = (f32[200,128]{1,0:T(8,128)S(1)}, f32[200,128]{1,0:T(8,128)S(1)}, u32[]{:S(2)}, u32[]{:S(2)}) collective-permute-start(f32[200,128]{1,0:T(8,128)S(1)} %add.21), channel_id=1, source_target_pairs={{0,16},{1,17},{2,18},{3,19},{4,20},{5,21},{6,22},{7,23},{8,10},{9,... | collective-permute-start | bytes 307208 | tf_op jit(solution)/shard_map/ppermute | solution.py:392
  22.4 2.1 %collective-permute-done.8 = f32[200,128]{1,0:T(8,128)S(1)} collective-permute-done((f32[200,128]{1,0:T(8,128)S(1)}, f32[200,128]{1,0:T(8,128)S(1)}, u32[]{:S(2)}, u32[]{:S(2)}) %collective-permute-start.8) | collective-permute-done | bytes 102432 | tf_op jit(solution)/shard_map/ppermute | solution.py:392
  24.5 0.8 %collective-permute-done.7 = f32[200,128]{1,0:T(8,128)S(1)} collective-permute-done((f32[200,128]{1,0:T(8,128)S(1)}, f32[200,128]{1,0:T(8,128)S(1)}, u32[]{:S(2)}, u32[]{:S(2)}) %collective-permute-start.7) | collective-permute-done | bytes 102432 | tf_op jit(solution)/shard_map/ppermute | solution.py:392
  25.2 0.9 %collective-permute-done.6 = f32[200,128]{1,0:T(8,128)S(1)} collective-permute-done((f32[200,128]{1,0:T(8,128)S(1)}, f32[200,128]{1,0:T(8,128)S(1)}, u32[]{:S(2)}, u32[]{:S(2)}) %collective-permute-start.6) | collective-permute-done | bytes 102432 | tf_op jit(solution)/shard_map/ppermute | solution.py:392
  26.2 2.4 %collective-permute-start.11 = (f32[200,128]{1,0:T(8,128)S(1)}, f32[200,128]{1,0:T(8,128)S(1)}, u32[]{:S(2)}, u32[]{:S(2)}) collective-permute-start(f32[200,128]{1,0:T(8,128)S(1)} %add_add_fusion.1), channel_id=1, source_target_pairs={{0,6},{1,7},{2,4},{3,5},{4,2},{5,3},{6,0},{7,1},{8,25},{9,24},{10,... | collective-permute-start | bytes 307208 | tf_op jit(solution)/shard_map/ppermute | solution.py:392
  28.6 2.0 %collective-permute-start.9 = (f32[200,128]{1,0:T(8,128)S(1)}, f32[200,128]{1,0:T(8,128)S(1)}, u32[]{:S(2)}, u32[]{:S(2)}) collective-permute-start(f32[200,128]{1,0:T(8,128)S(1)} %add_add_fusion.1), channel_id=1, source_target_pairs={{0,2},{1,3},{2,0},{3,1},{4,6},{5,7},{6,4},{7,5},{8,24},{9,25},{10,... | collective-permute-start | bytes 307208 | tf_op jit(solution)/shard_map/ppermute | solution.py:392
  30.6 1.3 %assemble.3 = f32[128,16,128]{2,1,0:T(8,128)} custom-call(f32[2,14,128,128]{3,2,1,0:T(8,128)S(1)} %get-tuple-element.40.inner, f32[2,2,128,128]{3,2,1,0:T(8,128)S(1)} %get-tuple-element.41.border), custom_call_target="tpu_custom_call" | custom-call | bytes 3690000 | tf_op jit(solution)/shard_map/assemble/pallas_call | solution.py:489
  31.9 1.3 %assemble.2 = f32[128,16,128]{2,1,0:T(8,128)} custom-call(f32[2,14,128,128]{3,2,1,0:T(8,128)S(1)} %get-tuple-element.40.inner, f32[2,2,128,128]{3,2,1,0:T(8,128)S(1)} %get-tuple-element.41.border), custom_call_target="tpu_custom_call" | custom-call | bytes 3690000 | tf_op jit(solution)/shard_map/assemble/pallas_call | solution.py:489
  33.2 1.7 %collective-permute-done.10 = f32[200,128]{1,0:T(8,128)S(1)} collective-permute-done((f32[200,128]{1,0:T(8,128)S(1)}, f32[200,128]{1,0:T(8,128)S(1)}, u32[]{:S(2)}, u32[]{:S(2)}) %collective-permute-start.10) | collective-permute-done | bytes 102432 | tf_op jit(solution)/shard_map/ppermute | solution.py:392
  35.0 1.3 %collective-permute-done.12.given = f32[200,128]{1,0:T(8,128)S(1)} collective-permute-done((f32[200,128]{1,0:T(8,128)S(1)}, f32[200,128]{1,0:T(8,128)S(1)}, u32[]{:S(2)}, u32[]{:S(2)}) %collective-permute-start.12) | collective-permute-done | bytes 102432 | tf_op jit(solution)/shard_map/ppermute | solution.py:392
  36.3 4.2 %factor.1 = f32[128,128]{1,0:T(8,128)} custom-call(f32[200,128]{1,0:T(8,128)S(1)} %add_add_fusion.kept, f32[200,128]{1,0:T(8,128)S(1)} %collective-permute-done.12.given), custom_call_target="tpu_custom_call" | custom-call | bytes 22140000 | tf_op jit(solution)/shard_map/factor/pallas_call | solution.py:508
  (15 shorter events, 0.2 us)
Async XLA Ops:
  0.6 3.7 %copy-start = (f32[3,132,16,128]{3,2,1,0:T(8,128)S(1)}, f32[3,132,16,128]{3,2,1,0:T(8,128)}, u32[]{:S(2)}) copy-start(f32[3,132,16,128]{3,2,1,0:T(8,128)} %fields.2) | copy-start | bytes 9732100
  1.9 14.7 %collective-permute-start = (f32[3,2,128,128]{3,2,1,0:T(8,128)S(1)}, f32[3,2,128,128]{3,2,1,0:T(8,128)S(1)}, u32[]{:S(2)}, u32[]{:S(2)}) collective-permute-start(f32[3,2,128,128]{3,2,1,0:T(8,128)S(1)} %far_face.1), channel_id=1, source_target_pairs={{0,24},{8,16},{16,8},{24,0},{1,25},{9,17},{17,9},{25,1},{2,26},{10... | collective-permute-start | bytes 1179656 | tf_op jit(solution)/shard_map/ppermute | solution.py:429
  5.9 8.7 %collective-permute-start.3 = (f32[3,128,128]{2,1,0:T(8,128)S(1)}, f32[3,128,128]{2,1,0:T(8,128)S(1)}, u32[]{:S(2)}, u32[]{:S(2)}) collective-permute-start(f32[3,128,128]{2,1,0:T(8,128)S(1)} %get-tuple-element.34), channel_id=1, source_target_pairs={{0,8},{8,0},{16,24},{24,16},{1,9},{9,1},{17,25},{25,17},{2,10},{10... | collective-permute-start | bytes 589832 | tf_op jit(solution)/shard_map/ppermute | solution.py:446
  6.7 8.0 %collective-permute-start.4 = (f32[3,128,128]{2,1,0:T(8,128)S(1)}, f32[3,128,128]{2,1,0:T(8,128)S(1)}, u32[]{:S(2)}, u32[]{:S(2)}) collective-permute-start(f32[3,128,128]{2,1,0:T(8,128)S(1)} %get-tuple-element.35), channel_id=1, source_target_pairs={{0,8},{8,0},{16,24},{24,16},{1,9},{9,1},{17,25},{25,17},{2,10},{10... | collective-permute-start | bytes 589832 | tf_op jit(solution)/shard_map/ppermute | solution.py:446
  6.7 7.9 %collective-permute-start.1 = (f32[128,128]{1,0:T(8,128)S(1)}, f32[128,128]{1,0:T(8,128)S(1)}, u32[]{:S(2)}, u32[]{:S(2)}) collective-permute-start(f32[128,128]{1,0:T(8,128)S(1)} %get-tuple-element.28), channel_id=1, source_target_pairs={{0,1},{1,2},{2,3},{3,4},{4,5},{5,6},{6,7},{7,0},{8,9},{9,10},{10,1... | collective-permute-start | bytes 196616 | tf_op jit(solution)/shard_map/ppermute | solution.py:447
  8.2 6.4 %collective-permute-start.2 = (f32[128,128]{1,0:T(8,128)S(1)}, f32[128,128]{1,0:T(8,128)S(1)}, u32[]{:S(2)}, u32[]{:S(2)}) collective-permute-start(f32[128,128]{1,0:T(8,128)S(1)} %get-tuple-element.29), channel_id=1, source_target_pairs={{0,7},{1,0},{2,1},{3,2},{4,3},{5,4},{6,5},{7,6},{8,15},{9,8},{10,9... | collective-permute-start | bytes 196616 | tf_op jit(solution)/shard_map/ppermute | solution.py:448
  17.5 1.4 %collective-permute-start.5 = (f32[200,128]{1,0:T(8,128)S(1)}, f32[200,128]{1,0:T(8,128)S(1)}, u32[]{:S(2)}, u32[]{:S(2)}) collective-permute-start(f32[200,128]{1,0:T(8,128)S(1)} %get-tuple-element.39), channel_id=1, source_target_pairs={{0,8},{1,9},{2,10},{3,11},{4,12},{5,13},{6,14},{7,15},{8,0},{9,1},... | collective-permute-start | bytes 307208 | tf_op jit(solution)/shard_map/ppermute | solution.py:392
  18.8 5.6 %collective-permute-start.8 = (f32[200,128]{1,0:T(8,128)S(1)}, f32[200,128]{1,0:T(8,128)S(1)}, u32[]{:S(2)}, u32[]{:S(2)}) collective-permute-start(f32[200,128]{1,0:T(8,128)S(1)} %add.21), channel_id=1, source_target_pairs={{0,17},{1,16},{2,19},{3,18},{4,21},{5,20},{6,23},{7,22},{8,14},{9,... | collective-permute-start | bytes 307208 | tf_op jit(solution)/shard_map/ppermute | solution.py:392
  19.8 5.4 %collective-permute-start.7 = (f32[200,128]{1,0:T(8,128)S(1)}, f32[200,128]{1,0:T(8,128)S(1)}, u32[]{:S(2)}, u32[]{:S(2)}) collective-permute-start(f32[200,128]{1,0:T(8,128)S(1)} %add.21), channel_id=1, source_target_pairs={{0,1},{1,0},{2,3},{3,2},{4,5},{5,4},{6,7},{7,6},{8,12},{9,13},{10,... | collective-permute-start | bytes 307208 | tf_op jit(solution)/shard_map/ppermute | solution.py:392
  21.5 4.7 %collective-permute-start.6 = (f32[200,128]{1,0:T(8,128)S(1)}, f32[200,128]{1,0:T(8,128)S(1)}, u32[]{:S(2)}, u32[]{:S(2)}) collective-permute-start(f32[200,128]{1,0:T(8,128)S(1)} %add.21), channel_id=1, source_target_pairs={{0,16},{1,17},{2,18},{3,19},{4,20},{5,21},{6,22},{7,23},{8,10},{9,... | collective-permute-start | bytes 307208 | tf_op jit(solution)/shard_map/ppermute | solution.py:392
  26.2 7.0 %collective-permute-start.11 = (f32[200,128]{1,0:T(8,128)S(1)}, f32[200,128]{1,0:T(8,128)S(1)}, u32[]{:S(2)}, u32[]{:S(2)}) collective-permute-start(f32[200,128]{1,0:T(8,128)S(1)} %add_add_fusion.1), channel_id=1, source_target_pairs={{0,6},{1,7},{2,4},{3,5},{4,2},{5,3},{6,0},{7,1},{8,25},{9,24},{10,... | collective-permute-start | bytes 307208 | tf_op jit(solution)/shard_map/ppermute | solution.py:392
  28.6 6.3 %collective-permute-start.10 = (f32[200,128]{1,0:T(8,128)S(1)}, f32[200,128]{1,0:T(8,128)S(1)}, u32[]{:S(2)}, u32[]{:S(2)}) collective-permute-start(f32[200,128]{1,0:T(8,128)S(1)} %add_add_fusion.1), channel_id=1, source_target_pairs={{0,4},{1,5},{2,6},{3,7},{4,0},{5,1},{6,2},{7,3},{8,9},{9,8},{10,11... | collective-permute-start | bytes 307208 | tf_op jit(solution)/shard_map/ppermute | solution.py:392
  28.6 6.3 %collective-permute-start.9 = (f32[200,128]{1,0:T(8,128)S(1)}, f32[200,128]{1,0:T(8,128)S(1)}, u32[]{:S(2)}, u32[]{:S(2)}) collective-permute-start(f32[200,128]{1,0:T(8,128)S(1)} %add_add_fusion.1), channel_id=1, source_target_pairs={{0,2},{1,3},{2,0},{3,1},{4,6},{5,7},{6,4},{7,5},{8,24},{9,25},{10,... | collective-permute-start | bytes 307208 | tf_op jit(solution)/shard_map/ppermute | solution.py:392
  34.9 1.4 %collective-permute-start.12 = (f32[200,128]{1,0:T(8,128)S(1)}, f32[200,128]{1,0:T(8,128)S(1)}, u32[]{:S(2)}, u32[]{:S(2)}) collective-permute-start(f32[200,128]{1,0:T(8,128)S(1)} %add_add_fusion.kept), channel_id=1, source_target_pairs={{0,8},{1,9},{2,10},{3,11},{4,12},{5,13},{6,14},{7,15},{8,0},{9,1},... | collective-permute-start | bytes 307208 | tf_op jit(solution)/shard_map/ppermute | solution.py:392

commit v7 on v6

--- a/solution.py
+++ b/solution.py
@@ -45,6 +45,27 @@
 def pack_pair(first, second):
     row, col = halves(first.shape[0])
     return jnp.where(row >= col, first, second)
+
+
+def fold(matrix):
+    half = matrix.shape[0] // 2
+    row = lax.broadcasted_iota(jnp.int32, (half, 2 * half), 0)
+    col = lax.broadcasted_iota(jnp.int32, (half, 2 * half), 1)
+    first = pltpu.roll(matrix[:half, :], half, 1)
+    last = matrix[half:, :]
+    return jnp.where((col >= half) & (row >= col - half), first, last)
+
+
+def unfold(folded, last_diagonal):
+    half = folded.shape[0]
+    row = lax.broadcasted_iota(jnp.int32, folded.shape, 0)
+    col = lax.broadcasted_iota(jnp.int32, folded.shape, 1)
+    first = pltpu.roll(folded, half, 1)
+    off_first = jnp.where(row > col, first, 0.0)
+    off_last = jnp.where((col < half) | (col - half > row), folded, 0.0)
+    on_first = jnp.where(row == col, first, 0.0)
+    on_last = jnp.where(row == col - half, last_diagonal, 0.0)
+    return jnp.concatenate([off_first, off_last], axis=0), jnp.concatenate([on_first, on_last], axis=0)
 
 
 def half_starts(length):
@@ -268,9 +289,11 @@
     grams = [gram_of(part[f] + square(pieces[f])) for f in range(2)] + [velocity[c] for c in range(3)]
     message[0:planes, :] = pack_pair(grams[0], grams[1])
     message[planes : 2 * planes, :] = pack_pair(grams[2], grams[3])
-    message[2 * planes : 3 * planes, :] = grams[4]
-    message[3 * planes : 3 * planes + 8, :] = jnp.broadcast_to(diagonal(grams[1]), (8, planes))
-    message[3 * planes + 8 : 3 * planes + 16, :] = jnp.broadcast_to(diagonal(grams[3]), (8, planes))
+    message[2 * planes : 5 * planes // 2, :] = fold(grams[4])
+    for i, f in enumerate((1, 3, 4)):
+        message[5 * planes // 2 + i : 5 * planes // 2 + i + 1, :] = diagonal(grams[f])
+    used = 5 * planes // 2 + 3
+    message[used:, :] = jnp.zeros((message.shape[0] - used, planes), jnp.float32)
     mine, other = half_starts(keep.shape[0])
     keep[...] = message[pl.ds(mine, keep.shape[0]), :]
     give[...] = message[pl.ds(other, keep.shape[0]), :]
@@ -367,12 +390,13 @@
         both = jnp.where(eye, packed * first_scale + second_diagonal * second_scale, 0.0)
         return lower, both
 
-    low_a, both_a = unpack(message[0:planes, :], message[3 * planes : 3 * planes + 1, :])
-    low_b, both_b = unpack(message[planes : 2 * planes, :], message[3 * planes + 8 : 3 * planes + 9, :])
-    third = message[2 * planes : 3 * planes, :]
-    third = third * scale(jnp.sum(jnp.where(eye, third, 0.0)))
-    triangles = low_a + low_b
-    cross = triangles + triangles.T + (both_a + both_b) + third
+    diagonals = [message[5 * planes // 2 + i : 5 * planes // 2 + i + 1, :] for i in range(3)]
+    low_a, both_a = unpack(message[0:planes, :], diagonals[0])
+    low_b, both_b = unpack(message[planes : 2 * planes, :], diagonals[1])
+    low_c, both_c = unfold(message[2 * planes : 5 * planes // 2, :], diagonals[2])
+    third = scale(jnp.sum(both_c))
+    triangles = low_a + low_b + low_c * third
+    cross = triangles + triangles.T + (both_a + both_b + both_c * third)
     wide = 16 if planes % 32 == 0 else 8
     widths = [8] * (planes // 16) + [wide] * (planes // 2 // wide)
     upper = factor_tiles([cross[t : t + 8, :] for t in range(0, planes, 8)], widths)
@@ -473,7 +497,7 @@
         cost_estimate=cost(1.9),
         name="interior",
     )(turned, own_z, *planar, *near, left, right)
-    half = 3 * planes // 2 + 8
+    half = -(-(5 * planes // 2 + 3) // 16) * 8
     message = pltpu.VMEM((2 * half, planes), jnp.float32)
     border, keep, give = pl.pallas_call(
         functools.partial(border_kernel, rows, planes),
@@ -500,9 +524,12 @@
     core = count_z
     kept = keep + exchange(give, core, core)
     masks = rounds()
-    for even, odd in zip(masks, masks[::-1]):
+    outputs = [enstrophy, strain_rate]
+    for i, (even, odd) in enumerate(zip(masks, masks[::-1])):
         kept = add_terms([kept] + [exchange(kept, *pair) for pair in zip(even, odd)])
-    kept, enstrophy, strain_rate = lax.optimization_barrier((kept, enstrophy, strain_rate))
+        if i < len(outputs):
+            kept, outputs[i] = lax.optimization_barrier((kept, outputs[i]))
+    enstrophy, strain_rate = outputs
     given = exchange(kept, core, core)
     cells = rows * cols * count_y * count_z
     factor = pl.pallas_call(

time: 40.7 us -> 40 us (0.983)
  waiting for transfers between devices: 8.08 us -> 7.33 us
    ppermute x8, waiting for transfers between devices: 8.06 us -> 7.31 us  [exchange(): lax.ppermute(values, AXES, [(i, i ^ (odd if i // count_z % 2 else even))...]
  transfers between devices with their start and end apart: 13 -> 13, of which waited for: 6 -> 7; matrix products, arithmetic and copies ran while one was open for 0% -> 0% of each run, Pallas kernels for 23% -> 23%
where the time goes in v7:
time: 40 us; the launch traced here: 39.8 us
  starting transfers between devices  16.2 us (40%)
  Pallas kernels  15.6 us (39%)
  waiting for transfers between devices  7.33 us (18%)
  between operations  0.73 us (2%)
    ppermute x8, starting transfers between devices, exchange(): lax.ppermute(values, AXES, [(i, i ^ (odd if i // count_z % 2 else even))...  8.14 us
    ppermute x8, waiting for transfers between devices, exchange(): lax.ppermute(values, AXES, [(i, i ^ (odd if i // count_z % 2 else even))...  7.31 us
    pallas_call x1, Pallas kernels, per_device(): pl.pallas_call(functools.partial(factor_kernel, float(cells), planes), ou...  4.29 us
    ppermute x1, starting transfers between devices, per_device(): lax.ppermute(behind, 'gz', [(i, (i - 1) % count_z) for i in range(count_z)])  3.23 us
    pallas_call x1, Pallas kernels, per_device(): pl.pallas_call(functools.partial(inner_kernel, rows, planes), out_shape=(...  3.12 us
    pallas_call x2, Pallas kernels, per_device(): pl.pallas_call(functools.partial(assemble_kernel, rows, planes, f), out_s...  2.55 us
    ppermute x1, starting transfers between devices, per_device(): lax.ppermute(far, 'gy', [(i, (i + 1 if i % 2 else i - 1) % count_y) for i...  2.47 us
    pallas_call x1, Pallas kernels, per_device(): pl.pallas_call(functools.partial(interior_kernel, rows, planes), out_shap...  2 us
  transfers between devices with their start and end apart: 13, of which 7 were waited for; matrix products, arithmetic and copies ran while one was open for 0% of the time, Pallas kernels for 23%

profile of v7, /device:TPU:0, one launch (start us, length us, event | category | flops | bytes accessed | tf_op | source)
XLA Modules:
  0.0 39.8 jit_solution(5091097184541098692)
XLA Ops:
  0.6 1.3 %far_face.1 = f32[3,2,128,128]{3,2,1,0:T(8,128)S(1)} custom-call(f32[3,132,16,128]{3,2,1,0:T(8,128)} %fields.2), custom_call_target="tpu_custom_call" | custom-call | bytes 3690000 | tf_op jit(solution)/shard_map/far_face/pallas_call | solution.py:442
  1.9 2.5 %collective-permute-start = (f32[3,2,128,128]{3,2,1,0:T(8,128)S(1)}, f32[3,2,128,128]{3,2,1,0:T(8,128)S(1)}, u32[]{:S(2)}, u32[]{:S(2)}) collective-permute-start(f32[3,2,128,128]{3,2,1,0:T(8,128)S(1)} %far_face.1), channel_id=1, source_target_pairs={{0,24},{8,16},{16,8},{24,0},{1,25},{9,17},{17,9},{25,1},{2,26},{10... | collective-permute-start | bytes 1179656 | tf_op jit(solution)/shard_map/ppermute | solution.py:453
  4.4 1.6 %faces.1 = (f32[3,16,132,128]{3,2,1,0:T(8,128)S(1)}, f32[3,128,128]{2,1,0:T(8,128)S(1)}, f32[3,128,128]{2,1,0:T(8,128)S(1)}, f32[128,128]{1,0:T(8,128)S(1)}, f32[128,128]{1,0:T(8,128)S(1)}) custom-call(f32[3,132,16,128]{3,2,1,0:T(8,128)S(1)} %copy-done), custom_call_target="tpu_custom_call" | custom-call | bytes 9225000 | tf_op jit(solution)/shard_map/faces/pallas_call | solution.py:454
  5.9 0.7 %collective-permute-start.3 = (f32[3,128,128]{2,1,0:T(8,128)S(1)}, f32[3,128,128]{2,1,0:T(8,128)S(1)}, u32[]{:S(2)}, u32[]{:S(2)}) collective-permute-start(f32[3,128,128]{2,1,0:T(8,128)S(1)} %get-tuple-element.35), channel_id=1, source_target_pairs={{0,8},{8,0},{16,24},{24,16},{1,9},{9,1},{17,25},{25,17},{2,10},{10... | collective-permute-start | bytes 589832 | tf_op jit(solution)/shard_map/ppermute | solution.py:470
  6.7 1.5 %collective-permute-start.1 = (f32[128,128]{1,0:T(8,128)S(1)}, f32[128,128]{1,0:T(8,128)S(1)}, u32[]{:S(2)}, u32[]{:S(2)}) collective-permute-start(f32[128,128]{1,0:T(8,128)S(1)} %get-tuple-element.29), channel_id=1, source_target_pairs={{0,1},{1,2},{2,3},{3,4},{4,5},{5,6},{6,7},{7,0},{8,9},{9,10},{10,1... | collective-permute-start | bytes 196616 | tf_op jit(solution)/shard_map/ppermute | solution.py:471
  8.2 3.2 %collective-permute-start.2 = (f32[128,128]{1,0:T(8,128)S(1)}, f32[128,128]{1,0:T(8,128)S(1)}, u32[]{:S(2)}, u32[]{:S(2)}) collective-permute-start(f32[128,128]{1,0:T(8,128)S(1)} %get-tuple-element.30), channel_id=1, source_target_pairs={{0,7},{1,0},{2,1},{3,2},{4,3},{5,4},{6,5},{7,6},{8,15},{9,8},{10,9... | collective-permute-start | bytes 196616 | tf_op jit(solution)/shard_map/ppermute | solution.py:472
  11.5 3.1 %inner.1 = (f32[3,128,128]{2,1,0:T(8,128)S(1)}, f32[3,16,128,128]{3,2,1,0:T(8,128)S(1)}, f32[12,128,128]{2,1,0:T(8,128)S(1)}, f32[12,128,128]{2,1,0:T(8,128)S(1)...) custom-call(f32[3,16,132,128]{3,2,1,0:T(8,128)S(1)} %get-tuple-element.26.fields), custom_call_target="tpu_custom_call" | custom-call | bytes 11070000 | tf_op jit(solution)/shard_map/inner/pallas_call | solution.py:475
  14.6 2.0 %interior.1 = (f32[2,14,128,128]{3,2,1,0:T(8,128)S(1)}, f32[2,256,256]{2,1,0:T(8,128)S(1)}) custom-call(f32[3,16,132,128]{3,2,1,0:T(8,128)S(1)} %get-tuple-element.26.fields, f32[3,16,128,128]{3,2,1,0:T(8,128)S(1)} %get-tuple-element.27.own_z, f32[12,128,128]{2,1,0:T(8,128)S(1)} %get-tuple-element.31.spin, f32[12,128,128]{2,1,0:T(8,128)S(1)} %get-tuple-element.32.stretch, ...), custom_call_target="tpu_custom_call" | custom-call | bytes 7011000 | tf_op jit(solution)/shard_map/interior/pallas_call | solution.py:490
  16.7 0.8 %border.1 = (f32[2,2,128,128]{3,2,1,0:T(8,128)S(1)}, f32[168,128]{1,0:T(8,128)S(1)}, f32[168,128]{1,0:T(8,128)S(1)}) custom-call(f32[3,16,132,128]{3,2,1,0:T(8,128)S(1)} %get-tuple-element.26.fields, f32[3,16,128,128]{3,2,1,0:T(8,128)S(1)} %get-tuple-element.27.own_z, f32[3,2,128,128]{3,2,1,0:T(8,128)S(1)} %collective-permute-done.far, ...), custom_call_target="tpu_custom_call" | custom-call | bytes 2583000 | tf_op jit(solution)/shard_map/border/pallas_call | solution.py:502
  17.5 1.3 %collective-permute-done.5 = f32[168,128]{1,0:T(8,128)S(1)} collective-permute-done((f32[168,128]{1,0:T(8,128)S(1)}, f32[168,128]{1,0:T(8,128)S(1)}, u32[]{:S(2)}, u32[]{:S(2)}) %collective-permute-start.5) | collective-permute-done | bytes 86048 | tf_op jit(solution)/shard_map/ppermute | solution.py:416
  18.8 0.9 %collective-permute-start.8 = (f32[168,128]{1,0:T(8,128)S(1)}, f32[168,128]{1,0:T(8,128)S(1)}, u32[]{:S(2)}, u32[]{:S(2)}) collective-permute-start(f32[168,128]{1,0:T(8,128)S(1)} %add.21), channel_id=1, source_target_pairs={{0,17},{1,16},{2,19},{3,18},{4,21},{5,20},{6,23},{7,22},{8,14},{9,... | collective-permute-start | bytes 258056 | tf_op jit(solution)/shard_map/ppermute | solution.py:416
  19.8 1.7 %collective-permute-start.7 = (f32[168,128]{1,0:T(8,128)S(1)}, f32[168,128]{1,0:T(8,128)S(1)}, u32[]{:S(2)}, u32[]{:S(2)}) collective-permute-start(f32[168,128]{1,0:T(8,128)S(1)} %add.21), channel_id=1, source_target_pairs={{0,1},{1,0},{2,3},{3,2},{4,5},{5,4},{6,7},{7,6},{8,12},{9,13},{10,... | collective-permute-start | bytes 258056 | tf_op jit(solution)/shard_map/ppermute | solution.py:416
  21.5 0.9 %collective-permute-start.6 = (f32[168,128]{1,0:T(8,128)S(1)}, f32[168,128]{1,0:T(8,128)S(1)}, u32[]{:S(2)}, u32[]{:S(2)}) collective-permute-start(f32[168,128]{1,0:T(8,128)S(1)} %add.21), channel_id=1, source_target_pairs={{0,16},{1,17},{2,18},{3,19},{4,20},{5,21},{6,22},{7,23},{8,10},{9,... | collective-permute-start | bytes 258056 | tf_op jit(solution)/shard_map/ppermute | solution.py:416
  22.4 1.3 %assemble.2 = f32[128,16,128]{2,1,0:T(8,128)} custom-call(f32[2,14,128,128]{3,2,1,0:T(8,128)S(1)} %get-tuple-element.41.inner, f32[2,2,128,128]{3,2,1,0:T(8,128)S(1)} %get-tuple-element.42.border), custom_call_target="tpu_custom_call" | custom-call | bytes 3690000 | tf_op jit(solution)/shard_map/assemble/pallas_call | solution.py:513
  23.7 0.6 %collective-permute-done.8 = f32[168,128]{1,0:T(8,128)S(1)} collective-permute-done((f32[168,128]{1,0:T(8,128)S(1)}, f32[168,128]{1,0:T(8,128)S(1)}, u32[]{:S(2)}, u32[]{:S(2)}) %collective-permute-start.8) | collective-permute-done | bytes 86048 | tf_op jit(solution)/shard_map/ppermute | solution.py:416
  24.3 0.6 %collective-permute-done.7 = f32[168,128]{1,0:T(8,128)S(1)} collective-permute-done((f32[168,128]{1,0:T(8,128)S(1)}, f32[168,128]{1,0:T(8,128)S(1)}, u32[]{:S(2)}, u32[]{:S(2)}) %collective-permute-start.7) | collective-permute-done | bytes 86048 | tf_op jit(solution)/shard_map/ppermute | solution.py:416
  24.9 1.1 %collective-permute-done.6 = f32[168,128]{1,0:T(8,128)S(1)} collective-permute-done((f32[168,128]{1,0:T(8,128)S(1)}, f32[168,128]{1,0:T(8,128)S(1)}, u32[]{:S(2)}, u32[]{:S(2)}) %collective-permute-start.6) | collective-permute-done | bytes 86048 | tf_op jit(solution)/shard_map/ppermute | solution.py:416
  26.0 2.4 %collective-permute-start.11 = (f32[168,128]{1,0:T(8,128)S(1)}, f32[168,128]{1,0:T(8,128)S(1)}, u32[]{:S(2)}, u32[]{:S(2)}) collective-permute-start(f32[168,128]{1,0:T(8,128)S(1)} %add_add_fusion.1), channel_id=1, source_target_pairs={{0,6},{1,7},{2,4},{3,5},{4,2},{5,3},{6,0},{7,1},{8,25},{9,24},{10,... | collective-permute-start | bytes 258056 | tf_op jit(solution)/shard_map/ppermute | solution.py:416
  28.4 2.0 %collective-permute-start.9 = (f32[168,128]{1,0:T(8,128)S(1)}, f32[168,128]{1,0:T(8,128)S(1)}, u32[]{:S(2)}, u32[]{:S(2)}) collective-permute-start(f32[168,128]{1,0:T(8,128)S(1)} %add_add_fusion.1), channel_id=1, source_target_pairs={{0,2},{1,3},{2,0},{3,1},{4,6},{5,7},{6,4},{7,5},{8,24},{9,25},{10,... | collective-permute-start | bytes 258056 | tf_op jit(solution)/shard_map/ppermute | solution.py:416
  30.4 1.3 %assemble.3 = f32[128,16,128]{2,1,0:T(8,128)} custom-call(f32[2,14,128,128]{3,2,1,0:T(8,128)S(1)} %get-tuple-element.41.inner, f32[2,2,128,128]{3,2,1,0:T(8,128)S(1)} %get-tuple-element.42.border), custom_call_target="tpu_custom_call" | custom-call | bytes 3690000 | tf_op jit(solution)/shard_map/assemble/pallas_call | solution.py:513
  31.7 0.7 %collective-permute-done.11 = f32[168,128]{1,0:T(8,128)S(1)} collective-permute-done((f32[168,128]{1,0:T(8,128)S(1)}, f32[168,128]{1,0:T(8,128)S(1)}, u32[]{:S(2)}, u32[]{:S(2)}) %collective-permute-start.11) | collective-permute-done | bytes 86048 | tf_op jit(solution)/shard_map/ppermute | solution.py:416
  32.4 1.8 %collective-permute-done.10 = f32[168,128]{1,0:T(8,128)S(1)} collective-permute-done((f32[168,128]{1,0:T(8,128)S(1)}, f32[168,128]{1,0:T(8,128)S(1)}, u32[]{:S(2)}, u32[]{:S(2)}) %collective-permute-start.10) | collective-permute-done | bytes 86048 | tf_op jit(solution)/shard_map/ppermute | solution.py:416
  34.3 1.3 %collective-permute-done.12.given = f32[168,128]{1,0:T(8,128)S(1)} collective-permute-done((f32[168,128]{1,0:T(8,128)S(1)}, f32[168,128]{1,0:T(8,128)S(1)}, u32[]{:S(2)}, u32[]{:S(2)}) %collective-permute-start.12) | collective-permute-done | bytes 86048 | tf_op jit(solution)/shard_map/ppermute | solution.py:416
  35.6 4.3 %factor.1 = f32[128,128]{1,0:T(8,128)} custom-call(f32[168,128]{1,0:T(8,128)S(1)} %add_add_fusion.kept, f32[168,128]{1,0:T(8,128)S(1)} %collective-permute-done.12.given), custom_call_target="tpu_custom_call" | custom-call | bytes 22140000 | tf_op jit(solution)/shard_map/factor/pallas_call | solution.py:535
  (15 shorter events, 0.3 us)
Async XLA Ops:
  0.6 3.7 %copy-start = (f32[3,132,16,128]{3,2,1,0:T(8,128)S(1)}, f32[3,132,16,128]{3,2,1,0:T(8,128)}, u32[]{:S(2)}) copy-start(f32[3,132,16,128]{3,2,1,0:T(8,128)} %fields.2) | copy-start | bytes 9732100
  1.9 14.7 %collective-permute-start = (f32[3,2,128,128]{3,2,1,0:T(8,128)S(1)}, f32[3,2,128,128]{3,2,1,0:T(8,128)S(1)}, u32[]{:S(2)}, u32[]{:S(2)}) collective-permute-start(f32[3,2,128,128]{3,2,1,0:T(8,128)S(1)} %far_face.1), channel_id=1, source_target_pairs={{0,24},{8,16},{16,8},{24,0},{1,25},{9,17},{17,9},{25,1},{2,26},{10... | collective-permute-start | bytes 1179656 | tf_op jit(solution)/shard_map/ppermute | solution.py:453
  5.9 8.7 %collective-permute-start.3 = (f32[3,128,128]{2,1,0:T(8,128)S(1)}, f32[3,128,128]{2,1,0:T(8,128)S(1)}, u32[]{:S(2)}, u32[]{:S(2)}) collective-permute-start(f32[3,128,128]{2,1,0:T(8,128)S(1)} %get-tuple-element.35), channel_id=1, source_target_pairs={{0,8},{8,0},{16,24},{24,16},{1,9},{9,1},{17,25},{25,17},{2,10},{10... | collective-permute-start | bytes 589832 | tf_op jit(solution)/shard_map/ppermute | solution.py:470
  6.7 8.0 %collective-permute-start.4 = (f32[3,128,128]{2,1,0:T(8,128)S(1)}, f32[3,128,128]{2,1,0:T(8,128)S(1)}, u32[]{:S(2)}, u32[]{:S(2)}) collective-permute-start(f32[3,128,128]{2,1,0:T(8,128)S(1)} %get-tuple-element.36), channel_id=1, source_target_pairs={{0,8},{8,0},{16,24},{24,16},{1,9},{9,1},{17,25},{25,17},{2,10},{10... | collective-permute-start | bytes 589832 | tf_op jit(solution)/shard_map/ppermute | solution.py:470
  6.7 7.9 %collective-permute-start.1 = (f32[128,128]{1,0:T(8,128)S(1)}, f32[128,128]{1,0:T(8,128)S(1)}, u32[]{:S(2)}, u32[]{:S(2)}) collective-permute-start(f32[128,128]{1,0:T(8,128)S(1)} %get-tuple-element.29), channel_id=1, source_target_pairs={{0,1},{1,2},{2,3},{3,4},{4,5},{5,6},{6,7},{7,0},{8,9},{9,10},{10,1... | collective-permute-start | bytes 196616 | tf_op jit(solution)/shard_map/ppermute | solution.py:471
  8.2 6.4 %collective-permute-start.2 = (f32[128,128]{1,0:T(8,128)S(1)}, f32[128,128]{1,0:T(8,128)S(1)}, u32[]{:S(2)}, u32[]{:S(2)}) collective-permute-start(f32[128,128]{1,0:T(8,128)S(1)} %get-tuple-element.30), channel_id=1, source_target_pairs={{0,7},{1,0},{2,1},{3,2},{4,3},{5,4},{6,5},{7,6},{8,15},{9,8},{10,9... | collective-permute-start | bytes 196616 | tf_op jit(solution)/shard_map/ppermute | solution.py:472
  17.5 1.3 %collective-permute-start.5 = (f32[168,128]{1,0:T(8,128)S(1)}, f32[168,128]{1,0:T(8,128)S(1)}, u32[]{:S(2)}, u32[]{:S(2)}) collective-permute-start(f32[168,128]{1,0:T(8,128)S(1)} %get-tuple-element.40), channel_id=1, source_target_pairs={{0,8},{1,9},{2,10},{3,11},{4,12},{5,13},{6,14},{7,15},{8,0},{9,1},... | collective-permute-start | bytes 258056 | tf_op jit(solution)/shard_map/ppermute | solution.py:416
  18.8 5.4 %collective-permute-start.8 = (f32[168,128]{1,0:T(8,128)S(1)}, f32[168,128]{1,0:T(8,128)S(1)}, u32[]{:S(2)}, u32[]{:S(2)}) collective-permute-start(f32[168,128]{1,0:T(8,128)S(1)} %add.21), channel_id=1, source_target_pairs={{0,17},{1,16},{2,19},{3,18},{4,21},{5,20},{6,23},{7,22},{8,14},{9,... | collective-permute-start | bytes 258056 | tf_op jit(solution)/shard_map/ppermute | solution.py:416
  19.8 5.1 %collective-permute-start.7 = (f32[168,128]{1,0:T(8,128)S(1)}, f32[168,128]{1,0:T(8,128)S(1)}, u32[]{:S(2)}, u32[]{:S(2)}) collective-permute-start(f32[168,128]{1,0:T(8,128)S(1)} %add.21), channel_id=1, source_target_pairs={{0,1},{1,0},{2,3},{3,2},{4,5},{5,4},{6,7},{7,6},{8,12},{9,13},{10,... | collective-permute-start | bytes 258056 | tf_op jit(solution)/shard_map/ppermute | solution.py:416
  21.5 4.5 %collective-permute-start.6 = (f32[168,128]{1,0:T(8,128)S(1)}, f32[168,128]{1,0:T(8,128)S(1)}, u32[]{:S(2)}, u32[]{:S(2)}) collective-permute-start(f32[168,128]{1,0:T(8,128)S(1)} %add.21), channel_id=1, source_target_pairs={{0,16},{1,17},{2,18},{3,19},{4,20},{5,21},{6,22},{7,23},{8,10},{9,... | collective-permute-start | bytes 258056 | tf_op jit(solution)/shard_map/ppermute | solution.py:416
  26.0 6.4 %collective-permute-start.11 = (f32[168,128]{1,0:T(8,128)S(1)}, f32[168,128]{1,0:T(8,128)S(1)}, u32[]{:S(2)}, u32[]{:S(2)}) collective-permute-start(f32[168,128]{1,0:T(8,128)S(1)} %add_add_fusion.1), channel_id=1, source_target_pairs={{0,6},{1,7},{2,4},{3,5},{4,2},{5,3},{6,0},{7,1},{8,25},{9,24},{10,... | collective-permute-start | bytes 258056 | tf_op jit(solution)/shard_map/ppermute | solution.py:416
  28.4 5.8 %collective-permute-start.10 = (f32[168,128]{1,0:T(8,128)S(1)}, f32[168,128]{1,0:T(8,128)S(1)}, u32[]{:S(2)}, u32[]{:S(2)}) collective-permute-start(f32[168,128]{1,0:T(8,128)S(1)} %add_add_fusion.1), channel_id=1, source_target_pairs={{0,4},{1,5},{2,6},{3,7},{4,0},{5,1},{6,2},{7,3},{8,9},{9,8},{10,11... | collective-permute-start | bytes 258056 | tf_op jit(solution)/shard_map/ppermute | solution.py:416
  28.4 5.8 %collective-permute-start.9 = (f32[168,128]{1,0:T(8,128)S(1)}, f32[168,128]{1,0:T(8,128)S(1)}, u32[]{:S(2)}, u32[]{:S(2)}) collective-permute-start(f32[168,128]{1,0:T(8,128)S(1)} %add_add_fusion.1), channel_id=1, source_target_pairs={{0,2},{1,3},{2,0},{3,1},{4,6},{5,7},{6,4},{7,5},{8,24},{9,25},{10,... | collective-permute-start | bytes 258056 | tf_op jit(solution)/shard_map/ppermute | solution.py:416
  34.2 1.3 %collective-permute-start.12 = (f32[168,128]{1,0:T(8,128)S(1)}, f32[168,128]{1,0:T(8,128)S(1)}, u32[]{:S(2)}, u32[]{:S(2)}) collective-permute-start(f32[168,128]{1,0:T(8,128)S(1)} %add_add_fusion.kept), channel_id=1, source_target_pairs={{0,8},{1,9},{2,10},{3,11},{4,12},{5,13},{6,14},{7,15},{8,0},{9,1},... | collective-permute-start | bytes 258056 | tf_op jit(solution)/shard_map/ppermute | solution.py:416

commit v8 on v7

--- a/solution.py
+++ b/solution.py
@@ -56,16 +56,13 @@
     return jnp.where((col >= half) & (row >= col - half), first, last)
 
 
-def unfold(folded, last_diagonal):
+def unfold(folded):
     half = folded.shape[0]
     row = lax.broadcasted_iota(jnp.int32, folded.shape, 0)
     col = lax.broadcasted_iota(jnp.int32, folded.shape, 1)
-    first = pltpu.roll(folded, half, 1)
-    off_first = jnp.where(row > col, first, 0.0)
-    off_last = jnp.where((col < half) | (col - half > row), folded, 0.0)
-    on_first = jnp.where(row == col, first, 0.0)
-    on_last = jnp.where(row == col - half, last_diagonal, 0.0)
-    return jnp.concatenate([off_first, off_last], axis=0), jnp.concatenate([on_first, on_last], axis=0)
+    first = jnp.where(row > col, pltpu.roll(folded, half, 1), 0.0)
+    last = jnp.where((col < half) | (col - half > row), folded, 0.0)
+    return jnp.concatenate([first, last], axis=0)
 
 
 def half_starts(length):
@@ -255,7 +252,7 @@
 
 
 def interior_kernel(
-    rows, planes, fields, own_z, spin, stretch, bend_x, bend_y, near_0, near_1, left, right, out, total, pieces, to_last, to_first
+    rows, planes, fields, own_z, spin, stretch, bend_x, bend_y, near_0, near_1, left, right, out, total, to_last, to_first, pieces
 ):
     size = own_z.shape[3]
     odd = lax.axis_index("gy") % 2 == 1
@@ -278,11 +275,10 @@
 
 
 def border_kernel(
-    rows, planes, fields, own_z, far, left, right, part, velocity, out, keep, give, message, pieces, to_last, to_first
+    rows, planes, fields, own_z, far, to_last, to_first, part, velocity, out, keep, give, message, pieces
 ):
     size = fields.shape[3]
     odd = lax.axis_index("gy") % 2 == 1
-    to_last[...], to_first[...] = edge_terms(left[...], right[...])
     for t in range(planes // TILE):
         for half, results in beside_face(rows, planes, fields, own_z, [far.at[:, i] for i in range(2)], ~odd, to_last, to_first, t):
             store_results(results, out, half, pieces, half, t, planes, size)
@@ -290,9 +286,9 @@
     message[0:planes, :] = pack_pair(grams[0], grams[1])
     message[planes : 2 * planes, :] = pack_pair(grams[2], grams[3])
     message[2 * planes : 5 * planes // 2, :] = fold(grams[4])
-    for i, f in enumerate((1, 3, 4)):
-        message[5 * planes // 2 + i : 5 * planes // 2 + i + 1, :] = diagonal(grams[f])
-    used = 5 * planes // 2 + 3
+    for i, gram in enumerate(grams):
+        message[5 * planes // 2 + i : 5 * planes // 2 + i + 1, :] = diagonal(gram)
+    used = 5 * planes // 2 + 5
     message[used:, :] = jnp.zeros((message.shape[0] - used, planes), jnp.float32)
     mine, other = half_starts(keep.shape[0])
     keep[...] = message[pl.ds(mine, keep.shape[0]), :]
@@ -324,51 +320,63 @@
     return jnp.broadcast_to(tile[:, at : at + 1], tile.shape)
 
 
-def factor_tiles(tiles, widths):
-    count, size = tiles[0].shape
+def thirds_of(values):
+    high = values.astype(jnp.bfloat16).astype(jnp.float32)
+    rest = values - high
+    middle = rest.astype(jnp.bfloat16).astype(jnp.float32)
+    return high, middle, rest - middle
+
+
+def eliminate(rows, first, width):
+    count, size = rows[0].shape
     sub = lax.broadcasted_iota(jnp.int32, (count, size), 0)
     lane = lax.broadcasted_iota(jnp.int32, (count, size), 1)
+    head = width // count
+    tall = len(rows)
+    made = [[spread_column(rows[t], first + j) for j in range(width)] for t in range(tall)]
+    spread = [[made[t][j] for t in range(tall)] for j in range(width)]
+    rows = list(rows)
+    results = [jnp.zeros((count, size), jnp.float32)] * head
+    entries = {}
+    pivot = splat(spread[0][0], 0)
+    for j in range(width):
+        t0, s0 = divmod(j, count)
+        inverse = 1.0 / pivot
+        for m in range(j + 1, width):
+            entries[j, m] = splat(spread[j][m // count], m % count)
+        if j + 1 < width:
+            t1, s1 = divmod(j + 1, count)
+            following = splat(spread[j + 1][t1], s1) - (entries[j, j + 1] * entries[j, j + 1]) * inverse
+        row = splat(rows[t0], s0)
+        results[t0] = jnp.where(sub == s0, row * lax.rsqrt(pivot), results[t0])
+        for t in range(t0, tall):
+            scaled = spread[j][t] * inverse
+            for m in range(j + 1, width):
+                spread[m][t] = spread[m][t] - scaled * entries[j, m]
+            rows[t] = rows[t] - scaled * row
+        if j + 1 < width:
+            pivot = following
+    results = [jnp.where(lane >= first + t * count + sub, results[t], 0.0) for t in range(head)]
+    return results, rows[head:]
+
+
+def factor_tiles(tiles, widths):
+    count = tiles[0].shape[0]
     tiles = list(tiles)
     out = []
     first = 0
-    for width in widths:
-        top = first // count
-        head = width // count
-        spread = [[spread_column(tiles[top + t], first + j) for t in range(head)] for j in range(width)]
-        rows = tiles[top : top + head]
-        results = [jnp.zeros((count, size), jnp.float32)] * head
-        inverses, entries, pivots = [], {}, []
-        pivot = splat(spread[0][0], 0)
-        for j in range(width):
-            t0, s0 = divmod(j, count)
-            inverse = 1.0 / pivot
-            inverses.append(inverse)
-            for m in range(j + 1, width):
-                entries[j, m] = splat(spread[j][m // count], m % count)
-            if j + 1 < width:
-                t1, s1 = divmod(j + 1, count)
-                following = splat(spread[j + 1][t1], s1) - (entries[j, j + 1] * entries[j, j + 1]) * inverse
-            row = splat(rows[t0], s0)
-            pivots.append(row)
-            results[t0] = jnp.where(sub == s0, row * lax.rsqrt(pivot), results[t0])
-            for t in range(t0, head):
-                scaled = spread[j][t] * inverse
-                for m in range(j + 1, width):
-                    spread[m][t] = spread[m][t] - scaled * entries[j, m]
-                rows[t] = rows[t] - scaled * row
-            if j + 1 < width:
-                pivot = following
-        for t in range(head):
-            out.append(jnp.where(lane >= first + t * count + sub, results[t], 0.0))
-        for t in range(top + head, len(tiles)):
-            tile = tiles[t]
-            columns = [spread_column(tile, first + j) for j in range(width)]
-            for j in range(width):
-                scaled = columns[j] * inverses[j]
-                for m in range(j + 1, width):
-                    columns[m] = columns[m] - scaled * entries[j, m]
-                tile = tile - scaled * pivots[j]
-            tiles[t] = tile
+    for i, width in enumerate(widths):
+        top, after = first // count, (first + width) // count
+        end = after + sum(widths[i + 1 : i + 3]) // count
+        results, tiles[after:end] = eliminate(tiles[top:end], first, width)
+        out += results
+        if end < len(tiles):
+            high, middle, low = thirds_of(jnp.concatenate(results, axis=0))
+            one = jnp.concatenate([high, high, middle, high, low, middle], axis=0).astype(jnp.bfloat16)
+            two = jnp.concatenate([high, middle, high, low, high, middle], axis=0).astype(jnp.bfloat16)
+            update = lax.dot_general(one, two, (((0,), (0,)), ((), ())), preferred_element_type=jnp.float32)
+            for t in range(end, len(tiles)):
+                tiles[t] = tiles[t] - update[t * count : (t + 1) * count, :]
         first += width
     return out
 
@@ -379,26 +387,21 @@
     message[pl.ds(other, kept.shape[0]), :] = given[...]
     row, col = halves(planes)
     eye = row == col
-
-    def scale(squares):
-        return 1.0 / (5.0 * cells * (squares / (planes * cells) + 1e-06))
-
-    def unpack(packed, second_diagonal):
-        first_scale = scale(jnp.sum(jnp.where(eye, packed, 0.0)))
-        second_scale = scale(jnp.sum(second_diagonal))
-        lower = jnp.where(row > col, packed * first_scale, jnp.where(row < col, packed * second_scale, 0.0))
-        both = jnp.where(eye, packed * first_scale + second_diagonal * second_scale, 0.0)
-        return lower, both
-
-    diagonals = [message[5 * planes // 2 + i : 5 * planes // 2 + i + 1, :] for i in range(3)]
-    low_a, both_a = unpack(message[0:planes, :], diagonals[0])
-    low_b, both_b = unpack(message[planes : 2 * planes, :], diagonals[1])
-    low_c, both_c = unfold(message[2 * planes : 5 * planes // 2, :], diagonals[2])
-    third = scale(jnp.sum(both_c))
-    triangles = low_a + low_b + low_c * third
-    cross = triangles + triangles.T + (both_a + both_b + both_c * third)
-    wide = 16 if planes % 32 == 0 else 8
-    widths = [8] * (planes // 16) + [wide] * (planes // 2 // wide)
+    diagonals = message[5 * planes // 2 : 5 * planes // 2 + 8, :]
+    squares = jnp.broadcast_to(jnp.sum(diagonals, axis=1, keepdims=True), diagonals.shape)
+    scales = 1.0 / (5.0 * cells * (squares / (planes * cells) + 1e-06))
+    scaled = diagonals * scales
+    scale = [scales[i : i + 1, :] for i in range(5)]
+
+    def pair(packed, first):
+        return jnp.where(row > col, packed * scale[first], packed * scale[first + 1])
+
+    folded = unfold(message[2 * planes : 5 * planes // 2, :])
+    triangles = jnp.where(eye, 0.0, pair(message[0:planes, :], 0) + pair(message[planes : 2 * planes, :], 2))
+    triangles = triangles + folded * scale[4]
+    cross = triangles + triangles.T + jnp.where(eye, jnp.sum(scaled[0:5], axis=0, keepdims=True), 0.0)
+    narrow = planes // 64 * 2
+    widths = [8] * narrow + [16] * (planes // 16 - narrow // 2)
     upper = factor_tiles([cross[t : t + 8, :] for t in range(0, planes, 8)], widths)
     factor[...] = jnp.concatenate(upper, axis=0).T
 
@@ -486,29 +489,33 @@
         name="inner",
     )(turned)
     pieces = pltpu.VMEM((2, 2, 2 * planes, 2 * cols), jnp.bfloat16)
-    edges = [pltpu.VMEM((planes, cols), jnp.float32)] * 2
-    inner, part = pl.pallas_call(
+    inner, part, to_last, to_first = pl.pallas_call(
         functools.partial(interior_kernel, rows, planes),
-        out_shape=(f32(2, rows - 2, planes, cols), f32(2, 2 * planes, 2 * planes)),
+        out_shape=(
+            f32(2, rows - 2, planes, cols),
+            f32(2, 2 * planes, 2 * planes),
+            f32(planes, cols),
+            f32(planes, cols),
+        ),
         in_specs=[VMEM] * 10,
-        out_specs=(VMEM, VMEM),
-        scratch_shapes=[pieces, *edges],
+        out_specs=(VMEM,) * 4,
+        scratch_shapes=[pieces],
         compiler_params=params(),
         cost_estimate=cost(1.9),
         name="interior",
     )(turned, own_z, *planar, *near, left, right)
-    half = -(-(5 * planes // 2 + 3) // 16) * 8
+    half = -(-(5 * planes // 2 + 8) // 16) * 8
     message = pltpu.VMEM((2 * half, planes), jnp.float32)
     border, keep, give = pl.pallas_call(
         functools.partial(border_kernel, rows, planes),
         out_shape=(f32(2, 2, planes, cols), f32(half, planes), f32(half, planes)),
         in_specs=[VMEM] * 7,
         out_specs=(VMEM, VMEM, VMEM),
-        scratch_shapes=[message, pltpu.VMEM((2, 2 * planes, 2 * cols), jnp.bfloat16), *edges],
+        scratch_shapes=[message, pltpu.VMEM((2, 2 * planes, 2 * cols), jnp.bfloat16)],
         compiler_params=params(),
         cost_estimate=cost(0.7),
         name="border",
-    )(turned, own_z, far, left, right, part, velocity)
+    )(turned, own_z, far, to_last, to_first, part, velocity)
     enstrophy, strain_rate = [
         pl.pallas_call(
             functools.partial(assemble_kernel, rows, planes, f),

time: 40 us -> 39.2 us (0.980)
  Pallas kernels: 15.6 us -> 14.8 us
    pallas_call x1, Pallas kernels: 4.29 us -> 3.66 us  [per_device(): pl.pallas_call(functools.partial(factor_kernel, float(cells), planes), ou...]
  transfers between devices with their start and end apart: 13 -> 13, of which waited for: 7 -> 7; matrix products, arithmetic and copies ran while one was open for 0% -> 0% of each run, Pallas kernels for 23% -> 24%
where the time goes in v8:
time: 39.2 us; the launch traced here: 39.1 us
  starting transfers between devices  16.2 us (41%)
  Pallas kernels  14.8 us (38%)
  waiting for transfers between devices  7.33 us (19%)
  between operations  0.73 us (2%)
    ppermute x8, starting transfers between devices, exchange(): lax.ppermute(values, AXES, [(i, i ^ (odd if i // count_z % 2 else even))...  8.14 us
    ppermute x8, waiting for transfers between devices, exchange(): lax.ppermute(values, AXES, [(i, i ^ (odd if i // count_z % 2 else even))...  7.31 us
    pallas_call x1, Pallas kernels, per_device(): pl.pallas_call(functools.partial(factor_kernel, float(cells), planes), ou...  3.66 us
    ppermute x1, starting transfers between devices, per_device(): lax.ppermute(behind, 'gz', [(i, (i - 1) % count_z) for i in range(count_z)])  3.23 us
    pallas_call x1, Pallas kernels, per_device(): pl.pallas_call(functools.partial(inner_kernel, rows, planes), out_shape=(...  3.12 us
    pallas_call x2, Pallas kernels, per_device(): pl.pallas_call(functools.partial(assemble_kernel, rows, planes, f), out_s...  2.55 us
    ppermute x1, starting transfers between devices, per_device(): lax.ppermute(far, 'gy', [(i, (i + 1 if i % 2 else i - 1) % count_y) for i...  2.47 us
    pallas_call x1, Pallas kernels, per_device(): pl.pallas_call(functools.partial(interior_kernel, rows, planes), out_shap...  1.97 us
  transfers between devices with their start and end apart: 13, of which 7 were waited for; matrix products, arithmetic and copies ran while one was open for 0% of the time, Pallas kernels for 24%

profile of v8, /device:TPU:0, one launch (start us, length us, event | category | flops | bytes accessed | tf_op | source)
XLA Modules:
  0.0 39.1 jit_solution(2018862520897336406)
XLA Ops:
  0.6 1.3 %far_face.1 = f32[3,2,128,128]{3,2,1,0:T(8,128)S(1)} custom-call(f32[3,132,16,128]{3,2,1,0:T(8,128)} %fields.2), custom_call_target="tpu_custom_call" | custom-call | bytes 3690000 | tf_op jit(solution)/shard_map/far_face/pallas_call | solution.py:445
  1.9 2.5 %collective-permute-start = (f32[3,2,128,128]{3,2,1,0:T(8,128)S(1)}, f32[3,2,128,128]{3,2,1,0:T(8,128)S(1)}, u32[]{:S(2)}, u32[]{:S(2)}) collective-permute-start(f32[3,2,128,128]{3,2,1,0:T(8,128)S(1)} %far_face.1), channel_id=1, source_target_pairs={{0,24},{8,16},{16,8},{24,0},{1,25},{9,17},{17,9},{25,1},{2,26},{10... | collective-permute-start | bytes 1179656 | tf_op jit(solution)/shard_map/ppermute | solution.py:456
  4.4 1.6 %faces.1 = (f32[3,16,132,128]{3,2,1,0:T(8,128)S(1)}, f32[3,128,128]{2,1,0:T(8,128)S(1)}, f32[3,128,128]{2,1,0:T(8,128)S(1)}, f32[128,128]{1,0:T(8,128)S(1)}, f32[128,128]{1,0:T(8,128)S(1)}) custom-call(f32[3,132,16,128]{3,2,1,0:T(8,128)S(1)} %copy-done), custom_call_target="tpu_custom_call" | custom-call | bytes 9225000 | tf_op jit(solution)/shard_map/faces/pallas_call | solution.py:457
  5.9 0.7 %collective-permute-start.1 = (f32[3,128,128]{2,1,0:T(8,128)S(1)}, f32[3,128,128]{2,1,0:T(8,128)S(1)}, u32[]{:S(2)}, u32[]{:S(2)}) collective-permute-start(f32[3,128,128]{2,1,0:T(8,128)S(1)} %get-tuple-element.35), channel_id=1, source_target_pairs={{0,8},{8,0},{16,24},{24,16},{1,9},{9,1},{17,25},{25,17},{2,10},{10... | collective-permute-start | bytes 589832 | tf_op jit(solution)/shard_map/ppermute | solution.py:473
  6.7 1.5 %collective-permute-start.3 = (f32[128,128]{1,0:T(8,128)S(1)}, f32[128,128]{1,0:T(8,128)S(1)}, u32[]{:S(2)}, u32[]{:S(2)}) collective-permute-start(f32[128,128]{1,0:T(8,128)S(1)} %get-tuple-element.37), channel_id=1, source_target_pairs={{0,1},{1,2},{2,3},{3,4},{4,5},{5,6},{6,7},{7,0},{8,9},{9,10},{10,1... | collective-permute-start | bytes 196616 | tf_op jit(solution)/shard_map/ppermute | solution.py:474
  8.2 3.2 %collective-permute-start.4 = (f32[128,128]{1,0:T(8,128)S(1)}, f32[128,128]{1,0:T(8,128)S(1)}, u32[]{:S(2)}, u32[]{:S(2)}) collective-permute-start(f32[128,128]{1,0:T(8,128)S(1)} %get-tuple-element.38), channel_id=1, source_target_pairs={{0,7},{1,0},{2,1},{3,2},{4,3},{5,4},{6,5},{7,6},{8,15},{9,8},{10,9... | collective-permute-start | bytes 196616 | tf_op jit(solution)/shard_map/ppermute | solution.py:475
  11.5 3.1 %inner.1 = (f32[3,128,128]{2,1,0:T(8,128)S(1)}, f32[3,16,128,128]{3,2,1,0:T(8,128)S(1)}, f32[12,128,128]{2,1,0:T(8,128)S(1)}, f32[12,128,128]{2,1,0:T(8,128)S(1)...) custom-call(f32[3,16,132,128]{3,2,1,0:T(8,128)S(1)} %get-tuple-element.28.fields), custom_call_target="tpu_custom_call" | custom-call | bytes 11070000 | tf_op jit(solution)/shard_map/inner/pallas_call | solution.py:478
  14.6 2.0 %interior.1 = (f32[2,14,128,128]{3,2,1,0:T(8,128)S(1)}, f32[2,256,256]{2,1,0:T(8,128)S(1)}, f32[128,128]{1,0:T(8,128)S(1)}, f32[128,128]{1,0:T(8,128)S(1)}) custom-call(f32[3,16,132,128]{3,2,1,0:T(8,128)S(1)} %get-tuple-element.28.fields, f32[3,16,128,128]{3,2,1,0:T(8,128)S(1)} %get-tuple-element.29.own_z, f32[12,128,128]{2,1,0:T(8,128)S(1)} %get-tuple-element.31.spin, ...), custom_call_target="tpu_custom_call" | custom-call | bytes 7011000 | tf_op jit(solution)/shard_map/interior/pallas_call | solution.py:492
  16.6 0.7 %border.1 = (f32[2,2,128,128]{3,2,1,0:T(8,128)S(1)}, f32[168,128]{1,0:T(8,128)S(1)}, f32[168,128]{1,0:T(8,128)S(1)}) custom-call(f32[3,16,132,128]{3,2,1,0:T(8,128)S(1)} %get-tuple-element.28.fields, f32[3,16,128,128]{3,2,1,0:T(8,128)S(1)} %get-tuple-element.29.own_z, f32[3,2,128,128]{3,2,1,0:T(8,128)S(1)} %collective-permute-done.far, ...), custom_call_target="tpu_custom_call" | custom-call | bytes 2583000 | tf_op jit(solution)/shard_map/border/pallas_call | solution.py:509
  17.4 1.3 %collective-permute-done.5 = f32[168,128]{1,0:T(8,128)S(1)} collective-permute-done((f32[168,128]{1,0:T(8,128)S(1)}, f32[168,128]{1,0:T(8,128)S(1)}, u32[]{:S(2)}, u32[]{:S(2)}) %collective-permute-start.5) | collective-permute-done | bytes 86048 | tf_op jit(solution)/shard_map/ppermute | solution.py:419
  18.7 1.0 %collective-permute-start.8 = (f32[168,128]{1,0:T(8,128)S(1)}, f32[168,128]{1,0:T(8,128)S(1)}, u32[]{:S(2)}, u32[]{:S(2)}) collective-permute-start(f32[168,128]{1,0:T(8,128)S(1)} %add.21), channel_id=1, source_target_pairs={{0,17},{1,16},{2,19},{3,18},{4,21},{5,20},{6,23},{7,22},{8,14},{9,... | collective-permute-start | bytes 258056 | tf_op jit(solution)/shard_map/ppermute | solution.py:419
  19.6 1.7 %collective-permute-start.7 = (f32[168,128]{1,0:T(8,128)S(1)}, f32[168,128]{1,0:T(8,128)S(1)}, u32[]{:S(2)}, u32[]{:S(2)}) collective-permute-start(f32[168,128]{1,0:T(8,128)S(1)} %add.21), channel_id=1, source_target_pairs={{0,1},{1,0},{2,3},{3,2},{4,5},{5,4},{6,7},{7,6},{8,12},{9,13},{10,... | collective-permute-start | bytes 258056 | tf_op jit(solution)/shard_map/ppermute | solution.py:419
  21.3 0.9 %collective-permute-start.6 = (f32[168,128]{1,0:T(8,128)S(1)}, f32[168,128]{1,0:T(8,128)S(1)}, u32[]{:S(2)}, u32[]{:S(2)}) collective-permute-start(f32[168,128]{1,0:T(8,128)S(1)} %add.21), channel_id=1, source_target_pairs={{0,16},{1,17},{2,18},{3,19},{4,20},{5,21},{6,22},{7,23},{8,10},{9,... | collective-permute-start | bytes 258056 | tf_op jit(solution)/shard_map/ppermute | solution.py:419
  22.2 1.3 %assemble.2 = f32[128,16,128]{2,1,0:T(8,128)} custom-call(f32[2,14,128,128]{3,2,1,0:T(8,128)S(1)} %get-tuple-element.45.inner, f32[2,2,128,128]{3,2,1,0:T(8,128)S(1)} %get-tuple-element.46.border), custom_call_target="tpu_custom_call" | custom-call | bytes 3690000 | tf_op jit(solution)/shard_map/assemble/pallas_call | solution.py:520
  23.5 0.6 %collective-permute-done.8 = f32[168,128]{1,0:T(8,128)S(1)} collective-permute-done((f32[168,128]{1,0:T(8,128)S(1)}, f32[168,128]{1,0:T(8,128)S(1)}, u32[]{:S(2)}, u32[]{:S(2)}) %collective-permute-start.8) | collective-permute-done | bytes 86048 | tf_op jit(solution)/shard_map/ppermute | solution.py:419
  24.1 0.6 %collective-permute-done.7 = f32[168,128]{1,0:T(8,128)S(1)} collective-permute-done((f32[168,128]{1,0:T(8,128)S(1)}, f32[168,128]{1,0:T(8,128)S(1)}, u32[]{:S(2)}, u32[]{:S(2)}) %collective-permute-start.7) | collective-permute-done | bytes 86048 | tf_op jit(solution)/shard_map/ppermute | solution.py:419
  24.7 1.1 %collective-permute-done.6 = f32[168,128]{1,0:T(8,128)S(1)} collective-permute-done((f32[168,128]{1,0:T(8,128)S(1)}, f32[168,128]{1,0:T(8,128)S(1)}, u32[]{:S(2)}, u32[]{:S(2)}) %collective-permute-start.6) | collective-permute-done | bytes 86048 | tf_op jit(solution)/shard_map/ppermute | solution.py:419
  25.8 2.4 %collective-permute-start.11 = (f32[168,128]{1,0:T(8,128)S(1)}, f32[168,128]{1,0:T(8,128)S(1)}, u32[]{:S(2)}, u32[]{:S(2)}) collective-permute-start(f32[168,128]{1,0:T(8,128)S(1)} %add_add_fusion.1), channel_id=1, source_target_pairs={{0,6},{1,7},{2,4},{3,5},{4,2},{5,3},{6,0},{7,1},{8,25},{9,24},{10,... | collective-permute-start | bytes 258056 | tf_op jit(solution)/shard_map/ppermute | solution.py:419
  28.2 2.0 %collective-permute-start.9 = (f32[168,128]{1,0:T(8,128)S(1)}, f32[168,128]{1,0:T(8,128)S(1)}, u32[]{:S(2)}, u32[]{:S(2)}) collective-permute-start(f32[168,128]{1,0:T(8,128)S(1)} %add_add_fusion.1), channel_id=1, source_target_pairs={{0,2},{1,3},{2,0},{3,1},{4,6},{5,7},{6,4},{7,5},{8,24},{9,25},{10,... | collective-permute-start | bytes 258056 | tf_op jit(solution)/shard_map/ppermute | solution.py:419
  30.3 1.3 %assemble.3 = f32[128,16,128]{2,1,0:T(8,128)} custom-call(f32[2,14,128,128]{3,2,1,0:T(8,128)S(1)} %get-tuple-element.45.inner, f32[2,2,128,128]{3,2,1,0:T(8,128)S(1)} %get-tuple-element.46.border), custom_call_target="tpu_custom_call" | custom-call | bytes 3690000 | tf_op jit(solution)/shard_map/assemble/pallas_call | solution.py:520
  31.6 0.7 %collective-permute-done.11 = f32[168,128]{1,0:T(8,128)S(1)} collective-permute-done((f32[168,128]{1,0:T(8,128)S(1)}, f32[168,128]{1,0:T(8,128)S(1)}, u32[]{:S(2)}, u32[]{:S(2)}) %collective-permute-start.11) | collective-permute-done | bytes 86048 | tf_op jit(solution)/shard_map/ppermute | solution.py:419
  32.2 1.8 %collective-permute-done.10 = f32[168,128]{1,0:T(8,128)S(1)} collective-permute-done((f32[168,128]{1,0:T(8,128)S(1)}, f32[168,128]{1,0:T(8,128)S(1)}, u32[]{:S(2)}, u32[]{:S(2)}) %collective-permute-start.10) | collective-permute-done | bytes 86048 | tf_op jit(solution)/shard_map/ppermute | solution.py:419
  34.1 1.3 %collective-permute-done.12.given = f32[168,128]{1,0:T(8,128)S(1)} collective-permute-done((f32[168,128]{1,0:T(8,128)S(1)}, f32[168,128]{1,0:T(8,128)S(1)}, u32[]{:S(2)}, u32[]{:S(2)}) %collective-permute-start.12) | collective-permute-done | bytes 86048 | tf_op jit(solution)/shard_map/ppermute | solution.py:419
  35.4 3.7 %factor.1 = f32[128,128]{1,0:T(8,128)} custom-call(f32[168,128]{1,0:T(8,128)S(1)} %add_add_fusion.kept, f32[168,128]{1,0:T(8,128)S(1)} %collective-permute-done.12.given), custom_call_target="tpu_custom_call" | custom-call | bytes 22140000 | tf_op jit(solution)/shard_map/factor/pallas_call | solution.py:542
  (15 shorter events, 0.3 us)
Async XLA Ops:
  0.6 3.7 %copy-start = (f32[3,132,16,128]{3,2,1,0:T(8,128)S(1)}, f32[3,132,16,128]{3,2,1,0:T(8,128)}, u32[]{:S(2)}) copy-start(f32[3,132,16,128]{3,2,1,0:T(8,128)} %fields.2) | copy-start | bytes 9732100
  1.9 14.7 %collective-permute-start = (f32[3,2,128,128]{3,2,1,0:T(8,128)S(1)}, f32[3,2,128,128]{3,2,1,0:T(8,128)S(1)}, u32[]{:S(2)}, u32[]{:S(2)}) collective-permute-start(f32[3,2,128,128]{3,2,1,0:T(8,128)S(1)} %far_face.1), channel_id=1, source_target_pairs={{0,24},{8,16},{16,8},{24,0},{1,25},{9,17},{17,9},{25,1},{2,26},{10... | collective-permute-start | bytes 1179656 | tf_op jit(solution)/shard_map/ppermute | solution.py:456
  5.9 8.7 %collective-permute-start.1 = (f32[3,128,128]{2,1,0:T(8,128)S(1)}, f32[3,128,128]{2,1,0:T(8,128)S(1)}, u32[]{:S(2)}, u32[]{:S(2)}) collective-permute-start(f32[3,128,128]{2,1,0:T(8,128)S(1)} %get-tuple-element.35), channel_id=1, source_target_pairs={{0,8},{8,0},{16,24},{24,16},{1,9},{9,1},{17,25},{25,17},{2,10},{10... | collective-permute-start | bytes 589832 | tf_op jit(solution)/shard_map/ppermute | solution.py:473
  6.7 8.0 %collective-permute-start.2 = (f32[3,128,128]{2,1,0:T(8,128)S(1)}, f32[3,128,128]{2,1,0:T(8,128)S(1)}, u32[]{:S(2)}, u32[]{:S(2)}) collective-permute-start(f32[3,128,128]{2,1,0:T(8,128)S(1)} %get-tuple-element.36), channel_id=1, source_target_pairs={{0,8},{8,0},{16,24},{24,16},{1,9},{9,1},{17,25},{25,17},{2,10},{10... | collective-permute-start | bytes 589832 | tf_op jit(solution)/shard_map/ppermute | solution.py:473
  6.7 7.9 %collective-permute-start.3 = (f32[128,128]{1,0:T(8,128)S(1)}, f32[128,128]{1,0:T(8,128)S(1)}, u32[]{:S(2)}, u32[]{:S(2)}) collective-permute-start(f32[128,128]{1,0:T(8,128)S(1)} %get-tuple-element.37), channel_id=1, source_target_pairs={{0,1},{1,2},{2,3},{3,4},{4,5},{5,6},{6,7},{7,0},{8,9},{9,10},{10,1... | collective-permute-start | bytes 196616 | tf_op jit(solution)/shard_map/ppermute | solution.py:474
  8.2 6.4 %collective-permute-start.4 = (f32[128,128]{1,0:T(8,128)S(1)}, f32[128,128]{1,0:T(8,128)S(1)}, u32[]{:S(2)}, u32[]{:S(2)}) collective-permute-start(f32[128,128]{1,0:T(8,128)S(1)} %get-tuple-element.38), channel_id=1, source_target_pairs={{0,7},{1,0},{2,1},{3,2},{4,3},{5,4},{6,5},{7,6},{8,15},{9,8},{10,9... | collective-permute-start | bytes 196616 | tf_op jit(solution)/shard_map/ppermute | solution.py:475
  17.3 1.3 %collective-permute-start.5 = (f32[168,128]{1,0:T(8,128)S(1)}, f32[168,128]{1,0:T(8,128)S(1)}, u32[]{:S(2)}, u32[]{:S(2)}) collective-permute-start(f32[168,128]{1,0:T(8,128)S(1)} %get-tuple-element.44), channel_id=1, source_target_pairs={{0,8},{1,9},{2,10},{3,11},{4,12},{5,13},{6,14},{7,15},{8,0},{9,1},... | collective-permute-start | bytes 258056 | tf_op jit(solution)/shard_map/ppermute | solution.py:419
  18.7 5.4 %collective-permute-start.8 = (f32[168,128]{1,0:T(8,128)S(1)}, f32[168,128]{1,0:T(8,128)S(1)}, u32[]{:S(2)}, u32[]{:S(2)}) collective-permute-start(f32[168,128]{1,0:T(8,128)S(1)} %add.21), channel_id=1, source_target_pairs={{0,17},{1,16},{2,19},{3,18},{4,21},{5,20},{6,23},{7,22},{8,14},{9,... | collective-permute-start | bytes 258056 | tf_op jit(solution)/shard_map/ppermute | solution.py:419
  19.6 5.1 %collective-permute-start.7 = (f32[168,128]{1,0:T(8,128)S(1)}, f32[168,128]{1,0:T(8,128)S(1)}, u32[]{:S(2)}, u32[]{:S(2)}) collective-permute-start(f32[168,128]{1,0:T(8,128)S(1)} %add.21), channel_id=1, source_target_pairs={{0,1},{1,0},{2,3},{3,2},{4,5},{5,4},{6,7},{7,6},{8,12},{9,13},{10,... | collective-permute-start | bytes 258056 | tf_op jit(solution)/shard_map/ppermute | solution.py:419
  21.3 4.5 %collective-permute-start.6 = (f32[168,128]{1,0:T(8,128)S(1)}, f32[168,128]{1,0:T(8,128)S(1)}, u32[]{:S(2)}, u32[]{:S(2)}) collective-permute-start(f32[168,128]{1,0:T(8,128)S(1)} %add.21), channel_id=1, source_target_pairs={{0,16},{1,17},{2,18},{3,19},{4,20},{5,21},{6,22},{7,23},{8,10},{9,... | collective-permute-start | bytes 258056 | tf_op jit(solution)/shard_map/ppermute | solution.py:419
  25.8 6.4 %collective-permute-start.11 = (f32[168,128]{1,0:T(8,128)S(1)}, f32[168,128]{1,0:T(8,128)S(1)}, u32[]{:S(2)}, u32[]{:S(2)}) collective-permute-start(f32[168,128]{1,0:T(8,128)S(1)} %add_add_fusion.1), channel_id=1, source_target_pairs={{0,6},{1,7},{2,4},{3,5},{4,2},{5,3},{6,0},{7,1},{8,25},{9,24},{10,... | collective-permute-start | bytes 258056 | tf_op jit(solution)/shard_map/ppermute | solution.py:419
  28.2 5.8 %collective-permute-start.10 = (f32[168,128]{1,0:T(8,128)S(1)}, f32[168,128]{1,0:T(8,128)S(1)}, u32[]{:S(2)}, u32[]{:S(2)}) collective-permute-start(f32[168,128]{1,0:T(8,128)S(1)} %add_add_fusion.1), channel_id=1, source_target_pairs={{0,4},{1,5},{2,6},{3,7},{4,0},{5,1},{6,2},{7,3},{8,9},{9,8},{10,11... | collective-permute-start | bytes 258056 | tf_op jit(solution)/shard_map/ppermute | solution.py:419
  28.2 5.8 %collective-permute-start.9 = (f32[168,128]{1,0:T(8,128)S(1)}, f32[168,128]{1,0:T(8,128)S(1)}, u32[]{:S(2)}, u32[]{:S(2)}) collective-permute-start(f32[168,128]{1,0:T(8,128)S(1)} %add_add_fusion.1), channel_id=1, source_target_pairs={{0,2},{1,3},{2,0},{3,1},{4,6},{5,7},{6,4},{7,5},{8,24},{9,25},{10,... | collective-permute-start | bytes 258056 | tf_op jit(solution)/shard_map/ppermute | solution.py:419
  34.0 1.3 %collective-permute-start.12 = (f32[168,128]{1,0:T(8,128)S(1)}, f32[168,128]{1,0:T(8,128)S(1)}, u32[]{:S(2)}, u32[]{:S(2)}) collective-permute-start(f32[168,128]{1,0:T(8,128)S(1)} %add_add_fusion.kept), channel_id=1, source_target_pairs={{0,8},{1,9},{2,10},{3,11},{4,12},{5,13},{6,14},{7,15},{8,0},{9,1},... | collective-permute-start | bytes 258056 | tf_op jit(solution)/shard_map/ppermute | solution.py:419

commit v9 on v8

--- a/solution.py
+++ b/solution.py
@@ -81,13 +81,14 @@
     for layer in range(2):
         for c in range(3):
             source = fields.at[c, pl.ds(2, planes), first + layer, :]
-            copies.append(pltpu.make_async_copy(source, far.at[c, layer], arrived.at[layer, c]))
+            copies.append(pltpu.make_async_copy(source, far.at[pl.ds((3 * layer + c) * planes, planes)], arrived.at[layer, c]))
             copies[-1].start()
+    far[6 * planes :, :] = jnp.zeros((far.shape[0] - 6 * planes, far.shape[1]), jnp.float32)
     for copy in copies:
         copy.wait()
 
 
-def faces_kernel(rows, planes, fields, turned_fields, near_0, near_1, behind, ahead, tails, heads):
+def faces_kernel(rows, planes, fields, turned_fields, near, behind, ahead, tails, heads):
     odd = lax.axis_index("gy") % 2
     size = fields.shape[3]
     depth = planes + 4
@@ -118,8 +119,8 @@
 
         if depth % 8:
             turn(c, depth - 8)
-        for layer, near in enumerate((near_0, near_1)):
-            near[c] = turned_fields[c, near_row + layer, 2 : planes + 2, :]
+        for layer in range(2):
+            near[layer, c] = turned_fields[c, near_row + layer, 2 : planes + 2, :]
     ahead[...] = tails[2 : planes + 2, :]
     behind[...] = heads[2 : planes + 2, :]
 
@@ -233,7 +234,7 @@
 
     def window(c):
         own = [fields[c, jnp.where(lower, 0, rows - 4) + i, within, :] for i in range(4)]
-        ends = [halo[i][c, at, :] for i in range(2)]
+        ends = [halo[i][c][at, :] for i in range(2)]
         before = [jnp.where(lower, ends[i], own[i]) for i in range(2)]
         centre = [jnp.where(lower, own[i], own[i + 2]) for i in range(2)]
         after = [jnp.where(lower, own[i + 2], ends[i]) for i in range(2)]
@@ -252,7 +253,7 @@
 
 
 def interior_kernel(
-    rows, planes, fields, own_z, spin, stretch, bend_x, bend_y, near_0, near_1, left, right, out, total, to_last, to_first, pieces
+    rows, planes, fields, own_z, spin, stretch, bend_x, bend_y, near, left, right, out, total, to_last, to_first, pieces
 ):
     size = own_z.shape[3]
     odd = lax.axis_index("gy") % 2 == 1
@@ -267,7 +268,7 @@
                     planar = [ref[index, t * TILE : (t + 1) * TILE, :] for ref in (spin, stretch, bend_x, bend_y)]
                     store_results(finish(*planar, z), out, index, buffer, half, t, planes, size)
             else:
-                for half, results in beside_face(rows, planes, fields, own_z, [near_0, near_1], odd, to_last, to_first, t):
+                for half, results in beside_face(rows, planes, fields, own_z, [[near.at[i, c] for c in range(3)] for i in range(2)], odd, to_last, to_first, t):
                     store_results(results, out, 2 * pair + half, buffer, half, t, planes, size)
         for f in range(2):
             product = square(buffer[f])
@@ -279,8 +280,9 @@
 ):
     size = fields.shape[3]
     odd = lax.axis_index("gy") % 2 == 1
+    halo = [[far.at[pl.ds((3 * i + c) * planes, planes)] for c in range(3)] for i in range(2)]
     for t in range(planes // TILE):
-        for half, results in beside_face(rows, planes, fields, own_z, [far.at[:, i] for i in range(2)], ~odd, to_last, to_first, t):
+        for half, results in beside_face(rows, planes, fields, own_z, halo, ~odd, to_last, to_first, t):
             store_results(results, out, half, pieces, half, t, planes, size)
     grams = [gram_of(part[f] + square(pieces[f])) for f in range(2)] + [velocity[c] for c in range(3)]
     message[0:planes, :] = pack_pair(grams[0], grams[1])
@@ -444,7 +446,7 @@
 
     far = pl.pallas_call(
         functools.partial(far_kernel, rows, planes),
-        out_shape=f32(3, 2, planes, cols),
+        out_shape=f32(6 * planes + 8, cols),
         in_specs=[pl.BlockSpec(memory_space=pl.ANY)],
         out_specs=VMEM,
         scratch_shapes=[pltpu.SemaphoreType.DMA((2, 3))],
@@ -454,23 +456,22 @@
     )(pltpu.with_memory_space_constraint(fields, pltpu.HBM))
     fields, far = lax.optimization_barrier((fields, far))
     far = lax.ppermute(far, "gy", [(i, (i + 1 if i % 2 else i - 1) % count_y) for i in range(count_y)])
-    turned, near_0, near_1, behind, ahead = pl.pallas_call(
+    turned, near, behind, ahead = pl.pallas_call(
         functools.partial(faces_kernel, rows, planes),
         out_shape=(
             pltpu.VMEM((3, rows, planes + 4, cols), jnp.float32),
-            f32(3, planes, cols),
-            f32(3, planes, cols),
+            f32(2, 3, planes, cols),
             f32(planes, cols),
             f32(planes, cols),
         ),
         in_specs=[VMEM],
-        out_specs=(VMEM,) * 5,
+        out_specs=(VMEM,) * 4,
         scratch_shapes=[pltpu.VMEM((planes + 4, cols), jnp.float32)] * 2,
         compiler_params=params(),
         cost_estimate=cost(2.5),
         name="faces",
     )(pltpu.with_memory_space_constraint(fields, pltpu.VMEM))
-    near = [lax.ppermute(layer, "gy", [(i, i ^ 1) for i in range(count_y)]) for layer in (near_0, near_1)]
+    near = lax.ppermute(near, "gy", [(i, i ^ 1) for i in range(count_y)])
     left = lax.ppermute(ahead, "gz", [(i, (i + 1) % count_z) for i in range(count_z)])
     right = lax.ppermute(behind, "gz", [(i, (i - 1) % count_z) for i in range(count_z)])
 
@@ -497,13 +498,13 @@
             f32(planes, cols),
             f32(planes, cols),
         ),
-        in_specs=[VMEM] * 10,
+        in_specs=[VMEM] * 9,
         out_specs=(VMEM,) * 4,
         scratch_shapes=[pieces],
         compiler_params=params(),
-        cost_estimate=cost(1.9),
+        cost_estimate=cost(0),
         name="interior",
-    )(turned, own_z, *planar, *near, left, right)
+    )(turned, own_z, *planar, near, left, right)
     half = -(-(5 * planes // 2 + 8) // 16) * 8
     message = pltpu.VMEM((2 * half, planes), jnp.float32)
     border, keep, give = pl.pallas_call(

time: 39.2 us -> 38.8 us (0.990)
    ppermute x2 -> x1, starting transfers between devices: 0.82 us -> 0.74 us  [per_device(): near = lax.ppermute(near, 'gy', [(i, i ^ 1) for i in range(count_y)])]
  transfers between devices with their start and end apart: 13 -> 12, of which waited for: 7 -> 7; matrix products, arithmetic and copies ran while one was open for 0% -> 0% of each run, Pallas kernels for 24% -> 24%
where the time goes in v9:
time: 38.8 us; the launch traced here: 38.6 us
  starting transfers between devices  16.1 us (41%)
  Pallas kernels  14.8 us (38%)
  waiting for transfers between devices  6.96 us (18%)
  between operations  0.72 us (2%)
    ppermute x8, starting transfers between devices, exchange(): lax.ppermute(values, AXES, [(i, i ^ (odd if i // count_z % 2 else even))...  8.14 us
    ppermute x8, waiting for transfers between devices, exchange(): lax.ppermute(values, AXES, [(i, i ^ (odd if i // count_z % 2 else even))...  6.95 us
    pallas_call x1, Pallas kernels, per_device(): pl.pallas_call(functools.partial(factor_kernel, float(cells), planes), ou...  3.66 us
    ppermute x1, starting transfers between devices, per_device(): lax.ppermute(behind, 'gz', [(i, (i - 1) % count_z) for i in range(count_z)])  3.23 us
    pallas_call x1, Pallas kernels, per_device(): pl.pallas_call(functools.partial(inner_kernel, rows, planes), out_shape=(...  3.12 us
    pallas_call x2, Pallas kernels, per_device(): pl.pallas_call(functools.partial(assemble_kernel, rows, planes, f), out_s...  2.55 us
    ppermute x1, starting transfers between devices, per_device(): lax.ppermute(far, 'gy', [(i, (i + 1 if i % 2 else i - 1) % count_y) for i...  2.47 us
    pallas_call x1, Pallas kernels, per_device(): pl.pallas_call(functools.partial(interior_kernel, rows, planes), out_shap...  1.98 us
  transfers between devices with their start and end apart: 12, of which 7 were waited for; matrix products, arithmetic and copies ran while one was open for 0% of the time, Pallas kernels for 24%

profile of v9, /device:TPU:0, one launch (start us, length us, event | category | flops | bytes accessed | tf_op | source)
XLA Modules:
  0.0 38.6 jit_solution(310854653162927178)
XLA Ops:
  0.6 1.3 %far_face.1 = f32[776,128]{1,0:T(8,128)S(1)} custom-call(f32[3,132,16,128]{3,2,1,0:T(8,128)} %fields.2), custom_call_target="tpu_custom_call" | custom-call | bytes 3690000 | tf_op jit(solution)/shard_map/far_face/pallas_call | solution.py:447
  1.9 2.5 %collective-permute-start = (f32[776,128]{1,0:T(8,128)S(1)}, f32[776,128]{1,0:T(8,128)S(1)}, u32[]{:S(2)}, u32[]{:S(2)}) collective-permute-start(f32[776,128]{1,0:T(8,128)S(1)} %far_face.1), channel_id=1, source_target_pairs={{0,24},{8,16},{16,8},{24,0},{1,25},{9,17},{17,9},{25,1},{2,26},{10... | collective-permute-start | bytes 1191944 | tf_op jit(solution)/shard_map/ppermute | solution.py:458
  4.4 1.6 %faces.1 = (f32[3,16,132,128]{3,2,1,0:T(8,128)S(1)}, f32[2,3,128,128]{3,2,1,0:T(8,128)S(1)}, f32[128,128]{1,0:T(8,128)S(1)}, f32[128,128]{1,0:T(8,128)S(1)}) custom-call(f32[3,132,16,128]{3,2,1,0:T(8,128)S(1)} %copy-done), custom_call_target="tpu_custom_call" | custom-call | bytes 9225000 | tf_op jit(solution)/shard_map/faces/pallas_call | solution.py:459
  5.9 0.7 %collective-permute-start.1 = (f32[2,3,128,128]{3,2,1,0:T(8,128)S(1)}, f32[2,3,128,128]{3,2,1,0:T(8,128)S(1)}, u32[]{:S(2)}, u32[]{:S(2)}) collective-permute-start(f32[2,3,128,128]{3,2,1,0:T(8,128)S(1)} %get-tuple-element.34), channel_id=1, source_target_pairs={{0,8},{8,0},{16,24},{24,16},{1,9},{9,1},{17,25},{25,17},{2,10},{10... | collective-permute-start | bytes 1179656 | tf_op jit(solution)/shard_map/ppermute | solution.py:474
  6.7 1.5 %collective-permute-start.2 = (f32[128,128]{1,0:T(8,128)S(1)}, f32[128,128]{1,0:T(8,128)S(1)}, u32[]{:S(2)}, u32[]{:S(2)}) collective-permute-start(f32[128,128]{1,0:T(8,128)S(1)} %get-tuple-element.35), channel_id=1, source_target_pairs={{0,1},{1,2},{2,3},{3,4},{4,5},{5,6},{6,7},{7,0},{8,9},{9,10},{10,1... | collective-permute-start | bytes 196616 | tf_op jit(solution)/shard_map/ppermute | solution.py:475
  8.2 3.2 %collective-permute-start.3 = (f32[128,128]{1,0:T(8,128)S(1)}, f32[128,128]{1,0:T(8,128)S(1)}, u32[]{:S(2)}, u32[]{:S(2)}) collective-permute-start(f32[128,128]{1,0:T(8,128)S(1)} %get-tuple-element.36), channel_id=1, source_target_pairs={{0,7},{1,0},{2,1},{3,2},{4,3},{5,4},{6,5},{7,6},{8,15},{9,8},{10,9... | collective-permute-start | bytes 196616 | tf_op jit(solution)/shard_map/ppermute | solution.py:476
  11.4 3.1 %inner.1 = (f32[3,128,128]{2,1,0:T(8,128)S(1)}, f32[3,16,128,128]{3,2,1,0:T(8,128)S(1)}, f32[12,128,128]{2,1,0:T(8,128)S(1)}, f32[12,128,128]{2,1,0:T(8,128)S(1)...) custom-call(f32[3,16,132,128]{3,2,1,0:T(8,128)S(1)} %get-tuple-element.27.fields), custom_call_target="tpu_custom_call" | custom-call | bytes 11070000 | tf_op jit(solution)/shard_map/inner/pallas_call | solution.py:479
  14.6 2.0 %interior.1 = (f32[2,14,128,128]{3,2,1,0:T(8,128)S(1)}, f32[2,256,256]{2,1,0:T(8,128)S(1)}, f32[128,128]{1,0:T(8,128)S(1)}, f32[128,128]{1,0:T(8,128)S(1)}) custom-call(f32[3,16,132,128]{3,2,1,0:T(8,128)S(1)} %get-tuple-element.27.fields, f32[3,16,128,128]{3,2,1,0:T(8,128)S(1)} %get-tuple-element.28.own_z, f32[12,128,128]{2,1,0:T(8,128)S(1)} %get-tuple-element.30.spin, ...), custom_call_target="tpu_custom_call" | custom-call | tf_op jit(solution)/shard_map/interior/pallas_call | solution.py:493
  16.5 0.7 %border.1 = (f32[2,2,128,128]{3,2,1,0:T(8,128)S(1)}, f32[168,128]{1,0:T(8,128)S(1)}, f32[168,128]{1,0:T(8,128)S(1)}) custom-call(f32[3,16,132,128]{3,2,1,0:T(8,128)S(1)} %get-tuple-element.27.fields, f32[3,16,128,128]{3,2,1,0:T(8,128)S(1)} %get-tuple-element.28.own_z, f32[776,128]{1,0:T(8,128)S(1)} %collective-permute-done.far, ...), custom_call_target="tpu_custom_call" | custom-call | bytes 2583000 | tf_op jit(solution)/shard_map/border/pallas_call | solution.py:510
  17.3 1.3 %collective-permute-done.4 = f32[168,128]{1,0:T(8,128)S(1)} collective-permute-done((f32[168,128]{1,0:T(8,128)S(1)}, f32[168,128]{1,0:T(8,128)S(1)}, u32[]{:S(2)}, u32[]{:S(2)}) %collective-permute-start.4) | collective-permute-done | bytes 86048 | tf_op jit(solution)/shard_map/ppermute | solution.py:421
  18.6 0.9 %collective-permute-start.7 = (f32[168,128]{1,0:T(8,128)S(1)}, f32[168,128]{1,0:T(8,128)S(1)}, u32[]{:S(2)}, u32[]{:S(2)}) collective-permute-start(f32[168,128]{1,0:T(8,128)S(1)} %add.21), channel_id=1, source_target_pairs={{0,17},{1,16},{2,19},{3,18},{4,21},{5,20},{6,23},{7,22},{8,14},{9,... | collective-permute-start | bytes 258056 | tf_op jit(solution)/shard_map/ppermute | solution.py:421
  19.4 1.4 %collective-permute-start.6 = (f32[168,128]{1,0:T(8,128)S(1)}, f32[168,128]{1,0:T(8,128)S(1)}, u32[]{:S(2)}, u32[]{:S(2)}) collective-permute-start(f32[168,128]{1,0:T(8,128)S(1)} %add.21), channel_id=1, source_target_pairs={{0,1},{1,0},{2,3},{3,2},{4,5},{5,4},{6,7},{7,6},{8,12},{9,13},{10,... | collective-permute-start | bytes 258056 | tf_op jit(solution)/shard_map/ppermute | solution.py:421
  20.9 1.3 %collective-permute-start.5 = (f32[168,128]{1,0:T(8,128)S(1)}, f32[168,128]{1,0:T(8,128)S(1)}, u32[]{:S(2)}, u32[]{:S(2)}) collective-permute-start(f32[168,128]{1,0:T(8,128)S(1)} %add.21), channel_id=1, source_target_pairs={{0,16},{1,17},{2,18},{3,19},{4,20},{5,21},{6,22},{7,23},{8,10},{9,... | collective-permute-start | bytes 258056 | tf_op jit(solution)/shard_map/ppermute | solution.py:421
  22.1 1.3 %assemble.2 = f32[128,16,128]{2,1,0:T(8,128)} custom-call(f32[2,14,128,128]{3,2,1,0:T(8,128)S(1)} %get-tuple-element.43.inner, f32[2,2,128,128]{3,2,1,0:T(8,128)S(1)} %get-tuple-element.44.border), custom_call_target="tpu_custom_call" | custom-call | bytes 3690000 | tf_op jit(solution)/shard_map/assemble/pallas_call | solution.py:521
  23.4 0.6 %collective-permute-done.7 = f32[168,128]{1,0:T(8,128)S(1)} collective-permute-done((f32[168,128]{1,0:T(8,128)S(1)}, f32[168,128]{1,0:T(8,128)S(1)}, u32[]{:S(2)}, u32[]{:S(2)}) %collective-permute-start.7) | collective-permute-done | bytes 86048 | tf_op jit(solution)/shard_map/ppermute | solution.py:421
  24.0 0.2 collective-permute-done.6
  24.3 1.1 %collective-permute-done.5 = f32[168,128]{1,0:T(8,128)S(1)} collective-permute-done((f32[168,128]{1,0:T(8,128)S(1)}, f32[168,128]{1,0:T(8,128)S(1)}, u32[]{:S(2)}, u32[]{:S(2)}) %collective-permute-start.5) | collective-permute-done | bytes 86048 | tf_op jit(solution)/shard_map/ppermute | solution.py:421
  25.4 2.8 %collective-permute-start.10 = (f32[168,128]{1,0:T(8,128)S(1)}, f32[168,128]{1,0:T(8,128)S(1)}, u32[]{:S(2)}, u32[]{:S(2)}) collective-permute-start(f32[168,128]{1,0:T(8,128)S(1)} %add_add_fusion.1), channel_id=1, source_target_pairs={{0,6},{1,7},{2,4},{3,5},{4,2},{5,3},{6,0},{7,1},{8,25},{9,24},{10,... | collective-permute-start | bytes 258056 | tf_op jit(solution)/shard_map/ppermute | solution.py:421
  28.2 1.7 %collective-permute-start.8 = (f32[168,128]{1,0:T(8,128)S(1)}, f32[168,128]{1,0:T(8,128)S(1)}, u32[]{:S(2)}, u32[]{:S(2)}) collective-permute-start(f32[168,128]{1,0:T(8,128)S(1)} %add_add_fusion.1), channel_id=1, source_target_pairs={{0,2},{1,3},{2,0},{3,1},{4,6},{5,7},{6,4},{7,5},{8,24},{9,25},{10,... | collective-permute-start | bytes 258056 | tf_op jit(solution)/shard_map/ppermute | solution.py:421
  29.8 1.3 %assemble.3 = f32[128,16,128]{2,1,0:T(8,128)} custom-call(f32[2,14,128,128]{3,2,1,0:T(8,128)S(1)} %get-tuple-element.43.inner, f32[2,2,128,128]{3,2,1,0:T(8,128)S(1)} %get-tuple-element.44.border), custom_call_target="tpu_custom_call" | custom-call | bytes 3690000 | tf_op jit(solution)/shard_map/assemble/pallas_call | solution.py:521
  31.1 0.6 %collective-permute-done.10 = f32[168,128]{1,0:T(8,128)S(1)} collective-permute-done((f32[168,128]{1,0:T(8,128)S(1)}, f32[168,128]{1,0:T(8,128)S(1)}, u32[]{:S(2)}, u32[]{:S(2)}) %collective-permute-start.10) | collective-permute-done | bytes 86048 | tf_op jit(solution)/shard_map/ppermute | solution.py:421
  31.7 1.8 %collective-permute-done.9 = f32[168,128]{1,0:T(8,128)S(1)} collective-permute-done((f32[168,128]{1,0:T(8,128)S(1)}, f32[168,128]{1,0:T(8,128)S(1)}, u32[]{:S(2)}, u32[]{:S(2)}) %collective-permute-start.9) | collective-permute-done | bytes 86048 | tf_op jit(solution)/shard_map/ppermute | solution.py:421
  33.7 1.3 %collective-permute-done.11.given = f32[168,128]{1,0:T(8,128)S(1)} collective-permute-done((f32[168,128]{1,0:T(8,128)S(1)}, f32[168,128]{1,0:T(8,128)S(1)}, u32[]{:S(2)}, u32[]{:S(2)}) %collective-permute-start.11) | collective-permute-done | bytes 86048 | tf_op jit(solution)/shard_map/ppermute | solution.py:421
  35.0 3.7 %factor.1 = f32[128,128]{1,0:T(8,128)} custom-call(f32[168,128]{1,0:T(8,128)S(1)} %add_add_fusion.kept, f32[168,128]{1,0:T(8,128)S(1)} %collective-permute-done.11.given), custom_call_target="tpu_custom_call" | custom-call | bytes 22140000 | tf_op jit(solution)/shard_map/factor/pallas_call | solution.py:543
  (13 shorter events, 0.2 us)
Async XLA Ops:
  0.6 3.7 %copy-start = (f32[3,132,16,128]{3,2,1,0:T(8,128)S(1)}, f32[3,132,16,128]{3,2,1,0:T(8,128)}, u32[]{:S(2)}) copy-start(f32[3,132,16,128]{3,2,1,0:T(8,128)} %fields.2) | copy-start | bytes 9732100
  1.9 14.6 %collective-permute-start = (f32[776,128]{1,0:T(8,128)S(1)}, f32[776,128]{1,0:T(8,128)S(1)}, u32[]{:S(2)}, u32[]{:S(2)}) collective-permute-start(f32[776,128]{1,0:T(8,128)S(1)} %far_face.1), channel_id=1, source_target_pairs={{0,24},{8,16},{16,8},{24,0},{1,25},{9,17},{17,9},{25,1},{2,26},{10... | collective-permute-start | bytes 1191944 | tf_op jit(solution)/shard_map/ppermute | solution.py:458
  5.9 8.6 %collective-permute-start.1 = (f32[2,3,128,128]{3,2,1,0:T(8,128)S(1)}, f32[2,3,128,128]{3,2,1,0:T(8,128)S(1)}, u32[]{:S(2)}, u32[]{:S(2)}) collective-permute-start(f32[2,3,128,128]{3,2,1,0:T(8,128)S(1)} %get-tuple-element.34), channel_id=1, source_target_pairs={{0,8},{8,0},{16,24},{24,16},{1,9},{9,1},{17,25},{25,17},{2,10},{10... | collective-permute-start | bytes 1179656 | tf_op jit(solution)/shard_map/ppermute | solution.py:474
  6.7 7.9 %collective-permute-start.2 = (f32[128,128]{1,0:T(8,128)S(1)}, f32[128,128]{1,0:T(8,128)S(1)}, u32[]{:S(2)}, u32[]{:S(2)}) collective-permute-start(f32[128,128]{1,0:T(8,128)S(1)} %get-tuple-element.35), channel_id=1, source_target_pairs={{0,1},{1,2},{2,3},{3,4},{4,5},{5,6},{6,7},{7,0},{8,9},{9,10},{10,1... | collective-permute-start | bytes 196616 | tf_op jit(solution)/shard_map/ppermute | solution.py:475
  8.2 6.4 %collective-permute-start.3 = (f32[128,128]{1,0:T(8,128)S(1)}, f32[128,128]{1,0:T(8,128)S(1)}, u32[]{:S(2)}, u32[]{:S(2)}) collective-permute-start(f32[128,128]{1,0:T(8,128)S(1)} %get-tuple-element.36), channel_id=1, source_target_pairs={{0,7},{1,0},{2,1},{3,2},{4,3},{5,4},{6,5},{7,6},{8,15},{9,8},{10,9... | collective-permute-start | bytes 196616 | tf_op jit(solution)/shard_map/ppermute | solution.py:476
  17.2 1.3 %collective-permute-start.4 = (f32[168,128]{1,0:T(8,128)S(1)}, f32[168,128]{1,0:T(8,128)S(1)}, u32[]{:S(2)}, u32[]{:S(2)}) collective-permute-start(f32[168,128]{1,0:T(8,128)S(1)} %get-tuple-element.42), channel_id=1, source_target_pairs={{0,8},{1,9},{2,10},{3,11},{4,12},{5,13},{6,14},{7,15},{8,0},{9,1},... | collective-permute-start | bytes 258056 | tf_op jit(solution)/shard_map/ppermute | solution.py:421
  18.6 5.4 %collective-permute-start.7 = (f32[168,128]{1,0:T(8,128)S(1)}, f32[168,128]{1,0:T(8,128)S(1)}, u32[]{:S(2)}, u32[]{:S(2)}) collective-permute-start(f32[168,128]{1,0:T(8,128)S(1)} %add.21), channel_id=1, source_target_pairs={{0,17},{1,16},{2,19},{3,18},{4,21},{5,20},{6,23},{7,22},{8,14},{9,... | collective-permute-start | bytes 258056 | tf_op jit(solution)/shard_map/ppermute | solution.py:421
  19.4 4.8 %collective-permute-start.6 = (f32[168,128]{1,0:T(8,128)S(1)}, f32[168,128]{1,0:T(8,128)S(1)}, u32[]{:S(2)}, u32[]{:S(2)}) collective-permute-start(f32[168,128]{1,0:T(8,128)S(1)} %add.21), channel_id=1, source_target_pairs={{0,1},{1,0},{2,3},{3,2},{4,5},{5,4},{6,7},{7,6},{8,12},{9,13},{10,... | collective-permute-start | bytes 258056 | tf_op jit(solution)/shard_map/ppermute | solution.py:421
  20.9 4.5 %collective-permute-start.5 = (f32[168,128]{1,0:T(8,128)S(1)}, f32[168,128]{1,0:T(8,128)S(1)}, u32[]{:S(2)}, u32[]{:S(2)}) collective-permute-start(f32[168,128]{1,0:T(8,128)S(1)} %add.21), channel_id=1, source_target_pairs={{0,16},{1,17},{2,18},{3,19},{4,20},{5,21},{6,22},{7,23},{8,10},{9,... | collective-permute-start | bytes 258056 | tf_op jit(solution)/shard_map/ppermute | solution.py:421
  25.4 6.3 %collective-permute-start.10 = (f32[168,128]{1,0:T(8,128)S(1)}, f32[168,128]{1,0:T(8,128)S(1)}, u32[]{:S(2)}, u32[]{:S(2)}) collective-permute-start(f32[168,128]{1,0:T(8,128)S(1)} %add_add_fusion.1), channel_id=1, source_target_pairs={{0,6},{1,7},{2,4},{3,5},{4,2},{5,3},{6,0},{7,1},{8,25},{9,24},{10,... | collective-permute-start | bytes 258056 | tf_op jit(solution)/shard_map/ppermute | solution.py:421
  28.1 5.4 %collective-permute-start.9 = (f32[168,128]{1,0:T(8,128)S(1)}, f32[168,128]{1,0:T(8,128)S(1)}, u32[]{:S(2)}, u32[]{:S(2)}) collective-permute-start(f32[168,128]{1,0:T(8,128)S(1)} %add_add_fusion.1), channel_id=1, source_target_pairs={{0,4},{1,5},{2,6},{3,7},{4,0},{5,1},{6,2},{7,3},{8,9},{9,8},{10,11... | collective-permute-start | bytes 258056 | tf_op jit(solution)/shard_map/ppermute | solution.py:421
  28.2 5.4 %collective-permute-start.8 = (f32[168,128]{1,0:T(8,128)S(1)}, f32[168,128]{1,0:T(8,128)S(1)}, u32[]{:S(2)}, u32[]{:S(2)}) collective-permute-start(f32[168,128]{1,0:T(8,128)S(1)} %add_add_fusion.1), channel_id=1, source_target_pairs={{0,2},{1,3},{2,0},{3,1},{4,6},{5,7},{6,4},{7,5},{8,24},{9,25},{10,... | collective-permute-start | bytes 258056 | tf_op jit(solution)/shard_map/ppermute | solution.py:421
  33.6 1.3 %collective-permute-start.11 = (f32[168,128]{1,0:T(8,128)S(1)}, f32[168,128]{1,0:T(8,128)S(1)}, u32[]{:S(2)}, u32[]{:S(2)}) collective-permute-start(f32[168,128]{1,0:T(8,128)S(1)} %add_add_fusion.kept), channel_id=1, source_target_pairs={{0,8},{1,9},{2,10},{3,11},{4,12},{5,13},{6,14},{7,15},{8,0},{9,1},... | collective-permute-start | bytes 258056 | tf_op jit(solution)/shard_map/ppermute | solution.py:421

commit v10 on v9

--- a/solution.py
+++ b/solution.py
@@ -113,7 +113,7 @@
 
     for c in range(3):
 
-        @pl.loop(0, depth // 8, unroll=8)
+        @pl.loop(0, depth // 8, unroll=16)
         def _(t):
             turn(c, pl.multiple_of(t * 8, 8))
 
@@ -227,7 +227,11 @@
         pieces[f, lower, half * size : (half + 1) * size] = low
 
 
-def beside_face(rows, planes, fields, own_z, halo, lower, to_last, to_first, t):
+def x_derivatives(fields, t, y):
+    return [derivative(*[fields[c, y, pl.ds(2 + t * TILE + k, TILE), :] for k in (-2, -1, 1, 2)]) for c in range(3)]
+
+
+def beside_face(rows, fields, halo, lower, t, x_and_z):
     at = pl.ds(t * TILE, TILE)
     within = pl.ds(2 + t * TILE, TILE)
     first = jnp.where(lower, 0, rows - 2)
@@ -242,9 +246,7 @@
 
     windows = [window(c) for c in range(3)]
     for i in range(2):
-        y = first + i
-        z = z_derivatives(own_z, to_last, to_first, t, y, rows)
-        along_x = [derivative(*[fields[c, y, pl.ds(2 + t * TILE + k, TILE), :] for k in (-2, -1, 1, 2)]) for c in range(3)]
+        along_x, z = x_and_z(i, first + i)
         along_y = [derivative(*[windows[c][2 + i + k] for k in (-2, -1, 1, 2)]) for c in range(3)]
         turn = along_x[1] - along_y[0]
         shear = along_x[1] + along_y[0]
@@ -253,7 +255,8 @@
 
 
 def interior_kernel(
-    rows, planes, fields, own_z, spin, stretch, bend_x, bend_y, near, left, right, out, total, to_last, to_first, pieces
+    rows, planes, fields, own_z, spin, stretch, bend_x, bend_y, near, left, right, velocity,
+    out, total, beside, packed, pieces, to_last, to_first
 ):
     size = own_z.shape[3]
     odd = lax.axis_index("gy") % 2 == 1
@@ -268,30 +271,46 @@
                     planar = [ref[index, t * TILE : (t + 1) * TILE, :] for ref in (spin, stretch, bend_x, bend_y)]
                     store_results(finish(*planar, z), out, index, buffer, half, t, planes, size)
             else:
-                for half, results in beside_face(rows, planes, fields, own_z, [[near.at[i, c] for c in range(3)] for i in range(2)], odd, to_last, to_first, t):
+                halo = [[near.at[i, c] for c in range(3)] for i in range(2)]
+
+                def x_and_z(i, y):
+                    return x_derivatives(fields, t, y), z_derivatives(own_z, to_last, to_first, t, y, rows)
+
+                for half, results in beside_face(rows, fields, halo, odd, t, x_and_z):
                     store_results(results, out, 2 * pair + half, buffer, half, t, planes, size)
+                for i in range(2):
+                    ready = x_and_z(i, jnp.where(odd, rows - 2, 0) + i)
+                    for c in range(3):
+                        beside[i, 0, c, t * TILE : (t + 1) * TILE, :] = ready[0][c]
+                        beside[i, 1, c, t * TILE : (t + 1) * TILE, :] = ready[1][c]
         for f in range(2):
             product = square(buffer[f])
             total[f] = product if pair == 0 else total[f] + product
-
-
-def border_kernel(
-    rows, planes, fields, own_z, far, to_last, to_first, part, velocity, out, keep, give, message, pieces
-):
+    packed[0:planes, :] = pack_pair(velocity[0], velocity[1])
+    packed[planes : 3 * planes // 2, :] = fold(velocity[2])
+    diagonals = [diagonal(velocity[c]) for c in range(3)]
+    packed[3 * planes // 2 :, :] = jnp.concatenate(diagonals + [jnp.zeros((5, planes), jnp.float32)], axis=0)
+
+
+def border_kernel(rows, planes, fields, far, beside, part, packed, out, keep, give, message, pieces):
     size = fields.shape[3]
     odd = lax.axis_index("gy") % 2 == 1
     halo = [[far.at[pl.ds((3 * i + c) * planes, planes)] for c in range(3)] for i in range(2)]
     for t in range(planes // TILE):
-        for half, results in beside_face(rows, planes, fields, own_z, halo, ~odd, to_last, to_first, t):
+
+        def x_and_z(i, y):
+            return [[beside[i, way, c, t * TILE : (t + 1) * TILE, :] for c in range(3)] for way in range(2)]
+
+        for half, results in beside_face(rows, fields, halo, ~odd, t, x_and_z):
             store_results(results, out, half, pieces, half, t, planes, size)
-    grams = [gram_of(part[f] + square(pieces[f])) for f in range(2)] + [velocity[c] for c in range(3)]
+    grams = [gram_of(part[f] + square(pieces[f])) for f in range(2)]
     message[0:planes, :] = pack_pair(grams[0], grams[1])
-    message[planes : 2 * planes, :] = pack_pair(grams[2], grams[3])
-    message[2 * planes : 5 * planes // 2, :] = fold(grams[4])
-    for i, gram in enumerate(grams):
-        message[5 * planes // 2 + i : 5 * planes // 2 + i + 1, :] = diagonal(gram)
-    used = 5 * planes // 2 + 5
-    message[used:, :] = jnp.zeros((message.shape[0] - used, planes), jnp.float32)
+    message[planes : 5 * planes // 2, :] = packed[0 : 3 * planes // 2, :]
+    used = 5 * planes // 2
+    message[used : used + 2, :] = jnp.concatenate([diagonal(grams[0]), diagonal(grams[1])], axis=0)
+    message[used + 2 : used + 8, :] = packed[3 * planes // 2 : 3 * planes // 2 + 6, :]
+    if message.shape[0] > used + 8:
+        message[used + 8 :, :] = jnp.zeros((message.shape[0] - used - 8, planes), jnp.float32)
     mine, other = half_starts(keep.shape[0])
     keep[...] = message[pl.ds(mine, keep.shape[0]), :]
     give[...] = message[pl.ds(other, keep.shape[0]), :]
@@ -490,33 +509,33 @@
         name="inner",
     )(turned)
     pieces = pltpu.VMEM((2, 2, 2 * planes, 2 * cols), jnp.bfloat16)
-    inner, part, to_last, to_first = pl.pallas_call(
+    inner, part, beside, packed = pl.pallas_call(
         functools.partial(interior_kernel, rows, planes),
         out_shape=(
             f32(2, rows - 2, planes, cols),
             f32(2, 2 * planes, 2 * planes),
-            f32(planes, cols),
-            f32(planes, cols),
+            pltpu.VMEM((2, 2, 3, planes, cols), jnp.float32),
+            f32(3 * planes // 2 + 8, planes),
         ),
-        in_specs=[VMEM] * 9,
+        in_specs=[VMEM] * 10,
         out_specs=(VMEM,) * 4,
-        scratch_shapes=[pieces],
+        scratch_shapes=[pieces, pltpu.VMEM((planes, cols), jnp.float32), pltpu.VMEM((planes, cols), jnp.float32)],
         compiler_params=params(),
         cost_estimate=cost(0),
         name="interior",
-    )(turned, own_z, *planar, near, left, right)
+    )(turned, own_z, *planar, near, left, right, velocity)
     half = -(-(5 * planes // 2 + 8) // 16) * 8
     message = pltpu.VMEM((2 * half, planes), jnp.float32)
     border, keep, give = pl.pallas_call(
         functools.partial(border_kernel, rows, planes),
         out_shape=(f32(2, 2, planes, cols), f32(half, planes), f32(half, planes)),
-        in_specs=[VMEM] * 7,
+        in_specs=[VMEM] * 5,
         out_specs=(VMEM, VMEM, VMEM),
         scratch_shapes=[message, pltpu.VMEM((2, 2 * planes, 2 * cols), jnp.bfloat16)],
         compiler_params=params(),
         cost_estimate=cost(0.7),
         name="border",
-    )(turned, own_z, far, to_last, to_first, part, velocity)
+    )(turned, far, beside, part, packed)
     enstrophy, strain_rate = [
         pl.pallas_call(
             functools.partial(assemble_kernel, rows, planes, f),

time: 38.8 us -> 38.6 us (level)
    pallas_call x1, Pallas kernels: 1.55 us -> 0.99 us  [per_device(): pl.pallas_call(functools.partial(faces_kernel, rows, planes), out_shape=(...]
    pallas_call x1, Pallas kernels: 3.12 us -> 3.52 us  [per_device(): pl.pallas_call(functools.partial(inner_kernel, rows, planes), out_shape=(...]
where the time goes in v10:
time: 38.6 us; the launch traced here: 38.5 us
  starting transfers between devices  16.1 us (42%)
  Pallas kernels  14.6 us (38%)
  waiting for transfers between devices  6.99 us (18%)
  between operations  0.72 us (2%)
    ppermute x8, starting transfers between devices, exchange(): lax.ppermute(values, AXES, [(i, i ^ (odd if i // count_z % 2 else even))...  8.15 us
    ppermute x8, waiting for transfers between devices, exchange(): lax.ppermute(values, AXES, [(i, i ^ (odd if i // count_z % 2 else even))...  6.98 us
    pallas_call x1, Pallas kernels, per_device(): pl.pallas_call(functools.partial(factor_kernel, float(cells), planes), ou...  3.66 us
    pallas_call x1, Pallas kernels, per_device(): pl.pallas_call(functools.partial(inner_kernel, rows, planes), out_shape=(...  3.52 us
    ppermute x1, starting transfers between devices, per_device(): lax.ppermute(behind, 'gz', [(i, (i - 1) % count_z) for i in range(count_z)])  3.23 us
    pallas_call x2, Pallas kernels, per_device(): pl.pallas_call(functools.partial(assemble_kernel, rows, planes, f), out_s...  2.55 us
    ppermute x1, starting transfers between devices, per_device(): lax.ppermute(far, 'gy', [(i, (i + 1 if i % 2 else i - 1) % count_y) for i...  2.47 us
    pallas_call x1, Pallas kernels, per_device(): pl.pallas_call(functools.partial(interior_kernel, rows, planes), out_shap...  2.11 us
  transfers between devices with their start and end apart: 12, of which 7 were waited for; matrix products, arithmetic and copies ran while one was open for 0% of the time, Pallas kernels for 24%

profile of v10, /device:TPU:0, one launch (start us, length us, event | category | flops | bytes accessed | tf_op | source)
XLA Modules:
  0.0 38.5 jit_solution(15145062925530091781)
XLA Ops:
  0.6 1.3 %far_face.1 = f32[776,128]{1,0:T(8,128)S(1)} custom-call(f32[3,132,16,128]{3,2,1,0:T(8,128)} %fields.2), custom_call_target="tpu_custom_call" | custom-call | bytes 3690000 | tf_op jit(solution)/shard_map/far_face/pallas_call | solution.py:466
  1.9 2.5 %collective-permute-start = (f32[776,128]{1,0:T(8,128)S(1)}, f32[776,128]{1,0:T(8,128)S(1)}, u32[]{:S(2)}, u32[]{:S(2)}) collective-permute-start(f32[776,128]{1,0:T(8,128)S(1)} %far_face.1), channel_id=1, source_target_pairs={{0,24},{8,16},{16,8},{24,0},{1,25},{9,17},{17,9},{25,1},{2,26},{10... | collective-permute-start | bytes 1191944 | tf_op jit(solution)/shard_map/ppermute | solution.py:477
  4.4 1.0 %faces.1 = (f32[3,16,132,128]{3,2,1,0:T(8,128)S(1)}, f32[2,3,128,128]{3,2,1,0:T(8,128)S(1)}, f32[128,128]{1,0:T(8,128)S(1)}, f32[128,128]{1,0:T(8,128)S(1)}) custom-call(f32[3,132,16,128]{3,2,1,0:T(8,128)S(1)} %copy-done), custom_call_target="tpu_custom_call" | custom-call | bytes 9225000 | tf_op jit(solution)/shard_map/faces/pallas_call | solution.py:478
  5.4 0.7 %collective-permute-start.1 = (f32[2,3,128,128]{3,2,1,0:T(8,128)S(1)}, f32[2,3,128,128]{3,2,1,0:T(8,128)S(1)}, u32[]{:S(2)}, u32[]{:S(2)}) collective-permute-start(f32[2,3,128,128]{3,2,1,0:T(8,128)S(1)} %get-tuple-element.34), channel_id=1, source_target_pairs={{0,8},{8,0},{16,24},{24,16},{1,9},{9,1},{17,25},{25,17},{2,10},{10... | collective-permute-start | bytes 1179656 | tf_op jit(solution)/shard_map/ppermute | solution.py:493
  6.1 1.5 %collective-permute-start.2 = (f32[128,128]{1,0:T(8,128)S(1)}, f32[128,128]{1,0:T(8,128)S(1)}, u32[]{:S(2)}, u32[]{:S(2)}) collective-permute-start(f32[128,128]{1,0:T(8,128)S(1)} %get-tuple-element.35), channel_id=1, source_target_pairs={{0,1},{1,2},{2,3},{3,4},{4,5},{5,6},{6,7},{7,0},{8,9},{9,10},{10,1... | collective-permute-start | bytes 196616 | tf_op jit(solution)/shard_map/ppermute | solution.py:494
  7.6 3.2 %collective-permute-start.3 = (f32[128,128]{1,0:T(8,128)S(1)}, f32[128,128]{1,0:T(8,128)S(1)}, u32[]{:S(2)}, u32[]{:S(2)}) collective-permute-start(f32[128,128]{1,0:T(8,128)S(1)} %get-tuple-element.36), channel_id=1, source_target_pairs={{0,7},{1,0},{2,1},{3,2},{4,3},{5,4},{6,5},{7,6},{8,15},{9,8},{10,9... | collective-permute-start | bytes 196616 | tf_op jit(solution)/shard_map/ppermute | solution.py:495
  10.8 3.5 %inner.1 = (f32[3,128,128]{2,1,0:T(8,128)S(1)}, f32[3,16,128,128]{3,2,1,0:T(8,128)S(1)}, f32[12,128,128]{2,1,0:T(8,128)S(1)}, f32[12,128,128]{2,1,0:T(8,128)S(1)...) custom-call(f32[3,16,132,128]{3,2,1,0:T(8,128)S(1)} %get-tuple-element.27.fields), custom_call_target="tpu_custom_call" | custom-call | bytes 11070000 | tf_op jit(solution)/shard_map/inner/pallas_call | solution.py:498
  14.4 2.1 %interior.1 = (f32[2,14,128,128]{3,2,1,0:T(8,128)S(1)}, f32[2,256,256]{2,1,0:T(8,128)S(1)}, f32[2,2,3,128,128]{4,3,2,1,0:T(8,128)S(1)}, f32[200,128]{1,0:T(8,128)S(1)}) custom-call(f32[3,16,132,128]{3,2,1,0:T(8,128)S(1)} %get-tuple-element.27.fields, f32[3,16,128,128]{3,2,1,0:T(8,128)S(1)} %get-tuple-element.29.own_z, ...), custom_call_target="tpu_custom_call" | custom-call | tf_op jit(solution)/shard_map/interior/pallas_call | solution.py:512
  16.5 0.6 %border.1 = (f32[2,2,128,128]{3,2,1,0:T(8,128)S(1)}, f32[168,128]{1,0:T(8,128)S(1)}, f32[168,128]{1,0:T(8,128)S(1)}) custom-call(f32[3,16,132,128]{3,2,1,0:T(8,128)S(1)} %get-tuple-element.27.fields, f32[776,128]{1,0:T(8,128)S(1)} %collective-permute-done.far, f32[2,2,3,128,128]{4,3,2,1,0:T(8,128)S(1)} %get-tuple-element.38.beside, ...), custom_call_target="tpu_custom_call" | custom-call | bytes 2583000 | tf_op jit(solution)/shard_map/border/pallas_call | solution.py:529
  17.1 1.3 %collective-permute-done.4 = f32[168,128]{1,0:T(8,128)S(1)} collective-permute-done((f32[168,128]{1,0:T(8,128)S(1)}, f32[168,128]{1,0:T(8,128)S(1)}, u32[]{:S(2)}, u32[]{:S(2)}) %collective-permute-start.4) | collective-permute-done | bytes 86048 | tf_op jit(solution)/shard_map/ppermute | solution.py:440
  18.4 0.9 %collective-permute-start.7 = (f32[168,128]{1,0:T(8,128)S(1)}, f32[168,128]{1,0:T(8,128)S(1)}, u32[]{:S(2)}, u32[]{:S(2)}) collective-permute-start(f32[168,128]{1,0:T(8,128)S(1)} %add.21), channel_id=1, source_target_pairs={{0,17},{1,16},{2,19},{3,18},{4,21},{5,20},{6,23},{7,22},{8,14},{9,... | collective-permute-start | bytes 258056 | tf_op jit(solution)/shard_map/ppermute | solution.py:440
  19.3 1.4 %collective-permute-start.6 = (f32[168,128]{1,0:T(8,128)S(1)}, f32[168,128]{1,0:T(8,128)S(1)}, u32[]{:S(2)}, u32[]{:S(2)}) collective-permute-start(f32[168,128]{1,0:T(8,128)S(1)} %add.21), channel_id=1, source_target_pairs={{0,1},{1,0},{2,3},{3,2},{4,5},{5,4},{6,7},{7,6},{8,12},{9,13},{10,... | collective-permute-start | bytes 258056 | tf_op jit(solution)/shard_map/ppermute | solution.py:440
  20.7 1.2 %collective-permute-start.5 = (f32[168,128]{1,0:T(8,128)S(1)}, f32[168,128]{1,0:T(8,128)S(1)}, u32[]{:S(2)}, u32[]{:S(2)}) collective-permute-start(f32[168,128]{1,0:T(8,128)S(1)} %add.21), channel_id=1, source_target_pairs={{0,16},{1,17},{2,18},{3,19},{4,20},{5,21},{6,22},{7,23},{8,10},{9,... | collective-permute-start | bytes 258056 | tf_op jit(solution)/shard_map/ppermute | solution.py:440
  22.0 1.3 %assemble.2 = f32[128,16,128]{2,1,0:T(8,128)} custom-call(f32[2,14,128,128]{3,2,1,0:T(8,128)S(1)} %get-tuple-element.43.inner, f32[2,2,128,128]{3,2,1,0:T(8,128)S(1)} %get-tuple-element.44.border), custom_call_target="tpu_custom_call" | custom-call | bytes 3690000 | tf_op jit(solution)/shard_map/assemble/pallas_call | solution.py:540
  23.2 0.6 %collective-permute-done.7 = f32[168,128]{1,0:T(8,128)S(1)} collective-permute-done((f32[168,128]{1,0:T(8,128)S(1)}, f32[168,128]{1,0:T(8,128)S(1)}, u32[]{:S(2)}, u32[]{:S(2)}) %collective-permute-start.7) | collective-permute-done | bytes 86048 | tf_op jit(solution)/shard_map/ppermute | solution.py:440
  23.9 0.2 collective-permute-done.6
  24.1 1.1 %collective-permute-done.5 = f32[168,128]{1,0:T(8,128)S(1)} collective-permute-done((f32[168,128]{1,0:T(8,128)S(1)}, f32[168,128]{1,0:T(8,128)S(1)}, u32[]{:S(2)}, u32[]{:S(2)}) %collective-permute-start.5) | collective-permute-done | bytes 86048 | tf_op jit(solution)/shard_map/ppermute | solution.py:440
  25.2 2.8 %collective-permute-start.10 = (f32[168,128]{1,0:T(8,128)S(1)}, f32[168,128]{1,0:T(8,128)S(1)}, u32[]{:S(2)}, u32[]{:S(2)}) collective-permute-start(f32[168,128]{1,0:T(8,128)S(1)} %add_add_fusion.1), channel_id=1, source_target_pairs={{0,6},{1,7},{2,4},{3,5},{4,2},{5,3},{6,0},{7,1},{8,25},{9,24},{10,... | collective-permute-start | bytes 258056 | tf_op jit(solution)/shard_map/ppermute | solution.py:440
  28.0 1.7 %collective-permute-start.8 = (f32[168,128]{1,0:T(8,128)S(1)}, f32[168,128]{1,0:T(8,128)S(1)}, u32[]{:S(2)}, u32[]{:S(2)}) collective-permute-start(f32[168,128]{1,0:T(8,128)S(1)} %add_add_fusion.1), channel_id=1, source_target_pairs={{0,2},{1,3},{2,0},{3,1},{4,6},{5,7},{6,4},{7,5},{8,24},{9,25},{10,... | collective-permute-start | bytes 258056 | tf_op jit(solution)/shard_map/ppermute | solution.py:440
  29.7 1.3 %assemble.3 = f32[128,16,128]{2,1,0:T(8,128)} custom-call(f32[2,14,128,128]{3,2,1,0:T(8,128)S(1)} %get-tuple-element.43.inner, f32[2,2,128,128]{3,2,1,0:T(8,128)S(1)} %get-tuple-element.44.border), custom_call_target="tpu_custom_call" | custom-call | bytes 3690000 | tf_op jit(solution)/shard_map/assemble/pallas_call | solution.py:540
  31.0 0.6 %collective-permute-done.10 = f32[168,128]{1,0:T(8,128)S(1)} collective-permute-done((f32[168,128]{1,0:T(8,128)S(1)}, f32[168,128]{1,0:T(8,128)S(1)}, u32[]{:S(2)}, u32[]{:S(2)}) %collective-permute-start.10) | collective-permute-done | bytes 86048 | tf_op jit(solution)/shard_map/ppermute | solution.py:440
  31.6 1.9 %collective-permute-done.9 = f32[168,128]{1,0:T(8,128)S(1)} collective-permute-done((f32[168,128]{1,0:T(8,128)S(1)}, f32[168,128]{1,0:T(8,128)S(1)}, u32[]{:S(2)}, u32[]{:S(2)}) %collective-permute-start.9) | collective-permute-done | bytes 86048 | tf_op jit(solution)/shard_map/ppermute | solution.py:440
  33.6 1.3 %collective-permute-done.11.given = f32[168,128]{1,0:T(8,128)S(1)} collective-permute-done((f32[168,128]{1,0:T(8,128)S(1)}, f32[168,128]{1,0:T(8,128)S(1)}, u32[]{:S(2)}, u32[]{:S(2)}) %collective-permute-start.11) | collective-permute-done | bytes 86048 | tf_op jit(solution)/shard_map/ppermute | solution.py:440
  34.8 3.7 %factor.1 = f32[128,128]{1,0:T(8,128)} custom-call(f32[168,128]{1,0:T(8,128)S(1)} %add_add_fusion.kept, f32[168,128]{1,0:T(8,128)S(1)} %collective-permute-done.11.given), custom_call_target="tpu_custom_call" | custom-call | bytes 22140000 | tf_op jit(solution)/shard_map/factor/pallas_call | solution.py:562
  (13 shorter events, 0.2 us)
Async XLA Ops:
  0.6 3.7 %copy-start = (f32[3,132,16,128]{3,2,1,0:T(8,128)S(1)}, f32[3,132,16,128]{3,2,1,0:T(8,128)}, u32[]{:S(2)}) copy-start(f32[3,132,16,128]{3,2,1,0:T(8,128)} %fields.2) | copy-start | bytes 9732100
  1.9 14.6 %collective-permute-start = (f32[776,128]{1,0:T(8,128)S(1)}, f32[776,128]{1,0:T(8,128)S(1)}, u32[]{:S(2)}, u32[]{:S(2)}) collective-permute-start(f32[776,128]{1,0:T(8,128)S(1)} %far_face.1), channel_id=1, source_target_pairs={{0,24},{8,16},{16,8},{24,0},{1,25},{9,17},{17,9},{25,1},{2,26},{10... | collective-permute-start | bytes 1191944 | tf_op jit(solution)/shard_map/ppermute | solution.py:477
  5.4 9.0 %collective-permute-start.1 = (f32[2,3,128,128]{3,2,1,0:T(8,128)S(1)}, f32[2,3,128,128]{3,2,1,0:T(8,128)S(1)}, u32[]{:S(2)}, u32[]{:S(2)}) collective-permute-start(f32[2,3,128,128]{3,2,1,0:T(8,128)S(1)} %get-tuple-element.34), channel_id=1, source_target_pairs={{0,8},{8,0},{16,24},{24,16},{1,9},{9,1},{17,25},{25,17},{2,10},{10... | collective-permute-start | bytes 1179656 | tf_op jit(solution)/shard_map/ppermute | solution.py:493
  6.1 8.3 %collective-permute-start.2 = (f32[128,128]{1,0:T(8,128)S(1)}, f32[128,128]{1,0:T(8,128)S(1)}, u32[]{:S(2)}, u32[]{:S(2)}) collective-permute-start(f32[128,128]{1,0:T(8,128)S(1)} %get-tuple-element.35), channel_id=1, source_target_pairs={{0,1},{1,2},{2,3},{3,4},{4,5},{5,6},{6,7},{7,0},{8,9},{9,10},{10,1... | collective-permute-start | bytes 196616 | tf_op jit(solution)/shard_map/ppermute | solution.py:494
  7.6 6.8 %collective-permute-start.3 = (f32[128,128]{1,0:T(8,128)S(1)}, f32[128,128]{1,0:T(8,128)S(1)}, u32[]{:S(2)}, u32[]{:S(2)}) collective-permute-start(f32[128,128]{1,0:T(8,128)S(1)} %get-tuple-element.36), channel_id=1, source_target_pairs={{0,7},{1,0},{2,1},{3,2},{4,3},{5,4},{6,5},{7,6},{8,15},{9,8},{10,9... | collective-permute-start | bytes 196616 | tf_op jit(solution)/shard_map/ppermute | solution.py:495
  17.1 1.3 %collective-permute-start.4 = (f32[168,128]{1,0:T(8,128)S(1)}, f32[168,128]{1,0:T(8,128)S(1)}, u32[]{:S(2)}, u32[]{:S(2)}) collective-permute-start(f32[168,128]{1,0:T(8,128)S(1)} %get-tuple-element.42), channel_id=1, source_target_pairs={{0,8},{1,9},{2,10},{3,11},{4,12},{5,13},{6,14},{7,15},{8,0},{9,1},... | collective-permute-start | bytes 258056 | tf_op jit(solution)/shard_map/ppermute | solution.py:440
  18.4 5.4 %collective-permute-start.7 = (f32[168,128]{1,0:T(8,128)S(1)}, f32[168,128]{1,0:T(8,128)S(1)}, u32[]{:S(2)}, u32[]{:S(2)}) collective-permute-start(f32[168,128]{1,0:T(8,128)S(1)} %add.21), channel_id=1, source_target_pairs={{0,17},{1,16},{2,19},{3,18},{4,21},{5,20},{6,23},{7,22},{8,14},{9,... | collective-permute-start | bytes 258056 | tf_op jit(solution)/shard_map/ppermute | solution.py:440
  19.3 4.8 %collective-permute-start.6 = (f32[168,128]{1,0:T(8,128)S(1)}, f32[168,128]{1,0:T(8,128)S(1)}, u32[]{:S(2)}, u32[]{:S(2)}) collective-permute-start(f32[168,128]{1,0:T(8,128)S(1)} %add.21), channel_id=1, source_target_pairs={{0,1},{1,0},{2,3},{3,2},{4,5},{5,4},{6,7},{7,6},{8,12},{9,13},{10,... | collective-permute-start | bytes 258056 | tf_op jit(solution)/shard_map/ppermute | solution.py:440
  20.7 4.5 %collective-permute-start.5 = (f32[168,128]{1,0:T(8,128)S(1)}, f32[168,128]{1,0:T(8,128)S(1)}, u32[]{:S(2)}, u32[]{:S(2)}) collective-permute-start(f32[168,128]{1,0:T(8,128)S(1)} %add.21), channel_id=1, source_target_pairs={{0,16},{1,17},{2,18},{3,19},{4,20},{5,21},{6,22},{7,23},{8,10},{9,... | collective-permute-start | bytes 258056 | tf_op jit(solution)/shard_map/ppermute | solution.py:440
  25.2 6.3 %collective-permute-start.10 = (f32[168,128]{1,0:T(8,128)S(1)}, f32[168,128]{1,0:T(8,128)S(1)}, u32[]{:S(2)}, u32[]{:S(2)}) collective-permute-start(f32[168,128]{1,0:T(8,128)S(1)} %add_add_fusion.1), channel_id=1, source_target_pairs={{0,6},{1,7},{2,4},{3,5},{4,2},{5,3},{6,0},{7,1},{8,25},{9,24},{10,... | collective-permute-start | bytes 258056 | tf_op jit(solution)/shard_map/ppermute | solution.py:440
  28.0 5.4 %collective-permute-start.9 = (f32[168,128]{1,0:T(8,128)S(1)}, f32[168,128]{1,0:T(8,128)S(1)}, u32[]{:S(2)}, u32[]{:S(2)}) collective-permute-start(f32[168,128]{1,0:T(8,128)S(1)} %add_add_fusion.1), channel_id=1, source_target_pairs={{0,4},{1,5},{2,6},{3,7},{4,0},{5,1},{6,2},{7,3},{8,9},{9,8},{10,11... | collective-permute-start | bytes 258056 | tf_op jit(solution)/shard_map/ppermute | solution.py:440
  28.0 5.4 %collective-permute-start.8 = (f32[168,128]{1,0:T(8,128)S(1)}, f32[168,128]{1,0:T(8,128)S(1)}, u32[]{:S(2)}, u32[]{:S(2)}) collective-permute-start(f32[168,128]{1,0:T(8,128)S(1)} %add_add_fusion.1), channel_id=1, source_target_pairs={{0,2},{1,3},{2,0},{3,1},{4,6},{5,7},{6,4},{7,5},{8,24},{9,25},{10,... | collective-permute-start | bytes 258056 | tf_op jit(solution)/shard_map/ppermute | solution.py:440
  33.5 1.3 %collective-permute-start.11 = (f32[168,128]{1,0:T(8,128)S(1)}, f32[168,128]{1,0:T(8,128)S(1)}, u32[]{:S(2)}, u32[]{:S(2)}) collective-permute-start(f32[168,128]{1,0:T(8,128)S(1)} %add_add_fusion.kept), channel_id=1, source_target_pairs={{0,8},{1,9},{2,10},{3,11},{4,12},{5,13},{6,14},{7,15},{8,0},{9,1},... | collective-permute-start | bytes 258056 | tf_op jit(solution)/shard_map/ppermute | solution.py:440

commit v11 on v10

--- a/solution.py
+++ b/solution.py
@@ -421,7 +421,7 @@
     triangles = jnp.where(eye, 0.0, pair(message[0:planes, :], 0) + pair(message[planes : 2 * planes, :], 2))
     triangles = triangles + folded * scale[4]
     cross = triangles + triangles.T + jnp.where(eye, jnp.sum(scaled[0:5], axis=0, keepdims=True), 0.0)
-    narrow = planes // 64 * 2
+    narrow = planes // 128 * 2
     widths = [8] * narrow + [16] * (planes // 16 - narrow // 2)
     upper = factor_tiles([cross[t : t + 8, :] for t in range(0, planes, 8)], widths)
     factor[...] = jnp.concatenate(upper, axis=0).T

time: 38.6 us -> 38.6 us (level)
  no operation moved by 1% of the time
where the time goes in v11:
time: 38.6 us; the launch traced here: 38.4 us
  starting transfers between devices  16.1 us (42%)
  Pallas kernels  14.6 us (38%)
  waiting for transfers between devices  6.99 us (18%)
  between operations  0.72 us (2%)
    ppermute x8, starting transfers between devices, exchange(): lax.ppermute(values, AXES, [(i, i ^ (odd if i // count_z % 2 else even))...  8.15 us
    ppermute x8, waiting for transfers between devices, exchange(): lax.ppermute(values, AXES, [(i, i ^ (odd if i // count_z % 2 else even))...  6.98 us
    pallas_call x1, Pallas kernels, per_device(): pl.pallas_call(functools.partial(factor_kernel, float(cells), planes), ou...  3.57 us
    pallas_call x1, Pallas kernels, per_device(): pl.pallas_call(functools.partial(inner_kernel, rows, planes), out_shape=(...  3.52 us
    ppermute x1, starting transfers between devices, per_device(): lax.ppermute(behind, 'gz', [(i, (i - 1) % count_z) for i in range(count_z)])  3.23 us
    pallas_call x2, Pallas kernels, per_device(): pl.pallas_call(functools.partial(assemble_kernel, rows, planes, f), out_s...  2.55 us
    ppermute x1, starting transfers between devices, per_device(): lax.ppermute(far, 'gy', [(i, (i + 1 if i % 2 else i - 1) % count_y) for i...  2.47 us
    pallas_call x1, Pallas kernels, per_device(): pl.pallas_call(functools.partial(interior_kernel, rows, planes), out_shap...  2.11 us
  transfers between devices with their start and end apart: 12, of which 7 were waited for; matrix products, arithmetic and copies ran while one was open for 0% of the time, Pallas kernels for 24%

profile of v11, /device:TPU:0, one launch (start us, length us, event | category | flops | bytes accessed | tf_op | source)
XLA Modules:
  0.0 38.4 jit_solution(14576479119597017866)
XLA Ops:
  0.6 1.3 %far_face.1 = f32[776,128]{1,0:T(8,128)S(1)} custom-call(f32[3,132,16,128]{3,2,1,0:T(8,128)} %fields.2), custom_call_target="tpu_custom_call" | custom-call | bytes 3690000 | tf_op jit(solution)/shard_map/far_face/pallas_call | solution.py:466
  1.9 2.5 %collective-permute-start = (f32[776,128]{1,0:T(8,128)S(1)}, f32[776,128]{1,0:T(8,128)S(1)}, u32[]{:S(2)}, u32[]{:S(2)}) collective-permute-start(f32[776,128]{1,0:T(8,128)S(1)} %far_face.1), channel_id=1, source_target_pairs={{0,24},{8,16},{16,8},{24,0},{1,25},{9,17},{17,9},{25,1},{2,26},{10... | collective-permute-start | bytes 1191944 | tf_op jit(solution)/shard_map/ppermute | solution.py:477
  4.4 1.0 %faces.1 = (f32[3,16,132,128]{3,2,1,0:T(8,128)S(1)}, f32[2,3,128,128]{3,2,1,0:T(8,128)S(1)}, f32[128,128]{1,0:T(8,128)S(1)}, f32[128,128]{1,0:T(8,128)S(1)}) custom-call(f32[3,132,16,128]{3,2,1,0:T(8,128)S(1)} %copy-done), custom_call_target="tpu_custom_call" | custom-call | bytes 9225000 | tf_op jit(solution)/shard_map/faces/pallas_call | solution.py:478
  5.4 0.7 %collective-permute-start.1 = (f32[2,3,128,128]{3,2,1,0:T(8,128)S(1)}, f32[2,3,128,128]{3,2,1,0:T(8,128)S(1)}, u32[]{:S(2)}, u32[]{:S(2)}) collective-permute-start(f32[2,3,128,128]{3,2,1,0:T(8,128)S(1)} %get-tuple-element.34), channel_id=1, source_target_pairs={{0,8},{8,0},{16,24},{24,16},{1,9},{9,1},{17,25},{25,17},{2,10},{10... | collective-permute-start | bytes 1179656 | tf_op jit(solution)/shard_map/ppermute | solution.py:493
  6.1 1.5 %collective-permute-start.2 = (f32[128,128]{1,0:T(8,128)S(1)}, f32[128,128]{1,0:T(8,128)S(1)}, u32[]{:S(2)}, u32[]{:S(2)}) collective-permute-start(f32[128,128]{1,0:T(8,128)S(1)} %get-tuple-element.35), channel_id=1, source_target_pairs={{0,1},{1,2},{2,3},{3,4},{4,5},{5,6},{6,7},{7,0},{8,9},{9,10},{10,1... | collective-permute-start | bytes 196616 | tf_op jit(solution)/shard_map/ppermute | solution.py:494
  7.6 3.2 %collective-permute-start.3 = (f32[128,128]{1,0:T(8,128)S(1)}, f32[128,128]{1,0:T(8,128)S(1)}, u32[]{:S(2)}, u32[]{:S(2)}) collective-permute-start(f32[128,128]{1,0:T(8,128)S(1)} %get-tuple-element.36), channel_id=1, source_target_pairs={{0,7},{1,0},{2,1},{3,2},{4,3},{5,4},{6,5},{7,6},{8,15},{9,8},{10,9... | collective-permute-start | bytes 196616 | tf_op jit(solution)/shard_map/ppermute | solution.py:495
  10.8 3.5 %inner.1 = (f32[3,128,128]{2,1,0:T(8,128)S(1)}, f32[3,16,128,128]{3,2,1,0:T(8,128)S(1)}, f32[12,128,128]{2,1,0:T(8,128)S(1)}, f32[12,128,128]{2,1,0:T(8,128)S(1)...) custom-call(f32[3,16,132,128]{3,2,1,0:T(8,128)S(1)} %get-tuple-element.27.fields), custom_call_target="tpu_custom_call" | custom-call | bytes 11070000 | tf_op jit(solution)/shard_map/inner/pallas_call | solution.py:498
  14.4 2.1 %interior.1 = (f32[2,14,128,128]{3,2,1,0:T(8,128)S(1)}, f32[2,256,256]{2,1,0:T(8,128)S(1)}, f32[2,2,3,128,128]{4,3,2,1,0:T(8,128)S(1)}, f32[200,128]{1,0:T(8,128)S(1)}) custom-call(f32[3,16,132,128]{3,2,1,0:T(8,128)S(1)} %get-tuple-element.27.fields, f32[3,16,128,128]{3,2,1,0:T(8,128)S(1)} %get-tuple-element.29.own_z, ...), custom_call_target="tpu_custom_call" | custom-call | tf_op jit(solution)/shard_map/interior/pallas_call | solution.py:512
  16.5 0.6 %border.1 = (f32[2,2,128,128]{3,2,1,0:T(8,128)S(1)}, f32[168,128]{1,0:T(8,128)S(1)}, f32[168,128]{1,0:T(8,128)S(1)}) custom-call(f32[3,16,132,128]{3,2,1,0:T(8,128)S(1)} %get-tuple-element.27.fields, f32[776,128]{1,0:T(8,128)S(1)} %collective-permute-done.far, f32[2,2,3,128,128]{4,3,2,1,0:T(8,128)S(1)} %get-tuple-element.38.beside, ...), custom_call_target="tpu_custom_call" | custom-call | bytes 2583000 | tf_op jit(solution)/shard_map/border/pallas_call | solution.py:529
  17.1 1.3 %collective-permute-done.4 = f32[168,128]{1,0:T(8,128)S(1)} collective-permute-done((f32[168,128]{1,0:T(8,128)S(1)}, f32[168,128]{1,0:T(8,128)S(1)}, u32[]{:S(2)}, u32[]{:S(2)}) %collective-permute-start.4) | collective-permute-done | bytes 86048 | tf_op jit(solution)/shard_map/ppermute | solution.py:440
  18.4 0.9 %collective-permute-start.7 = (f32[168,128]{1,0:T(8,128)S(1)}, f32[168,128]{1,0:T(8,128)S(1)}, u32[]{:S(2)}, u32[]{:S(2)}) collective-permute-start(f32[168,128]{1,0:T(8,128)S(1)} %add.21), channel_id=1, source_target_pairs={{0,17},{1,16},{2,19},{3,18},{4,21},{5,20},{6,23},{7,22},{8,14},{9,... | collective-permute-start | bytes 258056 | tf_op jit(solution)/shard_map/ppermute | solution.py:440
  19.3 1.4 %collective-permute-start.6 = (f32[168,128]{1,0:T(8,128)S(1)}, f32[168,128]{1,0:T(8,128)S(1)}, u32[]{:S(2)}, u32[]{:S(2)}) collective-permute-start(f32[168,128]{1,0:T(8,128)S(1)} %add.21), channel_id=1, source_target_pairs={{0,1},{1,0},{2,3},{3,2},{4,5},{5,4},{6,7},{7,6},{8,12},{9,13},{10,... | collective-permute-start | bytes 258056 | tf_op jit(solution)/shard_map/ppermute | solution.py:440
  20.7 1.2 %collective-permute-start.5 = (f32[168,128]{1,0:T(8,128)S(1)}, f32[168,128]{1,0:T(8,128)S(1)}, u32[]{:S(2)}, u32[]{:S(2)}) collective-permute-start(f32[168,128]{1,0:T(8,128)S(1)} %add.21), channel_id=1, source_target_pairs={{0,16},{1,17},{2,18},{3,19},{4,20},{5,21},{6,22},{7,23},{8,10},{9,... | collective-permute-start | bytes 258056 | tf_op jit(solution)/shard_map/ppermute | solution.py:440
  22.0 1.3 %assemble.2 = f32[128,16,128]{2,1,0:T(8,128)} custom-call(f32[2,14,128,128]{3,2,1,0:T(8,128)S(1)} %get-tuple-element.43.inner, f32[2,2,128,128]{3,2,1,0:T(8,128)S(1)} %get-tuple-element.44.border), custom_call_target="tpu_custom_call" | custom-call | bytes 3690000 | tf_op jit(solution)/shard_map/assemble/pallas_call | solution.py:540
  23.2 0.6 %collective-permute-done.7 = f32[168,128]{1,0:T(8,128)S(1)} collective-permute-done((f32[168,128]{1,0:T(8,128)S(1)}, f32[168,128]{1,0:T(8,128)S(1)}, u32[]{:S(2)}, u32[]{:S(2)}) %collective-permute-start.7) | collective-permute-done | bytes 86048 | tf_op jit(solution)/shard_map/ppermute | solution.py:440
  23.9 0.2 collective-permute-done.6
  24.1 1.1 %collective-permute-done.5 = f32[168,128]{1,0:T(8,128)S(1)} collective-permute-done((f32[168,128]{1,0:T(8,128)S(1)}, f32[168,128]{1,0:T(8,128)S(1)}, u32[]{:S(2)}, u32[]{:S(2)}) %collective-permute-start.5) | collective-permute-done | bytes 86048 | tf_op jit(solution)/shard_map/ppermute | solution.py:440
  25.2 2.8 %collective-permute-start.10 = (f32[168,128]{1,0:T(8,128)S(1)}, f32[168,128]{1,0:T(8,128)S(1)}, u32[]{:S(2)}, u32[]{:S(2)}) collective-permute-start(f32[168,128]{1,0:T(8,128)S(1)} %add_add_fusion.1), channel_id=1, source_target_pairs={{0,6},{1,7},{2,4},{3,5},{4,2},{5,3},{6,0},{7,1},{8,25},{9,24},{10,... | collective-permute-start | bytes 258056 | tf_op jit(solution)/shard_map/ppermute | solution.py:440
  28.0 1.7 %collective-permute-start.8 = (f32[168,128]{1,0:T(8,128)S(1)}, f32[168,128]{1,0:T(8,128)S(1)}, u32[]{:S(2)}, u32[]{:S(2)}) collective-permute-start(f32[168,128]{1,0:T(8,128)S(1)} %add_add_fusion.1), channel_id=1, source_target_pairs={{0,2},{1,3},{2,0},{3,1},{4,6},{5,7},{6,4},{7,5},{8,24},{9,25},{10,... | collective-permute-start | bytes 258056 | tf_op jit(solution)/shard_map/ppermute | solution.py:440
  29.7 1.3 %assemble.3 = f32[128,16,128]{2,1,0:T(8,128)} custom-call(f32[2,14,128,128]{3,2,1,0:T(8,128)S(1)} %get-tuple-element.43.inner, f32[2,2,128,128]{3,2,1,0:T(8,128)S(1)} %get-tuple-element.44.border), custom_call_target="tpu_custom_call" | custom-call | bytes 3690000 | tf_op jit(solution)/shard_map/assemble/pallas_call | solution.py:540
  31.0 0.6 %collective-permute-done.10 = f32[168,128]{1,0:T(8,128)S(1)} collective-permute-done((f32[168,128]{1,0:T(8,128)S(1)}, f32[168,128]{1,0:T(8,128)S(1)}, u32[]{:S(2)}, u32[]{:S(2)}) %collective-permute-start.10) | collective-permute-done | bytes 86048 | tf_op jit(solution)/shard_map/ppermute | solution.py:440
  31.6 1.9 %collective-permute-done.9 = f32[168,128]{1,0:T(8,128)S(1)} collective-permute-done((f32[168,128]{1,0:T(8,128)S(1)}, f32[168,128]{1,0:T(8,128)S(1)}, u32[]{:S(2)}, u32[]{:S(2)}) %collective-permute-start.9) | collective-permute-done | bytes 86048 | tf_op jit(solution)/shard_map/ppermute | solution.py:440
  33.6 1.3 %collective-permute-done.11.given = f32[168,128]{1,0:T(8,128)S(1)} collective-permute-done((f32[168,128]{1,0:T(8,128)S(1)}, f32[168,128]{1,0:T(8,128)S(1)}, u32[]{:S(2)}, u32[]{:S(2)}) %collective-permute-start.11) | collective-permute-done | bytes 86048 | tf_op jit(solution)/shard_map/ppermute | solution.py:440
  34.8 3.6 %factor.1 = f32[128,128]{1,0:T(8,128)} custom-call(f32[168,128]{1,0:T(8,128)S(1)} %add_add_fusion.kept, f32[168,128]{1,0:T(8,128)S(1)} %collective-permute-done.11.given), custom_call_target="tpu_custom_call" | custom-call | bytes 22140000 | tf_op jit(solution)/shard_map/factor/pallas_call | solution.py:562
  (13 shorter events, 0.2 us)
Async XLA Ops:
  0.6 3.7 %copy-start = (f32[3,132,16,128]{3,2,1,0:T(8,128)S(1)}, f32[3,132,16,128]{3,2,1,0:T(8,128)}, u32[]{:S(2)}) copy-start(f32[3,132,16,128]{3,2,1,0:T(8,128)} %fields.2) | copy-start | bytes 9732100
  1.9 14.6 %collective-permute-start = (f32[776,128]{1,0:T(8,128)S(1)}, f32[776,128]{1,0:T(8,128)S(1)}, u32[]{:S(2)}, u32[]{:S(2)}) collective-permute-start(f32[776,128]{1,0:T(8,128)S(1)} %far_face.1), channel_id=1, source_target_pairs={{0,24},{8,16},{16,8},{24,0},{1,25},{9,17},{17,9},{25,1},{2,26},{10... | collective-permute-start | bytes 1191944 | tf_op jit(solution)/shard_map/ppermute | solution.py:477
  5.4 9.0 %collective-permute-start.1 = (f32[2,3,128,128]{3,2,1,0:T(8,128)S(1)}, f32[2,3,128,128]{3,2,1,0:T(8,128)S(1)}, u32[]{:S(2)}, u32[]{:S(2)}) collective-permute-start(f32[2,3,128,128]{3,2,1,0:T(8,128)S(1)} %get-tuple-element.34), channel_id=1, source_target_pairs={{0,8},{8,0},{16,24},{24,16},{1,9},{9,1},{17,25},{25,17},{2,10},{10... | collective-permute-start | bytes 1179656 | tf_op jit(solution)/shard_map/ppermute | solution.py:493
  6.1 8.3 %collective-permute-start.2 = (f32[128,128]{1,0:T(8,128)S(1)}, f32[128,128]{1,0:T(8,128)S(1)}, u32[]{:S(2)}, u32[]{:S(2)}) collective-permute-start(f32[128,128]{1,0:T(8,128)S(1)} %get-tuple-element.35), channel_id=1, source_target_pairs={{0,1},{1,2},{2,3},{3,4},{4,5},{5,6},{6,7},{7,0},{8,9},{9,10},{10,1... | collective-permute-start | bytes 196616 | tf_op jit(solution)/shard_map/ppermute | solution.py:494
  7.6 6.8 %collective-permute-start.3 = (f32[128,128]{1,0:T(8,128)S(1)}, f32[128,128]{1,0:T(8,128)S(1)}, u32[]{:S(2)}, u32[]{:S(2)}) collective-permute-start(f32[128,128]{1,0:T(8,128)S(1)} %get-tuple-element.36), channel_id=1, source_target_pairs={{0,7},{1,0},{2,1},{3,2},{4,3},{5,4},{6,5},{7,6},{8,15},{9,8},{10,9... | collective-permute-start | bytes 196616 | tf_op jit(solution)/shard_map/ppermute | solution.py:495
  17.1 1.3 %collective-permute-start.4 = (f32[168,128]{1,0:T(8,128)S(1)}, f32[168,128]{1,0:T(8,128)S(1)}, u32[]{:S(2)}, u32[]{:S(2)}) collective-permute-start(f32[168,128]{1,0:T(8,128)S(1)} %get-tuple-element.42), channel_id=1, source_target_pairs={{0,8},{1,9},{2,10},{3,11},{4,12},{5,13},{6,14},{7,15},{8,0},{9,1},... | collective-permute-start | bytes 258056 | tf_op jit(solution)/shard_map/ppermute | solution.py:440
  18.4 5.4 %collective-permute-start.7 = (f32[168,128]{1,0:T(8,128)S(1)}, f32[168,128]{1,0:T(8,128)S(1)}, u32[]{:S(2)}, u32[]{:S(2)}) collective-permute-start(f32[168,128]{1,0:T(8,128)S(1)} %add.21), channel_id=1, source_target_pairs={{0,17},{1,16},{2,19},{3,18},{4,21},{5,20},{6,23},{7,22},{8,14},{9,... | collective-permute-start | bytes 258056 | tf_op jit(solution)/shard_map/ppermute | solution.py:440
  19.3 4.8 %collective-permute-start.6 = (f32[168,128]{1,0:T(8,128)S(1)}, f32[168,128]{1,0:T(8,128)S(1)}, u32[]{:S(2)}, u32[]{:S(2)}) collective-permute-start(f32[168,128]{1,0:T(8,128)S(1)} %add.21), channel_id=1, source_target_pairs={{0,1},{1,0},{2,3},{3,2},{4,5},{5,4},{6,7},{7,6},{8,12},{9,13},{10,... | collective-permute-start | bytes 258056 | tf_op jit(solution)/shard_map/ppermute | solution.py:440
  20.7 4.5 %collective-permute-start.5 = (f32[168,128]{1,0:T(8,128)S(1)}, f32[168,128]{1,0:T(8,128)S(1)}, u32[]{:S(2)}, u32[]{:S(2)}) collective-permute-start(f32[168,128]{1,0:T(8,128)S(1)} %add.21), channel_id=1, source_target_pairs={{0,16},{1,17},{2,18},{3,19},{4,20},{5,21},{6,22},{7,23},{8,10},{9,... | collective-permute-start | bytes 258056 | tf_op jit(solution)/shard_map/ppermute | solution.py:440
  25.2 6.3 %collective-permute-start.10 = (f32[168,128]{1,0:T(8,128)S(1)}, f32[168,128]{1,0:T(8,128)S(1)}, u32[]{:S(2)}, u32[]{:S(2)}) collective-permute-start(f32[168,128]{1,0:T(8,128)S(1)} %add_add_fusion.1), channel_id=1, source_target_pairs={{0,6},{1,7},{2,4},{3,5},{4,2},{5,3},{6,0},{7,1},{8,25},{9,24},{10,... | collective-permute-start | bytes 258056 | tf_op jit(solution)/shard_map/ppermute | solution.py:440
  28.0 5.4 %collective-permute-start.9 = (f32[168,128]{1,0:T(8,128)S(1)}, f32[168,128]{1,0:T(8,128)S(1)}, u32[]{:S(2)}, u32[]{:S(2)}) collective-permute-start(f32[168,128]{1,0:T(8,128)S(1)} %add_add_fusion.1), channel_id=1, source_target_pairs={{0,4},{1,5},{2,6},{3,7},{4,0},{5,1},{6,2},{7,3},{8,9},{9,8},{10,11... | collective-permute-start | bytes 258056 | tf_op jit(solution)/shard_map/ppermute | solution.py:440
  28.0 5.4 %collective-permute-start.8 = (f32[168,128]{1,0:T(8,128)S(1)}, f32[168,128]{1,0:T(8,128)S(1)}, u32[]{:S(2)}, u32[]{:S(2)}) collective-permute-start(f32[168,128]{1,0:T(8,128)S(1)} %add_add_fusion.1), channel_id=1, source_target_pairs={{0,2},{1,3},{2,0},{3,1},{4,6},{5,7},{6,4},{7,5},{8,24},{9,25},{10,... | collective-permute-start | bytes 258056 | tf_op jit(solution)/shard_map/ppermute | solution.py:440
  33.5 1.3 %collective-permute-start.11 = (f32[168,128]{1,0:T(8,128)S(1)}, f32[168,128]{1,0:T(8,128)S(1)}, u32[]{:S(2)}, u32[]{:S(2)}) collective-permute-start(f32[168,128]{1,0:T(8,128)S(1)} %add_add_fusion.kept), channel_id=1, source_target_pairs={{0,8},{1,9},{2,10},{3,11},{4,12},{5,13},{6,14},{7,15},{8,0},{9,1},... | collective-permute-start | bytes 258056 | tf_op jit(solution)/shard_map/ppermute | solution.py:440
